TPU v7x, 512 devices: a whole 4x4x16 slice. The times are simulated.
512 devices in a mesh: dp: 32 (over z, y_lo), mp: 16 (over x, y_hi, core).
Axes of the slice: x: 4, y: 4 (y_hi: 2, y_lo: 2; y = y_hi * 2 + y_lo), z: 16, core: 2. Of those that a mesh axis runs over, the one named last changes fastest.
Arguments:
- inputs: bfloat16 [8192, 16384], P('dp', 'mp'), may hold values from -6 to 6
- grad_out: bfloat16 [8192, 16384], P('dp', 'mp'), may hold values from -6 to 6
- up_first: bfloat16 [128, 128, 128], P('mp'), may hold values from -6 to 6
- up_second: bfloat16 [128, 128, 512], P('mp'), may hold values from -6 to 6
- down_first: bfloat16 [128, 512, 128], P('mp'), may hold values from -6 to 6
- down_second: bfloat16 [128, 128, 128], P('mp'), may hold values from -6 to 6
- dither_first: int32 [128, 128, 128], P('mp', 'dp'), may hold values from 0 to 32767
- dither_second: int32 [128, 128, 512], P('mp', 'dp'), may hold values from 0 to 32767
- dither_third: int32 [128, 512, 128], P('mp', 'dp'), may hold values from 0 to 32767
- dither_fourth: int32 [128, 128, 128], P('mp', 'dp'), may hold values from 0 to 32767
Outputs:
- grad_inputs: bfloat16 [8192, 16384], P('dp', 'mp')
- new_up_first: bfloat16 [128, 128, 128], P('mp', 'dp')
- new_up_second: bfloat16 [128, 128, 512], P('mp', 'dp')
- new_down_first: bfloat16 [128, 512, 128], P('mp', 'dp')
- new_down_second: bfloat16 [128, 128, 128], P('mp', 'dp')
Inputs may be any that keep to these rules, and one draw needn't show every extreme that they name: `dither_first`: random bits, one per weight element. `dither_second`: random bits, one per weight element. `dither_third`: random bits, one per weight element. `dither_fourth`: random bits, one per weight element.
All inputs are finite; a program needn't handle non-finite values.
Results may differ from a plain program's by a relative error of at most 0.01.
Values may be sent and summed in bfloat16 or wider, within the bound.
No kernel may reach another device: no remote copies, remote signals or barrier semaphores. Data moves between devices by JAX's collectives and lax.ppermute only.
A program may use at most 64 MiB of HBM per device.

v0:
```python
import math

import jax
import jax.numpy as jnp
from jax import lax
from jax.sharding import PartitionSpec as P

BLOCK_COUNT = 128
TILE_SPAN = 128
HB = 512
TOK_DEV = 256


grid_step = 0.25


def gelu_back(preactivation, dgated):
    return jax.vjp(jax.nn.gelu, preactivation)[1](dgated)[0]


def updated(weight, grad_sum, dither):
    rows_own = dither.shape[1]
    start = lax.axis_index("dp") * rows_own
    own = lax.dynamic_slice_in_dim(weight, start, rows_own, 1).astype(jnp.float32)
    rate = 4.0 / math.sqrt(TOK_DEV * lax.axis_size("dp"))
    noise = grid_step * (dither.astype(jnp.float32) / 32768.0 - 0.5)
    return (own - rate * grad_sum + noise).astype(jnp.bfloat16)


def on_device(
    inputs,
    grad_out,
    up_first,
    up_second,
    down_first,
    down_second,
    dither_first,
    dither_second,
    dither_third,
    dither_fourth,
):
    rows_here = inputs.shape[0]
    blocks_here = up_first.shape[0]
    blocks_in = inputs.reshape(rows_here, blocks_here, TILE_SPAN)
    leading_monarch_matrix = (
        jnp.einsum("tbi,bim->mbt", blocks_in, up_first, preferred_element_type=jnp.float32)
        * TILE_SPAN ** (-0.5)
    ).astype(jnp.bfloat16)
    piece = lax.all_to_all(leading_monarch_matrix, "mp", split_axis=0, concat_axis=1, tiled=True)
    pre_part = jnp.einsum(
        "mbt,mbc->mct", piece, up_second, preferred_element_type=jnp.float32
    ) * BLOCK_COUNT ** (-0.5)
    gated_part = jax.nn.gelu(pre_part).astype(jnp.bfloat16)
    down_part = (
        jnp.einsum("mct,mck->mkt", gated_part, down_first, preferred_element_type=jnp.float32)
        * HB ** (-0.5)
    ).astype(jnp.bfloat16)
    regrouped = piece
    down_moved = lax.all_to_all(down_part, "mp", split_axis=1, concat_axis=0, tiled=True)
    cot_blocks = grad_out.reshape(rows_here, blocks_here, TILE_SPAN)
    grad_fourth = jnp.einsum(
        "mkt,tkj->kmj", down_moved, cot_blocks, preferred_element_type=jnp.float32
    ) * BLOCK_COUNT ** (-0.5)
    back_down = (
        jnp.einsum("tkj,kmj->mkt", cot_blocks, down_second, preferred_element_type=jnp.float32)
        * BLOCK_COUNT ** (-0.5)
    ).astype(jnp.bfloat16)
    back_moved = lax.all_to_all(back_down, "mp", split_axis=0, concat_axis=1, tiled=True)
    grad_third = jnp.einsum(
        "mct,mkt->mck", gated_part, back_moved, preferred_element_type=jnp.float32
    ) * HB ** (-0.5)
    dgated = jnp.einsum(
        "mkt,mck->mct", back_moved, down_first, preferred_element_type=jnp.float32
    ) * HB ** (-0.5)
    preactivation_gradient = gelu_back(pre_part, dgated).astype(jnp.bfloat16)
    grad_second = jnp.einsum(
        "mbt,mct->mbc", regrouped, preactivation_gradient, preferred_element_type=jnp.float32
    ) * BLOCK_COUNT ** (-0.5)
    incoming_cotangent_signal = (
        jnp.einsum(
            "mct,mbc->mbt", preactivation_gradient, up_second, preferred_element_type=jnp.float32
        )
        * BLOCK_COUNT ** (-0.5)
    ).astype(jnp.bfloat16)
    piece = lax.all_to_all(incoming_cotangent_signal, "mp", split_axis=1, concat_axis=0, tiled=True)
    grad_part = jnp.einsum(
        "mbt,bim->bit", piece, up_first, preferred_element_type=jnp.float32
    ) * TILE_SPAN ** (-0.5)
    grad_blocks = grad_part.astype(jnp.bfloat16)
    grad_inputs = jnp.transpose(grad_blocks, (2, 0, 1)).reshape(rows_here, blocks_here * TILE_SPAN)
    grad_first = jnp.einsum(
        "tbi,mbt->bim", blocks_in, piece, preferred_element_type=jnp.float32
    ) * TILE_SPAN ** (-0.5)
    summed_first, summed_second, summed_third, summed_fourth = (
        lax.psum_scatter(
            grad_first.astype(jnp.bfloat16), "dp", scatter_dimension=1, tiled=True
        ).astype(jnp.float32),
        lax.psum_scatter(
            grad_second.astype(jnp.bfloat16), "dp", scatter_dimension=1, tiled=True
        ).astype(jnp.float32),
        lax.psum_scatter(
            grad_third.astype(jnp.bfloat16), "dp", scatter_dimension=1, tiled=True
        ).astype(jnp.float32),
        lax.psum_scatter(
            grad_fourth.astype(jnp.bfloat16), "dp", scatter_dimension=1, tiled=True
        ).astype(jnp.float32),
    )
    new_one = updated(up_first, summed_first, dither_first)
    new_two = updated(up_second, summed_second, dither_second)
    new_three = updated(down_first, summed_third, dither_third)
    new_four = updated(down_second, summed_fourth, dither_fourth)
    return (grad_inputs, new_one, new_two, new_three, new_four)


def solution(mesh):
    in_specs = (
        P("dp", "mp"),
        P("dp", "mp"),
        P("mp", None, None),
        P("mp", None, None),
        P("mp", None, None),
        P("mp", None, None),
        P("mp", "dp", None),
        P("mp", "dp", None),
        P("mp", "dp", None),
        P("mp", "dp", None),
    )
    out_specs = (
        P("dp", "mp"),
        P("mp", "dp", None),
        P("mp", "dp", None),
        P("mp", "dp", None),
        P("mp", "dp", None),
    )
    return jax.shard_map(
        on_device, mesh=mesh, in_specs=in_specs, out_specs=out_specs, check_vma=False
    )
```

profile of v0, /device:TPU:6, one launch (start us, length us, event | category | flops | bytes accessed | tf_op | source)
XLA Modules:
  0.0 638.4 jit_solution(1432273511980945466)
XLA Ops:
  7.2 1.6 fusion.19
  8.7 1.1 copy.121
  9.8 9.3 %all-to-all-start.1 = ((bf16[128,8,256]{2,1,0:T(8,128)(2,1)}), bf16[128,8,256]{2,1,0:T(8,128)(2,1)S(1)}, u32[]{:S(2)}, u32[]{:S(2)}) async-start(bf16[128,8,256]{2,1,0:T(8,128)(2,1)} %copy.121), calls=%async_computation.1 | async-start | bytes 1048576 | tf_op jit(solution)/shard_map/all_to_all | solution.py:49
  19.1 1.4 fusion.20
  20.5 1.1 copy.116
  21.6 7.5 %all-to-all-done.1 = bf16[128,8,256]{2,1,0:T(8,128)(2,1)S(1)} async-done(((bf16[128,8,256]{2,1,0:T(8,128)(2,1)}), bf16[128,8,256]{2,1,0:T(8,128)(2,1)S(1)}, u32[]{:S(2)}, u32[]{:S(2)}) %all-to-all-start.1) | async-done | bytes 524320 | tf_op jit(solution)/shard_map/all_to_all | solution.py:49
  29.2 6.4 %all-to-all-start = ((bf16[128,8,256]{2,1,0:T(8,128)(2,1)}), bf16[128,8,256]{2,1,0:T(8,128)(2,1)}, u32[]{:S(2)}, u32[]{:S(2)}) async-start(bf16[128,8,256]{2,1,0:T(8,128)(2,1)} %copy.116), calls=%async_computation | async-start | bytes 1048576 | tf_op jit(solution)/shard_map/all_to_all | solution.py:68
  35.6 4.6 fusion.7
  40.3 5.5 all-to-all-done
  45.8 6.1 fusion.6
  51.9 1.3 copy-done.1
  53.3 1.5 fusion.18
  54.8 2.2 copy.124
  57.0 6.5 %all-to-all-start.2 = ((bf16[8,128,256]{2,0,1:T(8,128)(2,1)}), bf16[8,128,256]{2,0,1:T(8,128)(2,1)}, u32[]{:S(2)}, u32[]{:S(2)}) async-start(bf16[8,128,256]{2,0,1:T(8,128)(2,1)} %copy.124), calls=%async_computation.2 | async-start | bytes 1048576 | tf_op jit(solution)/shard_map/all_to_all | solution.py:85
  63.5 2.7 fusion.16
  66.2 2.2 copy.139
  68.4 5.2 all-to-all-done.2
  73.7 6.4 %all-to-all-start.3 = ((bf16[8,128,256]{2,0,1:T(8,128)(2,1)}), bf16[8,128,256]{2,0,1:T(8,128)(2,1)}, u32[]{:S(2)}, u32[]{:S(2)}) async-start(bf16[8,128,256]{2,0,1:T(8,128)(2,1)} %copy.139), calls=%async_computation.6 | async-start | bytes 1048576 | tf_op jit(solution)/shard_map/all_to_all | solution.py:59
  80.1 0.0 reduce-scatter.5.cloned.1.call-start
  80.1 1.5 fusion.23
  81.6 0.9 copy.131
  82.5 0.0 reduce-scatter.5.cloned.1.call-update
  82.6 0.0 reduce-scatter.11.cloned.1.call-start
  82.6 7.7 %all-to-all-done.3 = bf16[8,128,256]{2,0,1:T(8,128)(2,1)} async-done(((bf16[8,128,256]{2,0,1:T(8,128)(2,1)}), bf16[8,128,256]{2,0,1:T(8,128)(2,1)}, u32[]{:S(2)}, u32[]{:S(2)}) %all-to-all-start.3) | async-done | bytes 524320 | tf_op jit(solution)/shard_map/all_to_all | solution.py:59
  90.3 1.5 fusion.22
  91.8 0.9 copy.143
  92.6 0.0 reduce-scatter.11.cloned.1.call-update
  92.7 0.0 reduce-scatter.7.cloned.1.call-start
  92.7 2.2 multiply_convert_fusion.1
  95.0 1.6 copy.135
  96.5 0.0 reduce-scatter.7.cloned.1.call-update
  96.6 0.0 reduce-scatter.9.cloned.1.call-start
  96.6 2.9 multiply_convert_fusion
  99.6 0.7 constant_dynamic-slice_fusion
  100.3 1.4 fusion.17
  101.7 0.2 copy.128
  102.0 1.0 copy.145
  103.0 117.7 %reduce-scatter.5.cloned.1.call-done = bf16[8,4,128]{2,0,1:T(8,128)(2,1)} async-done(((bf16[8,128,128]{2,0,1:T(8,128)(2,1)}), bf16[8,4,128]{2,0,1:T(8,128)(2,1)}) %reduce-scatter.5.cloned.1.call-update) | async-done | bytes 8208 | tf_op jit(solution)/shard_map/reduce_scatter | solution.py:95
  220.7 0.7 fusion.61
  221.4 0.6 copy.146
  222.0 134.4 %reduce-scatter.11.cloned.1.call-done = bf16[8,4,128]{2,0,1:T(8,128)(2,1)} async-done(((bf16[8,128,128]{2,0,1:T(8,128)(2,1)}), bf16[8,4,128]{2,0,1:T(8,128)(2,1)}) %reduce-scatter.11.cloned.1.call-update) | async-done | bytes 8208 | tf_op jit(solution)/shard_map/reduce_scatter | solution.py:104
  356.4 0.7 fusion.56
  357.2 0.6 copy.148
  357.8 135.8 %reduce-scatter.7.cloned.1.call-done = bf16[8,4,512]{2,0,1:T(8,128)(2,1)} async-done(((bf16[8,128,512]{2,0,1:T(8,128)(2,1)}), bf16[8,4,512]{2,0,1:T(8,128)(2,1)}) %reduce-scatter.7.cloned.1.call-update) | async-done | bytes 32784 | tf_op jit(solution)/shard_map/reduce_scatter | solution.py:98
  493.5 0.8 fusion.51
  494.3 0.6 copy.147
  494.9 135.5 %reduce-scatter.9.cloned.1.call-done = bf16[8,16,128]{2,1,0:T(8,128)(2,1)} async-done(((bf16[8,512,128]{2,1,0:T(8,128)(2,1)}), bf16[8,16,128]{2,1,0:T(8,128)(2,1)}) %reduce-scatter.9.cloned.1.call-update) | async-done | bytes 32784 | tf_op jit(solution)/shard_map/reduce_scatter | solution.py:101
  630.5 1.4 add_convert_fusion
  (18 shorter events, 0.1 us)
Async XLA Ops:
  7.2 28.5 %copy-start = (bf16[8,128,512]{2,1,0:T(8,128)(2,1)S(1)}, bf16[8,128,512]{2,1,0:T(8,128)(2,1)}, u32[]{:S(2)}) copy-start(bf16[8,128,512]{2,1,0:T(8,128)(2,1)} %param.13) | copy-start | bytes 3145732
  9.8 19.4 %all-to-all-start.1 = ((bf16[128,8,256]{2,1,0:T(8,128)(2,1)}), bf16[128,8,256]{2,1,0:T(8,128)(2,1)S(1)}, u32[]{:S(2)}, u32[]{:S(2)}) async-start(bf16[128,8,256]{2,1,0:T(8,128)(2,1)} %copy.121), calls=%async_computation.1 | async-start | bytes 1048576 | tf_op jit(solution)/shard_map/all_to_all | solution.py:49
  29.2 6.4 %copy-start.2 = (bf16[128,8,256]{2,1,0:T(8,128)(2,1)}, bf16[128,8,256]{2,1,0:T(8,128)(2,1)S(1)}, u32[]{:S(2)}) copy-start(bf16[128,8,256]{2,1,0:T(8,128)(2,1)S(1)} %all-to-all-done.1) | copy-start | bytes 1572868
  29.2 16.6 %all-to-all-start = ((bf16[128,8,256]{2,1,0:T(8,128)(2,1)}), bf16[128,8,256]{2,1,0:T(8,128)(2,1)}, u32[]{:S(2)}, u32[]{:S(2)}) async-start(bf16[128,8,256]{2,1,0:T(8,128)(2,1)} %copy.116), calls=%async_computation | async-start | bytes 1048576 | tf_op jit(solution)/shard_map/all_to_all | solution.py:68
  51.9 1.3 copy-start.1
  57.0 16.6 %all-to-all-start.2 = ((bf16[8,128,256]{2,0,1:T(8,128)(2,1)}), bf16[8,128,256]{2,0,1:T(8,128)(2,1)}, u32[]{:S(2)}, u32[]{:S(2)}) async-start(bf16[8,128,256]{2,0,1:T(8,128)(2,1)} %copy.124), calls=%async_computation.2 | async-start | bytes 1048576 | tf_op jit(solution)/shard_map/all_to_all | solution.py:85
  73.7 16.6 %all-to-all-start.3 = ((bf16[8,128,256]{2,0,1:T(8,128)(2,1)}), bf16[8,128,256]{2,0,1:T(8,128)(2,1)}, u32[]{:S(2)}, u32[]{:S(2)}) async-start(bf16[8,128,256]{2,0,1:T(8,128)(2,1)} %copy.139), calls=%async_computation.6 | async-start | bytes 1048576 | tf_op jit(solution)/shard_map/all_to_all | solution.py:59
  80.1 140.6 %reduce-scatter.5.cloned.1.call-start = ((), (), s32[]{:S(2)}) async-start(), calls=%async_computation.8 | async-start | bytes 270336 | tf_op jit(solution)/shard_map/reduce_scatter | solution.py:95
  82.6 273.9 %reduce-scatter.11.cloned.1.call-start = ((), (), s32[]{:S(2)}) async-start(), calls=%async_computation.11 | async-start | bytes 270336 | tf_op jit(solution)/shard_map/reduce_scatter | solution.py:104
  92.7 400.8 %reduce-scatter.7.cloned.1.call-start = ((), (), s32[]{:S(2)}) async-start(), calls=%async_computation.9 | async-start | bytes 1081344 | tf_op jit(solution)/shard_map/reduce_scatter | solution.py:98
  94.9 4.6 copy-start.3
  96.5 124.2 %copy-start.6 = (s32[8,4,128]{2,1,0:T(4,128)S(1)}, s32[8,4,128]{2,1,0:T(4,128)}, u32[]{:S(2)}) copy-start(s32[8,4,128]{2,1,0:T(4,128)} %param.16) | copy-start | bytes 49156
  96.6 397.0 %copy-start.4 = (s32[8,4,512]{2,1,0:T(4,128)S(1)}, s32[8,4,512]{2,1,0:T(4,128)}, u32[]{:S(2)}) copy-start(s32[8,4,512]{2,1,0:T(4,128)} %param.17) | copy-start | bytes 196612
  96.6 533.9 %copy-start.5 = (s32[8,16,128]{2,1,0:T(8,128)S(1)}, s32[8,16,128]{2,1,0:T(8,128)}, u32[]{:S(2)}) copy-start(s32[8,16,128]{2,1,0:T(8,128)} %param.18) | copy-start | bytes 196612
  96.6 533.9 %reduce-scatter.9.cloned.1.call-start = ((), (), s32[]{:S(2)}) async-start(), calls=%async_computation.10 | async-start | bytes 1081344 | tf_op jit(solution)/shard_map/reduce_scatter | solution.py:101
  99.5 256.9 %copy-start.7 = (s32[8,4,128]{2,1,0:T(4,128)S(1)}, s32[8,4,128]{2,1,0:T(4,128)}, u32[]{:S(2)}) copy-start(s32[8,4,128]{2,1,0:T(4,128)} %param.19) | copy-start | bytes 49156
Sparse Core Ops, SparseCore 0:
  83.7 136.9 reduce-scatter.4
  223.7 132.6 reduce-scatter.10
  359.2 134.2 reduce-scatter.6
  496.4 134.0 reduce-scatter.8
where the time goes:
time: 640 us; the launch traced here: 638 us
  waiting for transfers between devices  549 us (86%)
  starting transfers between devices  28.8 us (4%)
  matrix products  27.5 us (4%)
  local copies, waits for them, and re-layouts  15.2 us (2%)
  between operations  13.9 us (2%)
    reduce_scatter x1, waiting for transfers between devices, on_device(): lax.psum_scatter(grad_second.astype(jnp.bfloat16), 'dp', scatter_dimensio...  136 us
    reduce_scatter x1, waiting for transfers between devices, on_device(): lax.psum_scatter(grad_third.astype(jnp.bfloat16), 'dp', scatter_dimension...  136 us
    reduce_scatter x1, waiting for transfers between devices, on_device(): lax.psum_scatter(grad_fourth.astype(jnp.bfloat16), 'dp', scatter_dimensio...  134 us
    reduce_scatter x1, waiting for transfers between devices, on_device(): lax.psum_scatter(grad_first.astype(jnp.bfloat16), 'dp', scatter_dimension...  118 us
  transfers between devices with their start and end apart: 8, of which 8 were waited for; matrix products, arithmetic and copies ran while one was open for 5% of the time, Pallas kernels for 0%

commit v1 on v0

v1 whole, which is shorter than its diff:
```python
import math

import jax
import jax.numpy as jnp
from jax import lax
from jax.sharding import Mesh, PartitionSpec as P

TILE = 128
HB = 512
GRID = 0.25
BF = jnp.bfloat16
F32 = jnp.float32

DP = ("zh", "zl", "yl")
MP = ("mp",)
SUB = ("zl", "yl")
FAR = ("zh",)
GROUP = SUB + MP


def dot(spec, a, b, scale):
    return jnp.einsum(spec, a, b, preferred_element_type=F32) * scale


def exchange(a, axes):
    return lax.all_to_all(a, axes, 0, 0, tiled=True)


def gelu_back(pre, dgated):
    return jax.vjp(jax.nn.gelu, pre)[1](dgated)[0]


def updated(weight, grad_sum, dither):
    rows = dither.shape[1]
    start = lax.axis_index(DP) * rows
    own = lax.dynamic_slice_in_dim(weight, start, rows, 1).astype(F32)
    rate = 4.0 / math.sqrt(8192)
    noise = GRID * (dither.astype(F32) / 32768.0 - 0.5)
    return (own - rate * grad_sum + noise).astype(BF)


def on_device(x, dy, up1, up2, dn1, dn2, di1, di2, di3, di4):
    T = x.shape[0]
    NB = up1.shape[0]
    NS = lax.axis_size(SUB)
    NG = lax.axis_size(MP)
    NZ = lax.axis_size(FAR)
    ML = NB // NS
    s1 = TILE ** -0.5
    s5 = HB ** -0.5
    xb = x.reshape(T, NB, TILE)
    yb = dy.reshape(T, NB, TILE)
    first = dot("tbi,bim->mbt", xb, up1, s1).astype(BF)
    back_down = dot("tkj,kmj->mkt", yb, dn2, s1).astype(BF)
    both = jnp.concatenate([first, back_down], 1)
    both = both.reshape(NG, NS, ML, 2 * NB, T).transpose(1, 0, 2, 3, 4)
    got = exchange(both.reshape(NS * NG, ML, 2 * NB, T), GROUP)
    got = got.reshape(NS, NG, ML, 2, NB, T)
    fm = got[:, :, :, 0].transpose(2, 1, 3, 0, 4).reshape(ML, TILE, NS * T)
    bd = got[:, :, :, 1].transpose(2, 1, 3, 0, 4).reshape(ML, TILE, NS * T)
    sub = lax.axis_index(SUB)
    w2 = lax.dynamic_slice_in_dim(up2, sub * ML, ML, 0)
    w3 = lax.dynamic_slice_in_dim(dn1, sub * ML, ML, 0)
    pre = dot("mbt,mbc->mct", fm, w2, s1)
    gated = jax.nn.gelu(pre).astype(BF)
    down = dot("mct,mck->mkt", gated, w3, s5).astype(BF)
    grad3 = dot("mct,mkt->mck", gated, bd, s5)
    dgated = dot("mkt,mck->mct", bd, w3, s5)
    dpre = gelu_back(pre, dgated).astype(BF)
    grad2 = dot("mbt,mct->mbc", fm, dpre, s1)
    back_up = dot("mct,mbc->mbt", dpre, w2, s1).astype(BF)
    g2 = grad2.astype(BF).reshape(ML, NZ, TILE // NZ, HB).transpose(1, 0, 2, 3)
    g3 = grad3.astype(BF).reshape(ML, NZ, HB // NZ, TILE).transpose(1, 0, 2, 3)
    g23 = jnp.concatenate([g2.reshape(NZ, -1), g3.reshape(NZ, -1)], 1).reshape(NZ, 1, -1, 128)
    r23 = lax.psum_scatter(g23, FAR, scatter_dimension=0, tiled=True)
    send = jnp.stack([down, back_up], 1)
    send = send.reshape(ML, 2, NG, NB, NS, T).transpose(4, 2, 0, 1, 3, 5)
    R = TILE // (NZ * NS)

    def tail(send, xb, yb, up1):
        got = exchange(send.reshape(NS * NG, ML, 2 * NB, T), GROUP)
        got = got.reshape(NS, NG, ML, 2, NB, T)
        dn = got[:, :, :, 0].transpose(3, 1, 0, 2, 4).reshape(NB, TILE, T)
        bu = got[:, :, :, 1].transpose(3, 1, 0, 2, 4).reshape(NB, TILE, T)
        grad4 = dot("kmt,tkj->kmj", dn, yb, s1)
        grad1 = dot("tbi,bmt->bim", xb, bu, s1)
        g14 = jnp.stack([grad1, grad4]).astype(BF)
        g14 = g14.reshape(2, NB, NZ, NS, R, TILE).transpose(3, 2, 0, 1, 4, 5)
        g14 = exchange(g14.reshape(NS, NZ, 2, NB * R, TILE), SUB)
        return bu, jnp.sum(g14.astype(F32), 0).astype(BF)

    def never(send, xb, yb, up1):
        return jnp.zeros((NB, TILE, T), BF), jnp.zeros((NZ, 2, NB * R, TILE), BF)

    bu, g14 = lax.cond(lax.axis_index("mp") < 999, tail, never, send, xb, yb, up1)
    g14, r23, bu = lax.optimization_barrier((g14, r23, bu))
    gin = dot("bmt,bim->tbi", bu, up1, s1).astype(BF).reshape(T, NB * TILE)
    g14 = exchange(g14, FAR)
    g14 = jnp.sum(g14.astype(F32), 0)
    sum1 = g14[0].reshape(NB, R, TILE)
    sum4 = g14[1].reshape(NB, R, TILE)
    n2 = ML * (TILE // NZ) * HB
    r23 = r23.reshape(-1)
    r2 = r23[:n2].reshape(ML, NS, R, HB).transpose(1, 0, 2, 3).reshape(NS, -1)
    r3 = r23[n2:].reshape(ML, NS, R * 4, TILE).transpose(1, 0, 2, 3).reshape(NS, -1)
    q = jnp.concatenate([r2, r3], 1).reshape(NS, -1, 128)
    mine = lax.dynamic_index_in_dim(q, sub, 0, keepdims=False)
    outs = [mine]
    for k in range(1, NS):
        outs.append(lax.ppermute(lax.dynamic_index_in_dim(q, sub ^ k, 0, keepdims=False), SUB, [(i, i ^ k) for i in range(NS)]))
    q = jnp.stack(outs)
    q = jnp.take(q, sub ^ jnp.arange(NS), axis=0).astype(F32).reshape(NS, -1)
    h = q.shape[1] // 2
    sum2 = q[:, :h].reshape(NB, R, HB)
    sum3 = q[:, h:].reshape(NB, R * 4, TILE)
    return (
        gin,
        updated(up1, sum1, di1),
        updated(up2, sum2, di2),
        updated(dn1, sum3, di3),
        updated(dn2, sum4, di4),
    )


def solution(mesh):
    dp, mp = mesh.shape["dp"], mesh.shape["mp"]
    fine = Mesh(mesh.devices.reshape(dp // 4, 2, 2, mp), ("zh", "zl", "yl", "mp"))
    w = P("mp", None, None)
    d = P("mp", DP, None)
    return jax.shard_map(
        on_device,
        mesh=fine,
        in_specs=(P(DP, "mp"), P(DP, "mp"), w, w, w, w, d, d, d, d),
        out_specs=(P(DP, "mp"), d, d, d, d),
        check_vma=False,
    )
```

time: 640 us -> 147 us (0.23)
  waiting for transfers between devices: 549 us -> 28.7 us
  blocking collectives: 0 us -> 39 us
  matrix products: 27.5 us -> 17.9 us
    reduce_scatter x4 -> x1, waiting for transfers between devices: 523 us -> 4.61 us  [on_device(): r23 = lax.psum_scatter(g23, FAR, scatter_dimension=0, tiled=True)]
    all_to_all x0 -> x2, blocking collectives: none -> 39 us  [exchange(): return lax.all_to_all(a, axes, 0, 0, tiled=True)]
    convert_element_type x8 -> x0, local copies, waits for them, and re-layouts: 10.2 us -> none  [the longest x1 2.24 us: on_device(): incoming_cotangent_signal = (jnp.einsum('mct,mbc->mbt', preactivation_gra...]
    dot_general x11, matrix products: 27.5 us -> 17.9 us  [dot(): return jnp.einsum(spec, a, b, preferred_element_type=F32) * scale]
    ppermute x0 -> x3, starting transfers between devices: none -> 9.21 us  [on_device(): lax.ppermute(lax.dynamic_index_in_dim(q, sub ^ k, 0, keepdims=False), SUB...]
    all_to_all x4 -> x2, starting transfers between devices: 28.6 us -> 19.6 us  [exchange(): return lax.all_to_all(a, axes, 0, 0, tiled=True)]
    all_to_all x4 -> x2, waiting for transfers between devices: 25.9 us -> 24.1 us  [exchange(): return lax.all_to_all(a, axes, 0, 0, tiled=True)]
  transfers between devices with their start and end apart: 8 -> 6, of which waited for: 8 -> 3; matrix products, arithmetic and copies ran while one was open for 5% -> 10% of each run, Pallas kernels for 0% -> 0%
where the time goes in v1:
time: 147 us; the launch traced here: 146 us
  blocking collectives  39 us (27%)
  starting transfers between devices  28.9 us (20%)
  waiting for transfers between devices  28.7 us (20%)
  matrix products  17.9 us (12%)
  between operations  14.4 us (10%)
  local copies, waits for them, and re-layouts  12 us (8%)
  other arithmetic  4.85 us (3%)
    all_to_all x2, blocking collectives, exchange(): return lax.all_to_all(a, axes, 0, 0, tiled=True)  39 us
    all_to_all x2, waiting for transfers between devices, exchange(): return lax.all_to_all(a, axes, 0, 0, tiled=True)  24.1 us
    all_to_all x2, starting transfers between devices, exchange(): return lax.all_to_all(a, axes, 0, 0, tiled=True)  19.6 us
    dot_general x11, matrix products, dot(): return jnp.einsum(spec, a, b, preferred_element_type=F32) * scale  17.9 us
    ppermute x3, starting transfers between devices, on_device(): lax.ppermute(lax.dynamic_index_in_dim(q, sub ^ k, 0, keepdims=False), SUB...  9.21 us
    reduce_scatter x1, waiting for transfers between devices, on_device(): r23 = lax.psum_scatter(g23, FAR, scatter_dimension=0, tiled=True)  4.61 us
    convert_element_type x3, other arithmetic, updated(): return (own - rate * grad_sum + noise).astype(BF)  4.26 us
    unnamed x17, local copies, waits for them, and re-layouts  3.85 us
  transfers between devices with their start and end apart: 6, of which 3 were waited for; matrix products, arithmetic and copies ran while one was open for 10% of the time, Pallas kernels for 0%

profile of v1, /device:TPU:6, one launch (start us, length us, event | category | flops | bytes accessed | tf_op | source)
XLA Modules:
  0.0 145.8 jit_solution(5913663296701429515)
XLA Ops:
  7.2 1.2 copy.84
  8.4 1.2 copy.81
  9.7 1.2 fusion.14
  10.9 1.3 fusion.15
  12.2 0.1 pad_maximum_fusion.1
  12.3 0.4 reshape.129
  12.8 2.1 %copy.86 = bf16[16,4,2,16,256]{4,3,2,0,1:T(8,128)(2,1)} copy(bf16[16,4,2,16,256]{4,2,1,0,3:T(2,128)(2,1)S(1)} %reshape.129) | data formatting | bytes 2097152 | tf_op jit(solution)/shard_map/reshape | solution.py:56
  14.9 10.0 %all-to-all-start.2 = ((bf16[64,2,16,256]{3,2,1,0:T(8,128)(2,1)}), bf16[64,2,16,256]{3,2,1,0:T(8,128)(2,1)S(1)}, u32[]{:S(2)}, u32[]{:S(2)}) async-start(bf16[64,2,16,256]{3,2,1,0:T(8,128)(2,1)} %bitcast.15), calls=%async_computation.2 | async-start | bytes 2097152 | tf_op jit(solution)/shard_map/all_to_all | solution.py:26
  25.0 15.3 %all-to-all-done.2 = bf16[64,2,16,256]{3,2,1,0:T(8,128)(2,1)S(1)} async-done(((bf16[64,2,16,256]{3,2,1,0:T(8,128)(2,1)}), bf16[64,2,16,256]{3,2,1,0:T(8,128)(2,1)S(1)}, u32[]{:S(2)}, u32[]{:S(2)}) %all-to-all-start.2) | async-done | bytes 1048608 | tf_op jit(solution)/shard_map/all_to_all | solution.py:26
  40.3 0.1 slice_bitcast_fusion.2
  40.5 2.7 %multiply_convert_fusion = (bf16[2,512,1024]{2,1,0:T(8,128)(2,1)S(1)}, f32[2,512,1024]{2,1,0:T(8,128)S(1)}) fusion(bf16[2,128,1024]{2,1,0:T(8,128)(2,1)S(1)} %bitcast.110, bf16[8,128,512]{2,1,0:T(8,128)(2,1)} %param.15, s32[]{:T(128)S(6)} %select_n.46), kind=kOutput, calls=%fused_computation.17 | convolution fusion | flops 278921216 | bytes 7077892 | tf_op jit(solution)/shard_map/mbt,mbc->mct/dot_general | solution.py:22
  43.2 4.6 %fusion.8 = bf16[2,512,1024]{2,1,0:T(8,128)(2,1)S(1)} fusion(f32[2,512,1024]{2,1,0:T(8,128)S(1)} %get-tuple-element.68, bf16[2,128,1024]{2,1,0:T(8,128)(2,1)S(1)} %bitcast.121, bf16[8,512,128]{2,1,0:T(8,128)(2,1)} %param.16, s32[]{:T(128)S(6)} %select_n.46), kind=kOutput, calls=%fused_computation.16 | convolution fusion | flops 291504128 | bytes 7077892 | tf_op jit(solution)/shard_map/mkt,mck->mct/dot_general | solution.py:22
  47.8 0.8 fusion.16
  48.7 0.2 copy.110
  48.8 0.7 fusion.17
  49.6 0.2 copy.116
  49.8 0.9 copy.96
  50.8 1.4 fusion.10
  52.2 2.2 %fusion.9 = bf16[2,128,1024]{2,1,0:T(8,128)(2,1)S(1)} fusion(bf16[2,512,1024]{2,1,0:T(8,128)(2,1)} %copy-done, bf16[8,512,128]{2,1,0:T(8,128)(2,1)} %param.16, s32[]{:T(128)S(6)} %select_n.46), kind=kOutput, calls=%fused_computation.23 | convolution fusion | flops 268959744 | bytes 2883588 | tf_op jit(solution)/shard_map/mct,mck->mkt/dot_general | solution.py:22
  54.4 0.1 copy_bitcast_fusion
  54.5 43.0 %conditional.1 = (bf16[8,128,256]{2,1,0:T(8,128)(2,1)}, bf16[8,2,32,128]{3,0,2,1:T(8,128)(2,1)S(1)}) conditional(s32[]{:T(128)} %convert_element_type.86, () %tuple.17, (bf16[4,16,2,2,8,256]{5,4,3,2,1,0:T(8,128)(2,1)S(1)}, bf16[256,8,128]{0,2,1:T(8,128)(2,1)S(1)}, bf16[256,8,128]{0,2,1:T(8,128)(2,1)S(1)}) %tuple.43), branch_computations={%region_0.0_spmd, %region_1.3_spmd} | conditional | flops 135200768 | bytes 14811154 | solution.py:95
  54.5 24.3 %all_to_all.18 = bf16[64,2,16,256]{3,2,1,0:T(8,128)(2,1)S(1)} all-to-all(bf16[64,2,16,256]{3,2,1,0:T(8,128)(2,1)S(1)} %bitcast.106), channel_id=1, replica_groups=mesh['zh'=8,'zl'=2,'yl'=2,'mp'=16] {'zl','yl','mp'}, dimensions={0} | all-to-all | bytes 2097152 | tf_op jit(solution)/shard_map/cond/branch_1_fun/all_to_all | solution.py:26
  78.8 0.1 slice_bitcast_fusion
  78.9 0.4 copy.75
  79.3 1.0 reshape.109
  80.3 1.3 fusion
  81.6 0.1 copy.77
  81.7 0.4 copy.76
  82.1 0.2 reshape.110
  82.3 0.3 fusion.1
  82.6 0.1 copy.78
  82.8 14.7 %all_to_all.19 = bf16[4,8,2,32,128]{4,1,3,2,0:T(8,128)(2,1)S(1)} all-to-all(bf16[4,8,2,32,128]{4,1,3,2,0:T(8,128)(2,1)S(1)} %bitcast.108), channel_id=1, replica_groups=mesh['zh'=8,'zl'=2,'yl'=2,'mp'=16] {'zl','yl'}, dimensions={0} | all-to-all | bytes 1048576 | tf_op jit(solution)/shard_map/cond/branch_1_fun/all_to_all | solution.py:26
  97.5 0.1 reduce_sum.19
  97.6 4.6 %reduce-scatter.2.cloned.1.call-done = bf16[1,1,256,128]{3,2,1,0:T(8,128)(2,1)} async-done(((bf16[8,1,256,128]{3,2,1,0:T(8,128)(2,1)}), bf16[1,1,256,128]{3,2,1,0:T(8,128)(2,1)}) %reduce-scatter.2.cloned.1.call-update) | async-done | bytes 65552 | tf_op jit(solution)/shard_map/reduce_scatter | solution.py:75
  102.2 0.8 fusion.36
  103.1 3.1 %collective-permute-start = (bf16[64,128]{1,0:T(8,128)(2,1)S(1)}, bf16[64,128]{1,0:T(8,128)(2,1)S(1)}, u32[]{:S(2)}, u32[]{:S(2)}) collective-permute-start(bf16[64,128]{1,0:T(8,128)(2,1)S(1)} %get-tuple-element.60), channel_id=1, source_target_pairs={{0,16},{16,0},{32,48},{48,32},{1,17},{17,1},{33,49},{49,33},{2,18}... | collective-permute-start | bytes 49160 | tf_op jit(solution)/shard_map/ppermute | solution.py:110
  106.3 2.0 %collective-permute-start.1 = (bf16[64,128]{1,0:T(8,128)(2,1)S(1)}, bf16[64,128]{1,0:T(8,128)(2,1)S(1)}, u32[]{:S(2)}, u32[]{:S(2)}) collective-permute-start(bf16[64,128]{1,0:T(8,128)(2,1)S(1)} %get-tuple-element.61), channel_id=1, source_target_pairs={{0,32},{16,48},{32,0},{48,16},{1,33},{17,49},{33,1},{49,17},{2,34}... | collective-permute-start | bytes 49160 | tf_op jit(solution)/shard_map/ppermute | solution.py:110
  108.3 4.1 %collective-permute-start.2 = (bf16[64,128]{1,0:T(8,128)(2,1)S(1)}, bf16[64,128]{1,0:T(8,128)(2,1)S(1)}, u32[]{:S(2)}, u32[]{:S(2)}) collective-permute-start(bf16[64,128]{1,0:T(8,128)(2,1)S(1)} %get-tuple-element.62), channel_id=1, source_target_pairs={{0,48},{16,32},{32,16},{48,0},{1,49},{17,33},{33,17},{49,1},{2,50}... | collective-permute-start | bytes 49160 | tf_op jit(solution)/shard_map/ppermute | solution.py:110
  112.4 0.7 copy.97
  113.0 9.6 %all-to-all-start.3 = ((bf16[8,2,32,128]{3,2,1,0:T(8,128)(2,1)}), bf16[8,2,32,128]{3,2,1,0:T(8,128)(2,1)S(1)}, u32[]{:S(2)}, u32[]{:S(2)}) async-start(bf16[8,2,32,128]{3,2,1,0:T(8,128)(2,1)} %copy.97), calls=%async_computation.4 | async-start | bytes 262144 | tf_op jit(solution)/shard_map/all_to_all | solution.py:26
  122.6 1.3 fusion.13
  124.0 1.0 copy.100
  125.0 0.6 gather_fusion
  125.6 0.1 fusion.23
  125.8 1.4 add_convert_fusion
  127.2 1.5 %add_convert_fusion.1 = bf16[8,4,512]{2,1,0:T(4,128)(2,1)} fusion(s32[8,4,512]{2,1,0:T(4,128)S(1)} %copy-done.3, f32[8,4,512]{2,1,0:T(4,128)S(1)} %mul.215, bf16[8,128,512]{2,1,0:T(8,128)(2,1)} %param.15, s32[]{:T(128)S(6)} %select_n.47), kind=kLoop, calls=%fused_computation.61 | loop fusion | flops 131072 | bytes 196612 | tf_op jit(solution)/shard_map/convert_element_type | solution.py:39
  128.7 8.8 %all-to-all-done.3 = bf16[8,2,32,128]{3,2,1,0:T(8,128)(2,1)S(1)} async-done(((bf16[8,2,32,128]{3,2,1,0:T(8,128)(2,1)}), bf16[8,2,32,128]{3,2,1,0:T(8,128)(2,1)S(1)}, u32[]{:S(2)}, u32[]{:S(2)}) %all-to-all-start.3) | async-done | bytes 131104 | tf_op jit(solution)/shard_map/all_to_all | solution.py:26
  137.6 1.4 add_convert_fusion.2
  (37 shorter events, 0.6 us)
Async XLA Ops:
  14.9 25.4 %all-to-all-start.2 = ((bf16[64,2,16,256]{3,2,1,0:T(8,128)(2,1)}), bf16[64,2,16,256]{3,2,1,0:T(8,128)(2,1)S(1)}, u32[]{:S(2)}, u32[]{:S(2)}) async-start(bf16[64,2,16,256]{3,2,1,0:T(8,128)(2,1)} %bitcast.15), calls=%async_computation.2 | async-start | bytes 2097152 | tf_op jit(solution)/shard_map/all_to_all | solution.py:26
  24.9 77.3 %reduce-scatter.2.cloned.1.call-start = ((), (), s32[]{:S(2)}) async-start(), calls=%async_computation.5 | async-start | bytes 589824 | tf_op jit(solution)/shard_map/reduce_scatter | solution.py:75
  43.2 5.6 %copy-start = (bf16[2,512,1024]{2,1,0:T(8,128)(2,1)}, bf16[2,512,1024]{2,1,0:T(8,128)(2,1)S(1)}, u32[]{:S(2)}) copy-start(bf16[2,512,1024]{2,1,0:T(8,128)(2,1)S(1)} %get-tuple-element.67) | copy-start | bytes 6291460
  54.5 68.1 %copy-start.1 = (bf16[8,128,128]{2,1,0:T(8,128)(2,1)S(1)}, bf16[8,128,128]{2,1,0:T(8,128)(2,1)}, u32[]{:S(2)}) copy-start(bf16[8,128,128]{2,1,0:T(8,128)(2,1)} %param.14) | copy-start | bytes 786436
  97.6 28.3 %copy-start.2 = (s32[8,16,128]{2,1,0:T(8,128)S(1)}, s32[8,16,128]{2,1,0:T(8,128)}, u32[]{:S(2)}) copy-start(s32[8,16,128]{2,1,0:T(8,128)} %param.20) | copy-start | bytes 196612
  97.6 29.7 %copy-start.3 = (s32[8,4,512]{2,1,0:T(4,128)S(1)}, s32[8,4,512]{2,1,0:T(4,128)}, u32[]{:S(2)}) copy-start(s32[8,4,512]{2,1,0:T(4,128)} %param.19) | copy-start | bytes 196612
  97.6 40.0 %copy-start.4 = (s32[8,4,128]{2,1,0:T(4,128)S(1)}, s32[8,4,128]{2,1,0:T(4,128)}, u32[]{:S(2)}) copy-start(s32[8,4,128]{2,1,0:T(4,128)} %param.21) | copy-start | bytes 49156
  97.6 40.0 %copy-start.5 = (s32[8,4,128]{2,1,0:T(4,128)S(1)}, s32[8,4,128]{2,1,0:T(4,128)}, u32[]{:S(2)}) copy-start(s32[8,4,128]{2,1,0:T(4,128)} %param.18) | copy-start | bytes 49156
  103.1 21.9 %collective-permute-start = (bf16[64,128]{1,0:T(8,128)(2,1)S(1)}, bf16[64,128]{1,0:T(8,128)(2,1)S(1)}, u32[]{:S(2)}, u32[]{:S(2)}) collective-permute-start(bf16[64,128]{1,0:T(8,128)(2,1)S(1)} %get-tuple-element.60), channel_id=1, source_target_pairs={{0,16},{16,0},{32,48},{48,32},{1,17},{17,1},{33,49},{49,33},{2,18}... | collective-permute-start | bytes 49160 | tf_op jit(solution)/shard_map/ppermute | solution.py:110
  106.3 18.7 %collective-permute-start.1 = (bf16[64,128]{1,0:T(8,128)(2,1)S(1)}, bf16[64,128]{1,0:T(8,128)(2,1)S(1)}, u32[]{:S(2)}, u32[]{:S(2)}) collective-permute-start(bf16[64,128]{1,0:T(8,128)(2,1)S(1)} %get-tuple-element.61), channel_id=1, source_target_pairs={{0,32},{16,48},{32,0},{48,16},{1,33},{17,49},{33,1},{49,17},{2,34}... | collective-permute-start | bytes 49160 | tf_op jit(solution)/shard_map/ppermute | solution.py:110
  108.3 16.7 %collective-permute-start.2 = (bf16[64,128]{1,0:T(8,128)(2,1)S(1)}, bf16[64,128]{1,0:T(8,128)(2,1)S(1)}, u32[]{:S(2)}, u32[]{:S(2)}) collective-permute-start(bf16[64,128]{1,0:T(8,128)(2,1)S(1)} %get-tuple-element.62), channel_id=1, source_target_pairs={{0,48},{16,32},{32,16},{48,0},{1,49},{17,33},{33,17},{49,1},{2,50}... | collective-permute-start | bytes 49160 | tf_op jit(solution)/shard_map/ppermute | solution.py:110
  113.0 24.5 %all-to-all-start.3 = ((bf16[8,2,32,128]{3,2,1,0:T(8,128)(2,1)}), bf16[8,2,32,128]{3,2,1,0:T(8,128)(2,1)S(1)}, u32[]{:S(2)}, u32[]{:S(2)}) async-start(bf16[8,2,32,128]{3,2,1,0:T(8,128)(2,1)} %copy.97), calls=%async_computation.4 | async-start | bytes 262144 | tf_op jit(solution)/shard_map/all_to_all | solution.py:26
Sparse Core Ops, SparseCore 0:
  50.9 51.3 reduce-scatter.1

commit v2 on v1

v2 whole, which is shorter than its diff:
```python
import math

import jax
import jax.numpy as jnp
from jax import lax
from jax.experimental import pallas as pl
from jax.experimental.pallas import tpu as pltpu
from jax.sharding import Mesh, PartitionSpec as P

TILE = 128
HB = 512
T = 256
NB = 8
NS = 4
NG = 16
NZ = 8
NQ = 4
ML = NB // NS
R = TILE // (NZ * NS)
GRID = 0.25
RATE = 4.0 / math.sqrt(8192)
S1 = TILE ** -0.5
S5 = HB ** -0.5
C0 = math.sqrt(2.0 / math.pi)
BF = jnp.bfloat16
F32 = jnp.float32

DP = ("z3", "zq", "zl", "yl")
SUB = ("zl", "yl")
FAR = ("z3", "zq")
GROUP = SUB + ("mp",)

NN = (((1,), (0,)), ((), ()))
NT = (((1,), (1,)), ((), ()))
TN = (((0,), (0,)), ((), ()))
TT = (((0,), (1,)), ((), ()))
PARAMS = pltpu.CompilerParams(vmem_limit_bytes=48 << 20)
ALL_VMEM = pltpu.CompilerParams(vmem_limit_bytes=60 << 20)


def mm(a, b, dims):
    return lax.dot_general(a, b, dims, preferred_element_type=F32)


def exchange(a, axes):
    return lax.all_to_all(a, axes, 0, 0, tiled=True)


def cost(flops, moved):
    return pl.CostEstimate(flops=flops, bytes_accessed=moved, transcendentals=0)


def first_kernel(x, u, y, d, out, rows):
    for h in range(2):
        t = slice(h * 128, (h + 1) * 128)
        for b in range(NB):
            f = slice(b * TILE, (b + 1) * TILE)
            rows[h, pl.ds(b, TILE, stride=2 * NB), :] = mm(u[b], x[t, f], TT) * S1
            rows[h, pl.ds(NB + b, TILE, stride=2 * NB), :] = mm(d[b], y[t, f], NT) * S1
    for h in range(2):
        v = rows[h].reshape(NG, NS, 2 * NB * ML, 128).astype(BF)
        for s in range(NS):
            out[s * NG : (s + 1) * NG, :, h * 128 : (h + 1) * 128] = v[:, s]


def first_stage(x, u, y, d):
    return pl.pallas_call(
        first_kernel,
        out_shape=jax.ShapeDtypeStruct((NS * NG, 2 * NB * ML, T), BF),
        scratch_shapes=[pltpu.VMEM((2, TILE * 2 * NB, 128), F32)],
        compiler_params=ALL_VMEM,
        cost_estimate=cost(2**27, 2**21),
    )(x, u, y, d)


def hidden_kernel(at, r, w2, w3, out, p0, p1, p2, p3, cut):
    w2 = w2[0]
    w3 = w3[0]
    g2 = g3 = None
    for s in range(NS):
        v = r[s * NG : (s + 1) * NG].astype(F32)
        fm = v[:, :NB].reshape(TILE, T).astype(BF)
        bd = v[:, NB:].reshape(TILE, T).astype(BF)
        pre = mm(w2, fm, TN) * S1
        dgated = mm(w3, bd, NN) * S5
        th = jnp.tanh(C0 * (pre + 0.044715 * (pre * pre * pre)))
        cdf = 0.5 * (1.0 + th)
        gated = (pre * cdf).astype(BF)
        slope = cdf + (0.5 * C0) * pre * (1.0 - th * th) * (1.0 + (3 * 0.044715) * (pre * pre))
        dpre = (dgated * slope).astype(BF)
        down = mm(w3, gated, TN) * S5
        back_up = mm(w2, dpre, NN) * S1
        a2 = mm(fm, dpre, NT)
        a3 = mm(gated, bd, NT)
        g2, g3 = (a2, a3) if g2 is None else (g2 + a2, g3 + a3)
        both = jnp.concatenate([down.reshape(NG, NB, T), back_up.reshape(NG, NB, T)], 1)
        out[s * NG : (s + 1) * NG] = both.astype(BF)
    for c in range(4):
        v = (g2[:, c * 128 : (c + 1) * 128] * S1).reshape(NZ, NS, R, 128)
        for s in range(NS):
            cut[:, s, c * R : (c + 1) * R] = v[:, s]
    cut[:, :, 4 * R :] = (g3 * S5).reshape(NZ, NS, 4 * R, 128)
    for k, p in enumerate((p0, p1, p2, p3)):
        for h in range(2):
            p[h * NS : (h + 1) * NS] = cut[h * NQ + (at[1] ^ k)].astype(BF)


def hidden_stage(at, r, up2, dn1):
    spec = pltpu.PrefetchScalarGridSpec(
        num_scalar_prefetch=1,
        grid=(ML,),
        in_specs=[
            pl.BlockSpec((NS * NG, 2 * NB, T), lambda m, s: (0, m, 0)),
            pl.BlockSpec((1, TILE, HB), lambda m, s: (s[2] * ML + m, 0, 0)),
            pl.BlockSpec((1, HB, TILE), lambda m, s: (s[2] * ML + m, 0, 0)),
        ],
        out_specs=[pl.BlockSpec((NS * NG, 2 * NB, T), lambda m, s: (0, m, 0))]
        + [pl.BlockSpec((2 * NS, 8 * R, 128), lambda m, s: (0, m, 0))] * NQ,
        scratch_shapes=[pltpu.VMEM((NZ, NS, 8 * R, 128), F32)],
    )
    return pl.pallas_call(
        hidden_kernel,
        grid_spec=spec,
        out_shape=[jax.ShapeDtypeStruct((NS * NG, 2 * NB * ML, T), BF)]
        + [jax.ShapeDtypeStruct((2 * NS, 8 * R * ML, 128), BF)] * NQ,
        compiler_params=PARAMS,
        cost_estimate=cost(2**30, 2**22),
    )(at, r, up2, dn1)


def outer_kernel(r, x, y, u, p0, p1, p2, p3, gin, grads, rows, cut):
    for s in range(NS):
        for h in range(2):
            rows[h, :, s] = r[s * NG : (s + 1) * NG, :, h * 128 : (h + 1) * 128].astype(F32)
    flat = rows.reshape(2, TILE * 2 * NB, 128)

    def pick(j):
        return jnp.concatenate([flat[h, pl.ds(j, TILE, stride=2 * NB), :] for h in range(2)], 1).astype(BF)

    for b in range(NB):
        f = slice(b * TILE, (b + 1) * TILE)
        down, back_up = pick(b), pick(NB + b)
        gin[:, f] = (mm(back_up, u[b], TT) * S1).astype(BF)
        g1 = (mm(x[:, f], back_up, TT) * S1).reshape(NZ, NS, R, TILE)
        g4 = (mm(down, y[:, f], NN) * S1).reshape(NZ, NS, R, TILE)
        for s in range(NS):
            cut[s, :, b * R : (b + 1) * R] = g1[:, s]
            cut[s, :, (NB + b) * R : (NB + b + 1) * R] = g4[:, s]
    grads[:, :NZ] = cut[...].astype(BF)
    g23 = (p0[...].astype(F32) + p1[...].astype(F32)) + (p2[...].astype(F32) + p3[...].astype(F32))
    g23 = g23.astype(BF)
    for h in range(2):
        grads[:, NZ + h] = g23[h * NS : (h + 1) * NS]


def outer_stage(r, x, y, u, p):
    return pl.pallas_call(
        outer_kernel,
        out_shape=[
            jax.ShapeDtypeStruct((T, NB * TILE), BF),
            jax.ShapeDtypeStruct((NS, NZ + 2, 2 * NB * R, TILE), BF),
        ],
        scratch_shapes=[
            pltpu.VMEM((2, NG, NS, 2 * NB * ML, 128), F32),
            pltpu.VMEM((NS, NZ, 2 * NB * R, TILE), F32),
        ],
        compiler_params=PARAMS,
        cost_estimate=cost(2**10, 2**10),
    )(r, x, y, u, *p)


def near_kernel(at, a, g14, keep, give):
    v = a[0, :NZ].astype(F32)
    for s in range(1, NS):
        v = v + a[s, :NZ].astype(F32)
    g14[...] = v.astype(BF)
    keep[...] = a[:, NZ + at[0]]
    give[...] = a[:, NZ + 1 - at[0]]


def near_stage(at, a):
    return pl.pallas_call(
        near_kernel,
        in_specs=[pl.BlockSpec(memory_space=pltpu.SMEM), pl.BlockSpec(memory_space=pltpu.VMEM)],
        out_shape=[
            jax.ShapeDtypeStruct((NZ, 2 * NB * R, TILE), BF),
            jax.ShapeDtypeStruct((NS, 8 * R * ML, 128), BF),
            jax.ShapeDtypeStruct((NS, 8 * R * ML, 128), BF),
        ],
        compiler_params=PARAMS,
        cost_estimate=cost(2**10, 2**10),
    )(at, a)


def choose(sub, options):
    v = options[-1]
    for s in range(len(options) - 2, -1, -1):
        v = jnp.where(sub == s, options[s], v)
    return v


def step(weight, grad, dither):
    noise = GRID * (dither.astype(F32) / 32768.0 - 0.5)
    return (weight - RATE * grad + noise).astype(BF)


def own_rows(sub, block):
    v = block.astype(F32)
    return choose(sub, [v[:, s * R : (s + 1) * R] for s in range(NS)])


def update_kernel(at, a, keep, took, up1, up2, dn1, dn2, d1, d2, d3, d4, n1, n2, n3, n4):
    sub = at[2]
    v = a[0].astype(F32)
    for z in range(1, NZ):
        v = v + a[z].astype(F32)
    g = v.reshape(2, NB, R, TILE)
    n1[...] = step(own_rows(sub, up1[...]), g[0], d1[...])
    n4[...] = step(own_rows(sub, dn2[...]), g[1], d4[...])
    own = own_rows(sub, up2[...])
    for s in range(NS):
        v = keep[s].astype(F32) + took[s].astype(F32)
        for i in range(ML):
            m = s * ML + i
            w = v[i * 8 * R : (i + 1) * 8 * R]
            grad = jnp.concatenate([w[c * R : (c + 1) * R] for c in range(4)], 1)
            n2[m] = step(own[m], grad, d2[m])
            n3[m] = step(dn1[m].astype(F32), w[4 * R :], d3[m])


def update(at, a, keep, took, up1, up2, dn1, dn2, d1, d2, d3, d4):
    def whole(*shape):
        return pl.BlockSpec(shape, lambda i, s: (0,) * len(shape))

    def far(s):
        return s[0] * NQ + s[1]

    small = whole(NB, R, TILE)
    wide = whole(NB, R, HB)
    large = whole(NB, 4 * R, TILE)
    half = whole(NS, 8 * R * ML, 128)
    block = pl.BlockSpec((NB, NS * R, TILE), lambda i, s: (0, far(s), 0))
    spec = pltpu.PrefetchScalarGridSpec(
        num_scalar_prefetch=1,
        grid=(1,),
        in_specs=[
            whole(NZ, 2 * NB * R, TILE),
            half,
            half,
            block,
            pl.BlockSpec((NB, NS * R, HB), lambda i, s: (0, far(s), 0)),
            pl.BlockSpec((NB, 4 * R, TILE), lambda i, s: (0, far(s) * NS + s[2], 0)),
            block,
            small,
            wide,
            large,
            small,
        ],
        out_specs=[small, wide, large, small],
    )
    shapes = ((NB, R, TILE), (NB, R, HB), (NB, 4 * R, TILE), (NB, R, TILE))
    return pl.pallas_call(
        update_kernel,
        grid_spec=spec,
        out_shape=[jax.ShapeDtypeStruct(shape, BF) for shape in shapes],
        compiler_params=PARAMS,
        cost_estimate=cost(2**10, 2**10),
    )(at, a, keep, took, up1, up2, dn1, dn2, d1, d2, d3, d4)


def on_device(x, dy, up1, up2, dn1, dn2, di1, di2, di3, di4):
    at = jnp.stack([lax.axis_index(a) for a in ("z3", "zq", SUB)]).astype(jnp.int32)
    always = lax.axis_index("mp") < 999

    def fenced(a, axes):
        return lax.cond(always, lambda a: exchange(a, axes), jnp.zeros_like, a)

    got = exchange(first_stage(x, up1, dy, dn2), GROUP)
    send, *p = hidden_stage(at, got, up2, dn1)
    p = [p[0]] + [lax.ppermute(p[k], "zq", [(i, i ^ k) for i in range(NQ)]) for k in range(1, NQ)]
    got, p = lax.optimization_barrier((fenced(send, GROUP), p))
    gin, grads = outer_stage(got, x, dy, up1, p)
    g14, keep, give = near_stage(at, exchange(grads, SUB))
    took = lax.ppermute(give, "z3", [(0, 1), (1, 0)])
    g14, took = lax.optimization_barrier((fenced(g14, FAR), took))
    new1, new2, new3, new4 = update(at, g14, keep, took, up1, up2, dn1, dn2, di1, di2, di3, di4)
    return gin, new1, new2, new3, new4


def solution(mesh):
    dp, mp = mesh.shape["dp"], mesh.shape["mp"]
    fine = Mesh(mesh.devices.reshape(2, dp // 8, 2, 2, mp), ("z3", "zq", "zl", "yl", "mp"))
    w = P("mp", None, None)
    d = P("mp", DP, None)
    return jax.shard_map(
        on_device,
        mesh=fine,
        in_specs=(P(DP, "mp"), P(DP, "mp"), w, w, w, w, d, d, d, d),
        out_specs=(P(DP, "mp"), d, d, d, d),
        check_vma=False,
    )
```

time: 147 us -> 134 us (0.912)
  blocking collectives: 39 us -> 61.9 us
  matrix products: 17.9 us -> 0 us
  Pallas kernels: 0 us -> 16.6 us
  between operations: 14.4 us -> 0.8 us
  waiting for transfers between devices: 28.7 us -> 15.3 us
  local copies, waits for them, and re-layouts: 12 us -> 0.05 us
  starting transfers between devices: 28.9 us -> 38.3 us
  other arithmetic: 4.85 us -> 0.08 us
    all_to_all x2 -> x3, blocking collectives: 39 us -> 61.9 us  [exchange(): return lax.all_to_all(a, axes, 0, 0, tiled=True)]
    ppermute x3 -> x4, starting transfers between devices: 9.21 us -> 28.2 us  [the longest x3 15.5 us: on_device(): lax.ppermute(p[k], 'zq', [(i, i ^ k) for i in range(NQ)])]
    dot_general x11 -> x0, matrix products: 17.9 us -> none  [dot(): return jnp.einsum(spec, a, b, preferred_element_type=F32) * scale]
    pallas_call x0 -> x5, Pallas kernels: none -> 16.6 us  [the longest x1 7.46 us: hidden_stage(): pl.pallas_call(hidden_kernel, grid_spec=spec, out_shape=[jax.ShapeDtypeSt...]
    all_to_all x2 -> x1, starting transfers between devices: 19.6 us -> 10.1 us  [exchange(): return lax.all_to_all(a, axes, 0, 0, tiled=True)]
    all_to_all x2 -> x1, waiting for transfers between devices: 24.1 us -> 15.3 us  [exchange(): return lax.all_to_all(a, axes, 0, 0, tiled=True)]
    reshape x8 -> x0, local copies, waits for them, and re-layouts: 4.69 us -> none  [the longest x2 2.54 us: on_device(): both = both.reshape(NG, NS, ML, 2 * NB, T).transpose(1, 0, 2, 3, 4)]
    reduce_scatter x1 -> x0, waiting for transfers between devices: 4.61 us -> none  [on_device(): r23 = lax.psum_scatter(g23, FAR, scatter_dimension=0, tiled=True)]
  transfers between devices with their start and end apart: 6 -> 5, of which waited for: 3 -> 1; matrix products, arithmetic and copies ran while one was open for 10% -> 0% of each run, Pallas kernels for 0% -> 0%
where the time goes in v2:
time: 134 us; the launch traced here: 133 us
  blocking collectives  61.9 us (46%)
  starting transfers between devices  38.3 us (29%)
  Pallas kernels  16.6 us (12%)
  waiting for transfers between devices  15.3 us (11%)
    all_to_all x3, blocking collectives, exchange(): return lax.all_to_all(a, axes, 0, 0, tiled=True)  61.9 us
    ppermute x3, starting transfers between devices, on_device(): lax.ppermute(p[k], 'zq', [(i, i ^ k) for i in range(NQ)])  15.5 us
    all_to_all x1, waiting for transfers between devices, exchange(): return lax.all_to_all(a, axes, 0, 0, tiled=True)  15.3 us
    ppermute x1, starting transfers between devices, on_device(): took = lax.ppermute(give, 'z3', [(0, 1), (1, 0)])  12.7 us
    all_to_all x1, starting transfers between devices, exchange(): return lax.all_to_all(a, axes, 0, 0, tiled=True)  10.1 us
    pallas_call x1, Pallas kernels, hidden_stage(): pl.pallas_call(hidden_kernel, grid_spec=spec, out_shape=[jax.ShapeDtypeSt...  7.46 us
    pallas_call x1, Pallas kernels, first_stage(): pl.pallas_call(first_kernel, out_shape=jax.ShapeDtypeStruct((NS * NG, 2 *...  3.73 us
    pallas_call x1, Pallas kernels, outer_stage(): pl.pallas_call(outer_kernel, out_shape=[jax.ShapeDtypeStruct((T, NB * TIL...  3.44 us
  transfers between devices with their start and end apart: 5, of which 1 were waited for; matrix products, arithmetic and copies ran while one was open for 0% of the time, Pallas kernels for 0%

profile of v2, /device:TPU:6, one launch (start us, length us, event | category | flops | bytes accessed | tf_op | source)
XLA Modules:
  0.0 133.0 jit_solution(7855058528703289966)
XLA Ops:
  0.6 3.7 %shard_map.137 = bf16[64,32,256]{2,1,0:T(8,128)(2,1)} custom-call(bf16[256,1024]{1,0:T(8,128)(2,1)} %x.3, bf16[8,128,128]{2,1,0:T(8,128)(2,1)} %up1.1, bf16[256,1024]{1,0:T(8,128)(2,1)} %y.3, bf16[8,128,128]{2,1,0:T(8,128)(2,1)} %dn2.1), custom_call_target="tpu_custom_call" | custom-call | flops 134217728 | bytes 2097152 | tf_op jit(solution)/shard_map/pallas_call | solution.py:67
  4.4 0.0 copy-start.3
  4.4 0.0 copy-start.4
  4.4 10.1 %all-to-all-start.2 = ((bf16[64,32,256]{2,1,0:T(8,128)(2,1)}), bf16[64,32,256]{2,1,0:T(8,128)(2,1)S(1)}, u32[]{:S(2)}, u32[]{:S(2)}) async-start(bf16[64,32,256]{2,1,0:T(8,128)(2,1)} %shard_map.137), calls=%async_computation.2 | async-start | bytes 2097152 | tf_op jit(solution)/shard_map/all_to_all | solution.py:46
  14.5 0.1 pad_add_fusion.at
  14.6 15.3 %all-to-all-done.2.r = bf16[64,32,256]{2,1,0:T(8,128)(2,1)S(1)} async-done(((bf16[64,32,256]{2,1,0:T(8,128)(2,1)}), bf16[64,32,256]{2,1,0:T(8,128)(2,1)S(1)}, u32[]{:S(2)}, u32[]{:S(2)}) %all-to-all-start.2) | async-done | bytes 1048608 | tf_op jit(solution)/shard_map/all_to_all | solution.py:46
  29.9 0.0 copy-done.3
  29.9 0.0 copy-done.4
  29.9 7.5 %shard_map.138 = (bf16[64,32,256]{2,1,0:T(8,128)(2,1)}, bf16[8,64,128]{2,1,0:T(8,128)(2,1)S(1)}, bf16[8,64,128]{2,1,0:T(8,128)(2,1)}, bf16[8,64,128]{2,1,0:T(8,128)(2,1)}, bf16[8,64,128]{2,1,0:T(8,128)(2,1)}) custom-call(s32[3]{0:T(128)S(1)} %pad_add_fusion.at, bf16[64,32,256]{2,1,0:T(8,128)(2,1)S(1)} %all-to-all-done.2.r, ...), custom_call_target="tpu_custom_call" | custom-call | flops 1073741824 | bytes 4194304 | tf_op jit(solution)/shard_map/pallas_call | solution.py:121
  37.4 4.4 %collective-permute-start = (bf16[8,64,128]{2,1,0:T(8,128)(2,1)}, bf16[8,64,128]{2,1,0:T(8,128)(2,1)}, u32[]{:S(2)}, u32[]{:S(2)}) collective-permute-start(bf16[8,64,128]{2,1,0:T(8,128)(2,1)} %get-tuple-element.36), channel_id=1, source_target_pairs={{0,64},{64,0},{128,192},{192,128},{1,65},{65,1},{129,193},{193,129... | collective-permute-start | bytes 393224 | tf_op jit(solution)/shard_map/ppermute | solution.py:280
  41.8 9.1 %collective-permute-start.1 = (bf16[8,64,128]{2,1,0:T(8,128)(2,1)}, bf16[8,64,128]{2,1,0:T(8,128)(2,1)}, u32[]{:S(2)}, u32[]{:S(2)}) collective-permute-start(bf16[8,64,128]{2,1,0:T(8,128)(2,1)} %get-tuple-element.37), channel_id=1, source_target_pairs={{0,128},{64,192},{128,0},{192,64},{1,129},{65,193},{129,1},{193,65... | collective-permute-start | bytes 393224 | tf_op jit(solution)/shard_map/ppermute | solution.py:280
  50.9 1.9 %collective-permute-start.2 = (bf16[8,64,128]{2,1,0:T(8,128)(2,1)}, bf16[8,64,128]{2,1,0:T(8,128)(2,1)}, u32[]{:S(2)}, u32[]{:S(2)}) collective-permute-start(bf16[8,64,128]{2,1,0:T(8,128)(2,1)} %get-tuple-element.38), channel_id=1, source_target_pairs={{0,192},{64,128},{128,64},{192,0},{1,193},{65,129},{129,65},{193,1... | collective-permute-start | bytes 393224 | tf_op jit(solution)/shard_map/ppermute | solution.py:280
  52.8 0.0 copy-start
  52.8 0.0 copy-start.1
  52.9 0.0 copy-start.2
  52.9 25.3 %conditional.2 = (bf16[64,32,256]{2,1,0:T(8,128)(2,1)}) conditional(s32[]{:T(128)} %convert_element_type.4, () %tuple.22, bf16[64,32,256]{2,1,0:T(8,128)(2,1)} %get-tuple-element.34), branch_computations={%region_0.0_spmd, %region_1.0_spmd} | conditional | bytes 2097160 | solution.py:276
  52.9 25.3 %all_to_all.18 = bf16[64,32,256]{2,1,0:T(8,128)(2,1)} all-to-all(bf16[64,32,256]{2,1,0:T(8,128)(2,1)} %param.1), channel_id=1, replica_groups=mesh['z3'=2,'zq'=4,'zl'=2,'yl'=2,'mp'=16] {'zl','yl','mp'}, dimensions={0} | all-to-all | bytes 2097152 | tf_op jit(solution)/shard_map/cond/branch_1_fun/all_to_all | solution.py:46
  78.2 0.0 collective-permute-done.p1
  78.2 0.0 collective-permute-done.1.p2
  78.2 0.0 collective-permute-done.2.p3
  78.2 0.0 copy-done
  78.2 0.0 copy-done.1
  78.2 0.0 copy-done.2
  78.2 3.4 %shard_map.139 = (bf16[256,1024]{1,0:T(8,128)(2,1)}, bf16[4,10,64,128]{3,2,1,0:T(8,128)(2,1)S(1)}) custom-call(bf16[64,32,256]{2,1,0:T(8,128)(2,1)} %get-tuple-element.55.r, bf16[256,1024]{1,0:T(8,128)(2,1)S(1)} %copy-done.1, bf16[256,1024]{1,0:T(8,128)(2,1)S(1)} %copy-done.2, bf16[8,128,128]{2,1,0:T(8,128)(2,1)S(1)} %copy-done, ...), custom_call_target="tpu_custom_call" | custom-call | flops 1024 | bytes 1024 | tf_op jit(solution)/shard_map/pallas_call | solution.py:157
  81.7 13.4 %all_to_all.20.a = bf16[4,10,64,128]{3,2,1,0:T(8,128)(2,1)S(1)} all-to-all(bf16[4,10,64,128]{3,2,1,0:T(8,128)(2,1)S(1)} %get-tuple-element.45), channel_id=1, replica_groups=mesh['z3'=2,'zq'=4,'zl'=2,'yl'=2,'mp'=16] {'zl','yl'}, dimensions={0} | all-to-all | bytes 1310720 | tf_op jit(solution)/shard_map/all_to_all | solution.py:46
  95.0 0.0 copy-start.8
  95.0 0.0 copy-start.9
  95.0 0.6 shard_map.140
  95.7 0.0 copy-start.5
  95.7 12.7 %collective-permute-start.3 = (bf16[4,64,128]{2,1,0:T(8,128)(2,1)S(1)}, bf16[4,64,128]{2,1,0:T(8,128)(2,1)S(1)}, u32[]{:S(2)}, u32[]{:S(2)}) collective-permute-start(bf16[4,64,128]{2,1,0:T(8,128)(2,1)S(1)} %get-tuple-element.47), channel_id=1, source_target_pairs={{0,256},{256,0},{1,257},{257,1},{2,258},{258,2},{3,259},{259,3},{4... | collective-permute-start | bytes 196616 | tf_op jit(solution)/shard_map/ppermute | solution.py:284
  108.4 0.0 copy-start.6
  108.4 0.0 copy-start.7
  108.4 23.2 %conditional.3 = (bf16[8,64,128]{2,1,0:T(8,128)(2,1)S(1)}) conditional(s32[]{:T(128)} %convert_element_type.4, () %tuple.24, bf16[8,64,128]{2,1,0:T(8,128)(2,1)S(1)} %get-tuple-element.46), branch_computations={%region_2.0_spmd, %region_3.0_spmd} | conditional | bytes 262152 | solution.py:276
  108.4 23.2 %all_to_all.19 = bf16[8,64,128]{2,1,0:T(8,128)(2,1)S(1)} all-to-all(bf16[8,64,128]{2,1,0:T(8,128)(2,1)S(1)} %param.3), channel_id=1, replica_groups=mesh['z3'=2,'zq'=4,'zl'=2,'yl'=2,'mp'=16] {'z3','zq'}, dimensions={0} | all-to-all | bytes 262144 | tf_op jit(solution)/shard_map/cond/branch_1_fun/all_to_all | solution.py:46
  131.7 0.0 collective-permute-done.3.took
  131.7 0.0 copy-done.8
  131.7 0.0 copy-done.9
  131.7 0.0 copy-done.5
  131.7 0.0 copy-done.6
  131.7 0.0 copy-done.7
  131.7 1.3 %shard_map.141 = (bf16[8,4,128]{2,1,0:T(4,128)(2,1)}, bf16[8,4,512]{2,1,0:T(4,128)(2,1)}, bf16[8,16,128]{2,1,0:T(8,128)(2,1)}, bf16[8,4,128]{2,1,0:T(4,128)(2,1)}) custom-call(s32[3]{0:T(128)S(1)} %pad_add_fusion.at, bf16[8,64,128]{2,1,0:T(8,128)(2,1)S(1)} %get-tuple-element.56.a, bf16[4,64,128]{2,1,0:T(8,128)(2,1)S(1)} %get-tuple-element.49.keep, ...), custom_call_target="tpu_custom_call" | custom-call | flops 1024 | bytes 1024 | tf_op jit(solution)/shard_map/pallas_call | solution.py:262
Async XLA Ops:
  4.4 25.5 %copy-start.3 = (bf16[8,128,512]{2,1,0:T(8,128)(2,1)S(1)}, bf16[8,128,512]{2,1,0:T(8,128)(2,1)}, u32[]{:S(2)}) copy-start(bf16[8,128,512]{2,1,0:T(8,128)(2,1)} %up2.1) | copy-start | bytes 3145732
  4.4 25.5 %copy-start.4 = (bf16[8,512,128]{2,1,0:T(8,128)(2,1)S(1)}, bf16[8,512,128]{2,1,0:T(8,128)(2,1)}, u32[]{:S(2)}) copy-start(bf16[8,512,128]{2,1,0:T(8,128)(2,1)} %dn1.1) | copy-start | bytes 3145732
  4.4 25.5 %all-to-all-start.2 = ((bf16[64,32,256]{2,1,0:T(8,128)(2,1)}), bf16[64,32,256]{2,1,0:T(8,128)(2,1)S(1)}, u32[]{:S(2)}, u32[]{:S(2)}) async-start(bf16[64,32,256]{2,1,0:T(8,128)(2,1)} %shard_map.137), calls=%async_computation.2 | async-start | bytes 2097152 | tf_op jit(solution)/shard_map/all_to_all | solution.py:46
  37.4 40.8 %collective-permute-start = (bf16[8,64,128]{2,1,0:T(8,128)(2,1)}, bf16[8,64,128]{2,1,0:T(8,128)(2,1)}, u32[]{:S(2)}, u32[]{:S(2)}) collective-permute-start(bf16[8,64,128]{2,1,0:T(8,128)(2,1)} %get-tuple-element.36), channel_id=1, source_target_pairs={{0,64},{64,0},{128,192},{192,128},{1,65},{65,1},{129,193},{193,129... | collective-permute-start | bytes 393224 | tf_op jit(solution)/shard_map/ppermute | solution.py:280
  41.8 36.4 %collective-permute-start.1 = (bf16[8,64,128]{2,1,0:T(8,128)(2,1)}, bf16[8,64,128]{2,1,0:T(8,128)(2,1)}, u32[]{:S(2)}, u32[]{:S(2)}) collective-permute-start(bf16[8,64,128]{2,1,0:T(8,128)(2,1)} %get-tuple-element.37), channel_id=1, source_target_pairs={{0,128},{64,192},{128,0},{192,64},{1,129},{65,193},{129,1},{193,65... | collective-permute-start | bytes 393224 | tf_op jit(solution)/shard_map/ppermute | solution.py:280
  50.9 27.3 %collective-permute-start.2 = (bf16[8,64,128]{2,1,0:T(8,128)(2,1)}, bf16[8,64,128]{2,1,0:T(8,128)(2,1)}, u32[]{:S(2)}, u32[]{:S(2)}) collective-permute-start(bf16[8,64,128]{2,1,0:T(8,128)(2,1)} %get-tuple-element.38), channel_id=1, source_target_pairs={{0,192},{64,128},{128,64},{192,0},{1,193},{65,129},{129,65},{193,1... | collective-permute-start | bytes 393224 | tf_op jit(solution)/shard_map/ppermute | solution.py:280
  52.8 25.4 %copy-start = (bf16[8,128,128]{2,1,0:T(8,128)(2,1)S(1)}, bf16[8,128,128]{2,1,0:T(8,128)(2,1)}, u32[]{:S(2)}) copy-start(bf16[8,128,128]{2,1,0:T(8,128)(2,1)} %up1.1) | copy-start | bytes 786436
  52.8 25.4 %copy-start.1 = (bf16[256,1024]{1,0:T(8,128)(2,1)S(1)}, bf16[256,1024]{1,0:T(8,128)(2,1)}, u32[]{:S(2)}) copy-start(bf16[256,1024]{1,0:T(8,128)(2,1)} %x.3) | copy-start | bytes 1572868
  52.9 25.4 %copy-start.2 = (bf16[256,1024]{1,0:T(8,128)(2,1)S(1)}, bf16[256,1024]{1,0:T(8,128)(2,1)}, u32[]{:S(2)}) copy-start(bf16[256,1024]{1,0:T(8,128)(2,1)} %y.3) | copy-start | bytes 1572868
  95.0 36.6 %copy-start.8 = (s32[8,4,128]{2,1,0:T(4,128)S(1)}, s32[8,4,128]{2,1,0:T(4,128)}, u32[]{:S(2)}) copy-start(s32[8,4,128]{2,1,0:T(4,128)} %d1.1) | copy-start | bytes 49156
  95.0 36.6 %copy-start.9 = (s32[8,4,128]{2,1,0:T(4,128)S(1)}, s32[8,4,128]{2,1,0:T(4,128)}, u32[]{:S(2)}) copy-start(s32[8,4,128]{2,1,0:T(4,128)} %d4.1) | copy-start | bytes 49156
  95.7 36.0 %copy-start.5 = (bf16[8,128,128]{2,1,0:T(8,128)(2,1)S(1)}, bf16[8,128,128]{2,1,0:T(8,128)(2,1)}, u32[]{:S(2)}) copy-start(bf16[8,128,128]{2,1,0:T(8,128)(2,1)} %dn2.1) | copy-start | bytes 786436
  95.7 36.0 %collective-permute-start.3 = (bf16[4,64,128]{2,1,0:T(8,128)(2,1)S(1)}, bf16[4,64,128]{2,1,0:T(8,128)(2,1)S(1)}, u32[]{:S(2)}, u32[]{:S(2)}) collective-permute-start(bf16[4,64,128]{2,1,0:T(8,128)(2,1)S(1)} %get-tuple-element.47), channel_id=1, source_target_pairs={{0,256},{256,0},{1,257},{257,1},{2,258},{258,2},{3,259},{259,3},{4... | collective-permute-start | bytes 196616 | tf_op jit(solution)/shard_map/ppermute | solution.py:284
  108.4 23.3 %copy-start.6 = (s32[8,4,512]{2,1,0:T(4,128)S(1)}, s32[8,4,512]{2,1,0:T(4,128)}, u32[]{:S(2)}) copy-start(s32[8,4,512]{2,1,0:T(4,128)} %d2.1) | copy-start | bytes 196612
  108.4 23.3 %copy-start.7 = (s32[8,16,128]{2,1,0:T(8,128)S(1)}, s32[8,16,128]{2,1,0:T(8,128)}, u32[]{:S(2)}) copy-start(s32[8,16,128]{2,1,0:T(8,128)} %d3.1) | copy-start | bytes 196612

commit v3 on v2

--- a/solution.py
+++ b/solution.py
@@ -25,9 +25,9 @@
 BF = jnp.bfloat16
 F32 = jnp.float32
 
-DP = ("z3", "zq", "zl", "yl")
+DP = ("fq", "z1", "zl", "yl")
 SUB = ("zl", "yl")
-FAR = ("z3", "zq")
+FAR = ("fq", "z1")
 GROUP = SUB + ("mp",)
 
 NN = (((1,), (0,)), ((), ()))
@@ -35,6 +35,7 @@
 TN = (((0,), (0,)), ((), ()))
 TT = (((0,), (1,)), ((), ()))
 PARAMS = pltpu.CompilerParams(vmem_limit_bytes=48 << 20)
+FULL = pltpu.CompilerParams(vmem_limit_bytes=64 << 20)
 ALL_VMEM = pltpu.CompilerParams(vmem_limit_bytes=60 << 20)
 
 
@@ -102,7 +103,7 @@
     cut[:, :, 4 * R :] = (g3 * S5).reshape(NZ, NS, 4 * R, 128)
     for k, p in enumerate((p0, p1, p2, p3)):
         for h in range(2):
-            p[h * NS : (h + 1) * NS] = cut[h * NQ + (at[1] ^ k)].astype(BF)
+            p[h * NS : (h + 1) * NS] = cut[(at[0] ^ k) * 2 + h].astype(BF)
 
 
 def hidden_stage(at, r, up2, dn1):
@@ -121,14 +122,17 @@
     return pl.pallas_call(
         hidden_kernel,
         grid_spec=spec,
-        out_shape=[jax.ShapeDtypeStruct((NS * NG, 2 * NB * ML, T), BF)]
-        + [jax.ShapeDtypeStruct((2 * NS, 8 * R * ML, 128), BF)] * NQ,
+        out_shape=[pltpu.HBM((NS * NG, 2 * NB * ML, T), BF)]
+        + [pltpu.HBM((2 * NS, 8 * R * ML, 128), BF)] * NQ,
         compiler_params=PARAMS,
         cost_estimate=cost(2**30, 2**22),
     )(at, r, up2, dn1)
 
 
-def outer_kernel(r, x, y, u, p0, p1, p2, p3, gin, grads, rows, cut):
+def outer_kernel(r, x, y, u, p0, p1, p2, p3, gin, grads, rows, cut, held, sems):
+    copies = [pltpu.make_async_copy(p, held.at[k], sems.at[k]) for k, p in enumerate((p0, p1, p2, p3))]
+    for copy in copies:
+        copy.start()
     for s in range(NS):
         for h in range(2):
             rows[h, :, s] = r[s * NG : (s + 1) * NG, :, h * 128 : (h + 1) * 128].astype(F32)
@@ -147,7 +151,9 @@
             cut[s, :, b * R : (b + 1) * R] = g1[:, s]
             cut[s, :, (NB + b) * R : (NB + b + 1) * R] = g4[:, s]
     grads[:, :NZ] = cut[...].astype(BF)
-    g23 = (p0[...].astype(F32) + p1[...].astype(F32)) + (p2[...].astype(F32) + p3[...].astype(F32))
+    for copy in copies:
+        copy.wait()
+    g23 = (held[0].astype(F32) + held[1].astype(F32)) + (held[2].astype(F32) + held[3].astype(F32))
     g23 = g23.astype(BF)
     for h in range(2):
         grads[:, NZ + h] = g23[h * NS : (h + 1) * NS]
@@ -156,6 +162,7 @@
 def outer_stage(r, x, y, u, p):
     return pl.pallas_call(
         outer_kernel,
+        in_specs=[pl.BlockSpec(memory_space=pltpu.VMEM)] * 4 + [pl.BlockSpec(memory_space=pltpu.HBM)] * NQ,
         out_shape=[
             jax.ShapeDtypeStruct((T, NB * TILE), BF),
             jax.ShapeDtypeStruct((NS, NZ + 2, 2 * NB * R, TILE), BF),
@@ -163,8 +170,10 @@
         scratch_shapes=[
             pltpu.VMEM((2, NG, NS, 2 * NB * ML, 128), F32),
             pltpu.VMEM((NS, NZ, 2 * NB * R, TILE), F32),
-        ],
-        compiler_params=PARAMS,
+            pltpu.VMEM((NQ, 2 * NS, 8 * R * ML, 128), BF),
+            pltpu.SemaphoreType.DMA((NQ,)),
+        ],
+        compiler_params=FULL,
         cost_estimate=cost(2**10, 2**10),
     )(r, x, y, u, *p)
 
@@ -174,8 +183,8 @@
     for s in range(1, NS):
         v = v + a[s, :NZ].astype(F32)
     g14[...] = v.astype(BF)
-    keep[...] = a[:, NZ + at[0]]
-    give[...] = a[:, NZ + 1 - at[0]]
+    keep[...] = a[:, NZ + at[1]]
+    give[...] = a[:, NZ + 1 - at[1]]
 
 
 def near_stage(at, a):
@@ -233,7 +242,7 @@
         return pl.BlockSpec(shape, lambda i, s: (0,) * len(shape))
 
     def far(s):
-        return s[0] * NQ + s[1]
+        return s[0] * 2 + s[1]
 
     small = whole(NB, R, TILE)
     wide = whole(NB, R, HB)
@@ -269,27 +278,20 @@
 
 
 def on_device(x, dy, up1, up2, dn1, dn2, di1, di2, di3, di4):
-    at = jnp.stack([lax.axis_index(a) for a in ("z3", "zq", SUB)]).astype(jnp.int32)
-    always = lax.axis_index("mp") < 999
-
-    def fenced(a, axes):
-        return lax.cond(always, lambda a: exchange(a, axes), jnp.zeros_like, a)
-
+    at = jnp.stack([lax.axis_index(a) for a in ("fq", "z1", SUB)]).astype(jnp.int32)
     got = exchange(first_stage(x, up1, dy, dn2), GROUP)
     send, *p = hidden_stage(at, got, up2, dn1)
-    p = [p[0]] + [lax.ppermute(p[k], "zq", [(i, i ^ k) for i in range(NQ)]) for k in range(1, NQ)]
-    got, p = lax.optimization_barrier((fenced(send, GROUP), p))
-    gin, grads = outer_stage(got, x, dy, up1, p)
+    p = [p[0]] + [lax.ppermute(p[k], "fq", [(i, i ^ k) for i in range(NQ)]) for k in range(1, NQ)]
+    gin, grads = outer_stage(exchange(send, GROUP), x, dy, up1, p)
     g14, keep, give = near_stage(at, exchange(grads, SUB))
-    took = lax.ppermute(give, "z3", [(0, 1), (1, 0)])
-    g14, took = lax.optimization_barrier((fenced(g14, FAR), took))
-    new1, new2, new3, new4 = update(at, g14, keep, took, up1, up2, dn1, dn2, di1, di2, di3, di4)
+    took = lax.ppermute(give, "z1", [(0, 1), (1, 0)])
+    new1, new2, new3, new4 = update(at, exchange(g14, FAR), keep, took, up1, up2, dn1, dn2, di1, di2, di3, di4)
     return gin, new1, new2, new3, new4
 
 
 def solution(mesh):
     dp, mp = mesh.shape["dp"], mesh.shape["mp"]
-    fine = Mesh(mesh.devices.reshape(2, dp // 8, 2, 2, mp), ("z3", "zq", "zl", "yl", "mp"))
+    fine = Mesh(mesh.devices.reshape(dp // 8, 2, 2, 2, mp), ("fq", "z1", "zl", "yl", "mp"))
     w = P("mp", None, None)
     d = P("mp", DP, None)
     return jax.shard_map(

time: 134 us -> 137 us (1.022)
  blocking collectives: 61.9 us -> 16.4 us
  waiting for transfers between devices: 15.3 us -> 50.1 us
  starting transfers between devices: 38.3 us -> 50.2 us
    all_to_all x3 -> x1, blocking collectives: 61.9 us -> 16.4 us  [exchange(): return lax.all_to_all(a, axes, 0, 0, tiled=True)]
    ppermute x4, waiting for transfers between devices: 0.01 us -> 28.7 us  [the longest x3 23.3 us: on_device(): lax.ppermute(p[k], 'fq', [(i, i ^ k) for i in range(NQ)])]
    all_to_all x1 -> x3, starting transfers between devices: 10.1 us -> 25.1 us  [exchange(): return lax.all_to_all(a, axes, 0, 0, tiled=True)]
    all_to_all x1 -> x3, waiting for transfers between devices: 15.3 us -> 21.3 us  [exchange(): return lax.all_to_all(a, axes, 0, 0, tiled=True)]
    ppermute x4, starting transfers between devices: 28.2 us -> 25.1 us  [the longest x3 20.3 us: on_device(): lax.ppermute(p[k], 'fq', [(i, i ^ k) for i in range(NQ)])]
  transfers between devices with their start and end apart: 5 -> 7, of which waited for: 1 -> 5; matrix products, arithmetic and copies ran while one was open for 0% -> 0% of each run, Pallas kernels for 0% -> 0%
where the time goes in v3:
time: 137 us
  starting transfers between devices  50.2 us (37%)
  waiting for transfers between devices  50.1 us (37%)
  Pallas kernels  17.8 us (13%)
  blocking collectives  16.4 us (12%)
    all_to_all x3, starting transfers between devices, exchange(): return lax.all_to_all(a, axes, 0, 0, tiled=True)  25.1 us
    ppermute x3, waiting for transfers between devices, on_device(): lax.ppermute(p[k], 'fq', [(i, i ^ k) for i in range(NQ)])  23.3 us
    all_to_all x3, waiting for transfers between devices, exchange(): return lax.all_to_all(a, axes, 0, 0, tiled=True)  21.3 us
    ppermute x3, starting transfers between devices, on_device(): lax.ppermute(p[k], 'fq', [(i, i ^ k) for i in range(NQ)])  20.3 us
    all_to_all x1, blocking collectives, exchange(): return lax.all_to_all(a, axes, 0, 0, tiled=True)  16.4 us
    pallas_call x1, Pallas kernels, hidden_stage(): pl.pallas_call(hidden_kernel, grid_spec=spec, out_shape=[pltpu.HBM((NS *...  7.51 us
    ppermute x1, waiting for transfers between devices, on_device(): took = lax.ppermute(give, 'z1', [(0, 1), (1, 0)])  5.46 us
    ppermute x1, starting transfers between devices, on_device(): took = lax.ppermute(give, 'z1', [(0, 1), (1, 0)])  4.82 us
  transfers between devices with their start and end apart: 7, of which 5 were waited for; matrix products, arithmetic and copies ran while one was open for 0% of the time, Pallas kernels for 0%

profile of v3, /device:TPU:6, one launch (start us, length us, event | category | flops | bytes accessed | tf_op | source)
XLA Modules:
  0.0 136.7 jit_solution(14283192301859884701)
XLA Ops:
  0.6 3.8 %shard_map.137 = bf16[64,32,256]{2,1,0:T(8,128)(2,1)} custom-call(bf16[256,1024]{1,0:T(8,128)(2,1)} %x.3, bf16[8,128,128]{2,1,0:T(8,128)(2,1)} %up1.1, bf16[256,1024]{1,0:T(8,128)(2,1)} %y.3, bf16[8,128,128]{2,1,0:T(8,128)(2,1)} %dn2.1), custom_call_target="tpu_custom_call" | custom-call | flops 134217728 | bytes 2097152 | tf_op jit(solution)/shard_map/pallas_call | solution.py:68
  4.4 0.0 copy-start.1
  4.4 0.0 copy-start.3
  4.4 10.1 %all-to-all-start = ((bf16[64,32,256]{2,1,0:T(8,128)(2,1)}), bf16[64,32,256]{2,1,0:T(8,128)(2,1)S(1)}, u32[]{:S(2)}, u32[]{:S(2)}) async-start(bf16[64,32,256]{2,1,0:T(8,128)(2,1)} %shard_map.137), calls=%async_computation | async-start | bytes 2097152 | tf_op jit(solution)/shard_map/all_to_all | solution.py:47
  14.5 0.1 pad_add_fusion.at
  14.6 0.0 copy-start.10
  14.6 15.3 %all-to-all-done.r = bf16[64,32,256]{2,1,0:T(8,128)(2,1)S(1)} async-done(((bf16[64,32,256]{2,1,0:T(8,128)(2,1)}), bf16[64,32,256]{2,1,0:T(8,128)(2,1)S(1)}, u32[]{:S(2)}, u32[]{:S(2)}) %all-to-all-start) | async-done | bytes 1048608 | tf_op jit(solution)/shard_map/all_to_all | solution.py:47
  29.9 0.0 copy-done.1
  29.9 0.0 copy-done.3
  29.9 7.5 %shard_map.138 = (bf16[64,32,256]{2,1,0:T(8,128)(2,1)}, bf16[8,64,128]{2,1,0:T(8,128)(2,1)}, bf16[8,64,128]{2,1,0:T(8,128)(2,1)}, bf16[8,64,128]{2,1,0:T(8,128)(2,1)}, bf16[8,64,128]{2,1,0:T(8,128)(2,1)}) custom-call(s32[3]{0:T(128)S(1)} %pad_add_fusion.at, bf16[64,32,256]{2,1,0:T(8,128)(2,1)S(1)} %all-to-all-done.r, bf16[8,128,512]{2,1,0:T(8,128)(2,1)S(1)} %copy-done.1, ...), custom_call_target="tpu_custom_call" | custom-call | flops 1073741824 | bytes 4194304 | tf_op jit(solution)/shard_map/pallas_call | solution.py:122
  37.4 0.0 copy-done.10
  37.4 0.0 copy-start.14
  37.4 0.0 copy-start.13
  37.4 0.0 copy-start.12
  37.5 8.5 %all-to-all-start.1 = ((bf16[64,32,256]{2,1,0:T(8,128)(2,1)}), bf16[64,32,256]{2,1,0:T(8,128)(2,1)}, u32[]{:S(2)}, u32[]{:S(2)}) async-start(bf16[64,32,256]{2,1,0:T(8,128)(2,1)} %get-tuple-element.19), calls=%async_computation.1 | async-start | bytes 2097152 | tf_op jit(solution)/shard_map/all_to_all | solution.py:47
  46.0 0.0 copy-done.14
  46.0 8.4 %collective-permute-start = (bf16[8,64,128]{2,1,0:T(8,128)(2,1)S(1)}, bf16[8,64,128]{2,1,0:T(8,128)(2,1)}, u32[]{:S(2)}, u32[]{:S(2)}) collective-permute-start(bf16[8,64,128]{2,1,0:T(8,128)(2,1)S(1)} %copy-done.14), channel_id=1, source_target_pairs={{0,128},{128,0},{256,384},{384,256},{1,129},{129,1},{257,385},{385... | collective-permute-start | bytes 393224 | tf_op jit(solution)/shard_map/ppermute | solution.py:284
  54.4 0.0 copy-done.13
  54.4 10.0 %collective-permute-start.1 = (bf16[8,64,128]{2,1,0:T(8,128)(2,1)S(1)}, bf16[8,64,128]{2,1,0:T(8,128)(2,1)}, u32[]{:S(2)}, u32[]{:S(2)}) collective-permute-start(bf16[8,64,128]{2,1,0:T(8,128)(2,1)S(1)} %copy-done.13), channel_id=1, source_target_pairs={{0,256},{128,384},{256,0},{384,128},{1,257},{129,385},{257,1},{385... | collective-permute-start | bytes 393224 | tf_op jit(solution)/shard_map/ppermute | solution.py:284
  64.4 0.0 copy-done.12
  64.4 1.9 %collective-permute-start.2 = (bf16[8,64,128]{2,1,0:T(8,128)(2,1)S(1)}, bf16[8,64,128]{2,1,0:T(8,128)(2,1)}, u32[]{:S(2)}, u32[]{:S(2)}) collective-permute-start(bf16[8,64,128]{2,1,0:T(8,128)(2,1)S(1)} %copy-done.12), channel_id=1, source_target_pairs={{0,384},{128,256},{256,128},{384,0},{1,385},{129,257},{257,129},{3... | collective-permute-start | bytes 393224 | tf_op jit(solution)/shard_map/ppermute | solution.py:284
  66.3 0.0 collective-permute-done.p1
  66.3 10.9 %collective-permute-done.1.p2 = bf16[8,64,128]{2,1,0:T(8,128)(2,1)} collective-permute-done((bf16[8,64,128]{2,1,0:T(8,128)(2,1)S(1)}, bf16[8,64,128]{2,1,0:T(8,128)(2,1)}, u32[]{:S(2)}, u32[]{:S(2)}) %collective-permute-start.1) | collective-permute-done | bytes 131104 | tf_op jit(solution)/shard_map/ppermute | solution.py:284
  77.3 12.3 %collective-permute-done.2.p3 = bf16[8,64,128]{2,1,0:T(8,128)(2,1)} collective-permute-done((bf16[8,64,128]{2,1,0:T(8,128)(2,1)S(1)}, bf16[8,64,128]{2,1,0:T(8,128)(2,1)}, u32[]{:S(2)}, u32[]{:S(2)}) %collective-permute-start.2) | collective-permute-done | bytes 131104 | tf_op jit(solution)/shard_map/ppermute | solution.py:284
  89.6 0.0 all-to-all-done.1.r
  89.6 3.9 %shard_map.139 = (bf16[256,1024]{1,0:T(8,128)(2,1)}, bf16[4,10,64,128]{3,2,1,0:T(8,128)(2,1)}) custom-call(bf16[64,32,256]{2,1,0:T(8,128)(2,1)} %all-to-all-done.1.r, bf16[256,1024]{1,0:T(8,128)(2,1)} %x.3, bf16[256,1024]{1,0:T(8,128)(2,1)} %y.3, bf16[8,128,128]{2,1,0:T(8,128)(2,1)} %up1.1, bf16[8,64,128]{2,1,0:T(8,128)(2,1)} %get-tuple-element.20.p0, ...), custom_call_target="tpu_custom_call" | custom-call | flops 1024 | bytes 1024 | tf_op jit(solution)/shard_map/pallas_call | solution.py:163
  93.6 0.0 copy-start.11
  93.6 0.0 copy-start.2
  93.6 16.4 %all_to_all.20.a = bf16[4,10,64,128]{3,2,1,0:T(8,128)(2,1)S(1)} all-to-all(bf16[4,10,64,128]{3,2,1,0:T(8,128)(2,1)} %get-tuple-element.25), channel_id=1, replica_groups=mesh['fq'=4,'z1'=2,'zl'=2,'yl'=2,'mp'=16] {'zl','yl'}, dimensions={0} | all-to-all | bytes 1310720 | tf_op jit(solution)/shard_map/all_to_all | solution.py:47
  110.0 0.0 copy-done.11
  110.0 0.0 copy-start.5
  110.0 0.0 copy-start.8
  110.0 0.0 copy-start.9
  110.0 1.3 shard_map.140
  111.3 6.5 %all-to-all-start.3 = ((bf16[8,64,128]{2,1,0:T(8,128)(2,1)}), bf16[8,64,128]{2,1,0:T(8,128)(2,1)S(1)}, u32[]{:S(2)}, u32[]{:S(2)}) async-start(bf16[8,64,128]{2,1,0:T(8,128)(2,1)} %get-tuple-element.26), calls=%async_computation.3 | async-start | bytes 262144 | tf_op jit(solution)/shard_map/all_to_all | solution.py:47
  117.8 4.8 %collective-permute-start.3 = (bf16[4,64,128]{2,1,0:T(8,128)(2,1)S(1)}, bf16[4,64,128]{2,1,0:T(8,128)(2,1)S(1)}, u32[]{:S(2)}, u32[]{:S(2)}) collective-permute-start(bf16[4,64,128]{2,1,0:T(8,128)(2,1)S(1)} %get-tuple-element.28), channel_id=1, source_target_pairs={{0,64},{64,0},{1,65},{65,1},{2,66},{66,2},{3,67},{67,3},{4,68},{68... | collective-permute-start | bytes 196616 | tf_op jit(solution)/shard_map/ppermute | solution.py:287
  122.6 5.5 %collective-permute-done.3.took = bf16[4,64,128]{2,1,0:T(8,128)(2,1)S(1)} collective-permute-done((bf16[4,64,128]{2,1,0:T(8,128)(2,1)S(1)}, bf16[4,64,128]{2,1,0:T(8,128)(2,1)S(1)}, u32[]{:S(2)}, u32[]{:S(2)}) %collective-permute-start.3) | collective-permute-done | bytes 65568 | tf_op jit(solution)/shard_map/ppermute | solution.py:287
  128.1 6.1 %all-to-all-done.3.a = bf16[8,64,128]{2,1,0:T(8,128)(2,1)S(1)} async-done(((bf16[8,64,128]{2,1,0:T(8,128)(2,1)}), bf16[8,64,128]{2,1,0:T(8,128)(2,1)S(1)}, u32[]{:S(2)}, u32[]{:S(2)}) %all-to-all-start.3) | async-done | bytes 131104 | tf_op jit(solution)/shard_map/all_to_all | solution.py:47
  134.1 0.0 copy-done.2
  134.1 0.0 copy-done.5
  134.1 0.0 copy-done.6
  134.1 0.0 copy-done.7
  134.2 0.0 copy-done.8
  134.2 0.0 copy-done.9
  134.2 0.0 copy-done
  134.2 0.0 copy-start.4
  134.2 1.2 copy-done.4
  135.4 1.3 shard_map.141
  (3 shorter events, 0.0 us)
Async XLA Ops:
  4.4 25.5 %copy-start.1 = (bf16[8,128,512]{2,1,0:T(8,128)(2,1)S(1)}, bf16[8,128,512]{2,1,0:T(8,128)(2,1)}, u32[]{:S(2)}) copy-start(bf16[8,128,512]{2,1,0:T(8,128)(2,1)} %up2.1) | copy-start | bytes 3145732
  4.4 25.5 %copy-start.3 = (bf16[8,512,128]{2,1,0:T(8,128)(2,1)S(1)}, bf16[8,512,128]{2,1,0:T(8,128)(2,1)}, u32[]{:S(2)}) copy-start(bf16[8,512,128]{2,1,0:T(8,128)(2,1)} %dn1.1) | copy-start | bytes 3145732
  4.4 25.5 %all-to-all-start = ((bf16[64,32,256]{2,1,0:T(8,128)(2,1)}), bf16[64,32,256]{2,1,0:T(8,128)(2,1)S(1)}, u32[]{:S(2)}, u32[]{:S(2)}) async-start(bf16[64,32,256]{2,1,0:T(8,128)(2,1)} %shard_map.137), calls=%async_computation | async-start | bytes 2097152 | tf_op jit(solution)/shard_map/all_to_all | solution.py:47
  14.6 22.8 %copy-start.10 = (s32[3]{0:T(128)}, s32[3]{0:T(128)S(1)}, u32[]{:S(2)}) copy-start(s32[3]{0:T(128)S(1)} %pad_add_fusion.at) | copy-start | bytes 40
  37.4 8.5 %copy-start.14 = (bf16[8,64,128]{2,1,0:T(8,128)(2,1)S(1)}, bf16[8,64,128]{2,1,0:T(8,128)(2,1)}, u32[]{:S(2)}) copy-start(bf16[8,64,128]{2,1,0:T(8,128)(2,1)} %get-tuple-element.21) | copy-start | bytes 393220
  37.4 16.9 %copy-start.13 = (bf16[8,64,128]{2,1,0:T(8,128)(2,1)S(1)}, bf16[8,64,128]{2,1,0:T(8,128)(2,1)}, u32[]{:S(2)}) copy-start(bf16[8,64,128]{2,1,0:T(8,128)(2,1)} %get-tuple-element.22) | copy-start | bytes 393220
  37.4 26.9 %copy-start.12 = (bf16[8,64,128]{2,1,0:T(8,128)(2,1)S(1)}, bf16[8,64,128]{2,1,0:T(8,128)(2,1)}, u32[]{:S(2)}) copy-start(bf16[8,64,128]{2,1,0:T(8,128)(2,1)} %get-tuple-element.23) | copy-start | bytes 393220
  37.5 52.2 %all-to-all-start.1 = ((bf16[64,32,256]{2,1,0:T(8,128)(2,1)}), bf16[64,32,256]{2,1,0:T(8,128)(2,1)}, u32[]{:S(2)}, u32[]{:S(2)}) async-start(bf16[64,32,256]{2,1,0:T(8,128)(2,1)} %get-tuple-element.19), calls=%async_computation.1 | async-start | bytes 2097152 | tf_op jit(solution)/shard_map/all_to_all | solution.py:47
  46.0 20.4 %collective-permute-start = (bf16[8,64,128]{2,1,0:T(8,128)(2,1)S(1)}, bf16[8,64,128]{2,1,0:T(8,128)(2,1)}, u32[]{:S(2)}, u32[]{:S(2)}) collective-permute-start(bf16[8,64,128]{2,1,0:T(8,128)(2,1)S(1)} %copy-done.14), channel_id=1, source_target_pairs={{0,128},{128,0},{256,384},{384,256},{1,129},{129,1},{257,385},{385... | collective-permute-start | bytes 393224 | tf_op jit(solution)/shard_map/ppermute | solution.py:284
  54.4 22.9 %collective-permute-start.1 = (bf16[8,64,128]{2,1,0:T(8,128)(2,1)S(1)}, bf16[8,64,128]{2,1,0:T(8,128)(2,1)}, u32[]{:S(2)}, u32[]{:S(2)}) collective-permute-start(bf16[8,64,128]{2,1,0:T(8,128)(2,1)S(1)} %copy-done.13), channel_id=1, source_target_pairs={{0,256},{128,384},{256,0},{384,128},{1,257},{129,385},{257,1},{385... | collective-permute-start | bytes 393224 | tf_op jit(solution)/shard_map/ppermute | solution.py:284
  64.4 25.2 %collective-permute-start.2 = (bf16[8,64,128]{2,1,0:T(8,128)(2,1)S(1)}, bf16[8,64,128]{2,1,0:T(8,128)(2,1)}, u32[]{:S(2)}, u32[]{:S(2)}) collective-permute-start(bf16[8,64,128]{2,1,0:T(8,128)(2,1)S(1)} %copy-done.12), channel_id=1, source_target_pairs={{0,384},{128,256},{256,128},{384,0},{1,385},{129,257},{257,129},{3... | collective-permute-start | bytes 393224 | tf_op jit(solution)/shard_map/ppermute | solution.py:284
  93.6 16.5 %copy-start.11 = (s32[3]{0:T(128)S(1)}, s32[3]{0:T(128)}, u32[]{:S(2)}) copy-start(s32[3]{0:T(128)} %copy-done.10) | copy-start | bytes 40
  93.6 40.6 %copy-start.2 = (bf16[8,128,512]{2,1,0:T(8,128)(2,1)S(1)}, bf16[8,128,512]{2,1,0:T(8,128)(2,1)}, u32[]{:S(2)}) copy-start(bf16[8,128,512]{2,1,0:T(8,128)(2,1)} %up2.1) | copy-start | bytes 3145732
  110.0 24.1 %copy-start.5 = (bf16[8,128,128]{2,1,0:T(8,128)(2,1)S(1)}, bf16[8,128,128]{2,1,0:T(8,128)(2,1)}, u32[]{:S(2)}) copy-start(bf16[8,128,128]{2,1,0:T(8,128)(2,1)} %dn2.1) | copy-start | bytes 786436
  110.0 24.1 %copy-start.6 = (s32[8,4,512]{2,1,0:T(4,128)S(1)}, s32[8,4,512]{2,1,0:T(4,128)}, u32[]{:S(2)}) copy-start(s32[8,4,512]{2,1,0:T(4,128)} %d2.1) | copy-start | bytes 196612
  110.0 24.1 %copy-start.7 = (s32[8,16,128]{2,1,0:T(8,128)S(1)}, s32[8,16,128]{2,1,0:T(8,128)}, u32[]{:S(2)}) copy-start(s32[8,16,128]{2,1,0:T(8,128)} %d3.1) | copy-start | bytes 196612
  110.0 24.1 %copy-start.8 = (s32[8,4,128]{2,1,0:T(4,128)S(1)}, s32[8,4,128]{2,1,0:T(4,128)}, u32[]{:S(2)}) copy-start(s32[8,4,128]{2,1,0:T(4,128)} %d1.1) | copy-start | bytes 49156
  110.0 24.1 %copy-start.9 = (s32[8,4,128]{2,1,0:T(4,128)S(1)}, s32[8,4,128]{2,1,0:T(4,128)}, u32[]{:S(2)}) copy-start(s32[8,4,128]{2,1,0:T(4,128)} %d4.1) | copy-start | bytes 49156
  111.3 22.9 %copy-start = (bf16[8,128,128]{2,1,0:T(8,128)(2,1)S(1)}, bf16[8,128,128]{2,1,0:T(8,128)(2,1)}, u32[]{:S(2)}) copy-start(bf16[8,128,128]{2,1,0:T(8,128)(2,1)} %up1.1) | copy-start | bytes 786436
  111.3 22.8 %all-to-all-start.3 = ((bf16[8,64,128]{2,1,0:T(8,128)(2,1)}), bf16[8,64,128]{2,1,0:T(8,128)(2,1)S(1)}, u32[]{:S(2)}, u32[]{:S(2)}) async-start(bf16[8,64,128]{2,1,0:T(8,128)(2,1)} %get-tuple-element.26), calls=%async_computation.3 | async-start | bytes 262144 | tf_op jit(solution)/shard_map/all_to_all | solution.py:47
  117.8 10.3 %collective-permute-start.3 = (bf16[4,64,128]{2,1,0:T(8,128)(2,1)S(1)}, bf16[4,64,128]{2,1,0:T(8,128)(2,1)S(1)}, u32[]{:S(2)}, u32[]{:S(2)}) collective-permute-start(bf16[4,64,128]{2,1,0:T(8,128)(2,1)S(1)} %get-tuple-element.28), channel_id=1, source_target_pairs={{0,64},{64,0},{1,65},{65,1},{2,66},{66,2},{3,67},{67,3},{4,68},{68... | collective-permute-start | bytes 196616 | tf_op jit(solution)/shard_map/ppermute | solution.py:287
  134.2 1.2 copy-start.4

commit v4 on v3

--- a/solution.py
+++ b/solution.py
@@ -27,7 +27,8 @@
 
 DP = ("fq", "z1", "zl", "yl")
 SUB = ("zl", "yl")
-FAR = ("fq", "z1")
+NEAR = ("z1", "zl", "yl")
+FAR = ("fq",)
 GROUP = SUB + ("mp",)
 
 NN = (((1,), (0,)), ((), ()))
@@ -74,7 +75,7 @@
     )(x, u, y, d)
 
 
-def hidden_kernel(at, r, w2, w3, out, p0, p1, p2, p3, cut):
+def hidden_kernel(at, r, w2, w3, out, g, cut):
     w2 = w2[0]
     w3 = w3[0]
     g2 = g3 = None
@@ -101,9 +102,8 @@
         for s in range(NS):
             cut[:, s, c * R : (c + 1) * R] = v[:, s]
     cut[:, :, 4 * R :] = (g3 * S5).reshape(NZ, NS, 4 * R, 128)
-    for k, p in enumerate((p0, p1, p2, p3)):
-        for h in range(2):
-            p[h * NS : (h + 1) * NS] = cut[(at[0] ^ k) * 2 + h].astype(BF)
+    for z in range(NZ):
+        g[(z % 2) * NS : (z % 2 + 1) * NS, z // 2] = cut[z].astype(BF)
 
 
 def hidden_stage(at, r, up2, dn1):
@@ -116,23 +116,22 @@
             pl.BlockSpec((1, HB, TILE), lambda m, s: (s[2] * ML + m, 0, 0)),
         ],
         out_specs=[pl.BlockSpec((NS * NG, 2 * NB, T), lambda m, s: (0, m, 0))]
-        + [pl.BlockSpec((2 * NS, 8 * R, 128), lambda m, s: (0, m, 0))] * NQ,
+        + [pl.BlockSpec((2 * NS, NQ, 8 * R, 128), lambda m, s: (0, 0, m, 0))],
         scratch_shapes=[pltpu.VMEM((NZ, NS, 8 * R, 128), F32)],
     )
     return pl.pallas_call(
         hidden_kernel,
         grid_spec=spec,
         out_shape=[pltpu.HBM((NS * NG, 2 * NB * ML, T), BF)]
-        + [pltpu.HBM((2 * NS, 8 * R * ML, 128), BF)] * NQ,
+        + [pltpu.HBM((2 * NS, NQ, 8 * R * ML, 128), BF)],
         compiler_params=PARAMS,
         cost_estimate=cost(2**30, 2**22),
     )(at, r, up2, dn1)
 
 
-def outer_kernel(r, x, y, u, p0, p1, p2, p3, gin, grads, rows, cut, held, sems):
-    copies = [pltpu.make_async_copy(p, held.at[k], sems.at[k]) for k, p in enumerate((p0, p1, p2, p3))]
-    for copy in copies:
-        copy.start()
+def outer_kernel(r, x, y, u, g23, gin, grads, rows, cut, sem):
+    copy = pltpu.make_async_copy(g23, grads.at[:, :, 1], sem)
+    copy.start()
     for s in range(NS):
         for h in range(2):
             rows[h, :, s] = r[s * NG : (s + 1) * NG, :, h * 128 : (h + 1) * 128].astype(F32)
@@ -148,57 +147,48 @@
         g1 = (mm(x[:, f], back_up, TT) * S1).reshape(NZ, NS, R, TILE)
         g4 = (mm(down, y[:, f], NN) * S1).reshape(NZ, NS, R, TILE)
         for s in range(NS):
-            cut[s, :, b * R : (b + 1) * R] = g1[:, s]
-            cut[s, :, (NB + b) * R : (NB + b + 1) * R] = g4[:, s]
-    grads[:, :NZ] = cut[...].astype(BF)
-    for copy in copies:
-        copy.wait()
-    g23 = (held[0].astype(F32) + held[1].astype(F32)) + (held[2].astype(F32) + held[3].astype(F32))
-    g23 = g23.astype(BF)
-    for h in range(2):
-        grads[:, NZ + h] = g23[h * NS : (h + 1) * NS]
-
-
-def outer_stage(r, x, y, u, p):
+            cut[:, s, b * R : (b + 1) * R] = g1[:, s]
+            cut[:, s, (NB + b) * R : (NB + b + 1) * R] = g4[:, s]
+    for z in range(NZ):
+        grads[(z % 2) * NS : (z % 2 + 1) * NS, z // 2, 0] = cut[z].astype(BF)
+    copy.wait()
+
+
+def outer_stage(r, x, y, u, g23):
     return pl.pallas_call(
         outer_kernel,
-        in_specs=[pl.BlockSpec(memory_space=pltpu.VMEM)] * 4 + [pl.BlockSpec(memory_space=pltpu.HBM)] * NQ,
+        in_specs=[pl.BlockSpec(memory_space=pltpu.VMEM)] * 4 + [pl.BlockSpec(memory_space=pltpu.HBM)],
         out_shape=[
             jax.ShapeDtypeStruct((T, NB * TILE), BF),
-            jax.ShapeDtypeStruct((NS, NZ + 2, 2 * NB * R, TILE), BF),
+            jax.ShapeDtypeStruct((2 * NS, NQ, 2, 2 * NB * R, TILE), BF),
         ],
         scratch_shapes=[
             pltpu.VMEM((2, NG, NS, 2 * NB * ML, 128), F32),
-            pltpu.VMEM((NS, NZ, 2 * NB * R, TILE), F32),
-            pltpu.VMEM((NQ, 2 * NS, 8 * R * ML, 128), BF),
-            pltpu.SemaphoreType.DMA((NQ,)),
-        ],
-        compiler_params=FULL,
+            pltpu.VMEM((NZ, NS, 2 * NB * R, TILE), F32),
+            pltpu.SemaphoreType.DMA,
+        ],
+        compiler_params=PARAMS,
         cost_estimate=cost(2**10, 2**10),
-    )(r, x, y, u, *p)
-
-
-def near_kernel(at, a, g14, keep, give):
-    v = a[0, :NZ].astype(F32)
-    for s in range(1, NS):
-        v = v + a[s, :NZ].astype(F32)
-    g14[...] = v.astype(BF)
-    keep[...] = a[:, NZ + at[1]]
-    give[...] = a[:, NZ + 1 - at[1]]
-
-
-def near_stage(at, a):
+    )(r, x, y, u, g23)
+
+
+def near_kernel(a, out):
+    for q in range(NQ):
+        v = a[0, q, 0].astype(F32)
+        for n in range(1, 2 * NS):
+            v = v + a[n, q, 0].astype(F32)
+        out[q, 0] = v.astype(BF)
+        for s in range(NS):
+            out[q, 1 + s] = (a[s, q, 1].astype(F32) + a[NS + s, q, 1].astype(F32)).astype(BF)
+
+
+def near_stage(a):
     return pl.pallas_call(
         near_kernel,
-        in_specs=[pl.BlockSpec(memory_space=pltpu.SMEM), pl.BlockSpec(memory_space=pltpu.VMEM)],
-        out_shape=[
-            jax.ShapeDtypeStruct((NZ, 2 * NB * R, TILE), BF),
-            jax.ShapeDtypeStruct((NS, 8 * R * ML, 128), BF),
-            jax.ShapeDtypeStruct((NS, 8 * R * ML, 128), BF),
-        ],
+        out_shape=jax.ShapeDtypeStruct((NQ, 1 + NS, 2 * NB * R, TILE), BF),
         compiler_params=PARAMS,
         cost_estimate=cost(2**10, 2**10),
-    )(at, a)
+    )(a)
 
 
 def choose(sub, options):
@@ -218,17 +208,18 @@
     return choose(sub, [v[:, s * R : (s + 1) * R] for s in range(NS)])
 
 
-def update_kernel(at, a, keep, took, up1, up2, dn1, dn2, d1, d2, d3, d4, n1, n2, n3, n4):
+def update_kernel(at, a, up1, up2, dn1, dn2, d1, d2, d3, d4, n1, n2, n3, n4):
     sub = at[2]
-    v = a[0].astype(F32)
-    for z in range(1, NZ):
-        v = v + a[z].astype(F32)
-    g = v.reshape(2, NB, R, TILE)
+
+    def total(i):
+        return (a[0, i].astype(F32) + a[1, i].astype(F32)) + (a[2, i].astype(F32) + a[3, i].astype(F32))
+
+    g = total(0).reshape(2, NB, R, TILE)
     n1[...] = step(own_rows(sub, up1[...]), g[0], d1[...])
     n4[...] = step(own_rows(sub, dn2[...]), g[1], d4[...])
     own = own_rows(sub, up2[...])
     for s in range(NS):
-        v = keep[s].astype(F32) + took[s].astype(F32)
+        v = total(1 + s)
         for i in range(ML):
             m = s * ML + i
             w = v[i * 8 * R : (i + 1) * 8 * R]
@@ -237,7 +228,7 @@
             n3[m] = step(dn1[m].astype(F32), w[4 * R :], d3[m])
 
 
-def update(at, a, keep, took, up1, up2, dn1, dn2, d1, d2, d3, d4):
+def update(at, a, up1, up2, dn1, dn2, d1, d2, d3, d4):
     def whole(*shape):
         return pl.BlockSpec(shape, lambda i, s: (0,) * len(shape))
 
@@ -247,15 +238,12 @@
     small = whole(NB, R, TILE)
     wide = whole(NB, R, HB)
     large = whole(NB, 4 * R, TILE)
-    half = whole(NS, 8 * R * ML, 128)
     block = pl.BlockSpec((NB, NS * R, TILE), lambda i, s: (0, far(s), 0))
     spec = pltpu.PrefetchScalarGridSpec(
         num_scalar_prefetch=1,
         grid=(1,),
         in_specs=[
-            whole(NZ, 2 * NB * R, TILE),
-            half,
-            half,
+            whole(NQ, 1 + NS, 2 * NB * R, TILE),
             block,
             pl.BlockSpec((NB, NS * R, HB), lambda i, s: (0, far(s), 0)),
             pl.BlockSpec((NB, 4 * R, TILE), lambda i, s: (0, far(s) * NS + s[2], 0)),
@@ -274,18 +262,16 @@
         out_shape=[jax.ShapeDtypeStruct(shape, BF) for shape in shapes],
         compiler_params=PARAMS,
         cost_estimate=cost(2**10, 2**10),
-    )(at, a, keep, took, up1, up2, dn1, dn2, d1, d2, d3, d4)
+    )(at, a, up1, up2, dn1, dn2, d1, d2, d3, d4)
 
 
 def on_device(x, dy, up1, up2, dn1, dn2, di1, di2, di3, di4):
     at = jnp.stack([lax.axis_index(a) for a in ("fq", "z1", SUB)]).astype(jnp.int32)
     got = exchange(first_stage(x, up1, dy, dn2), GROUP)
-    send, *p = hidden_stage(at, got, up2, dn1)
-    p = [p[0]] + [lax.ppermute(p[k], "fq", [(i, i ^ k) for i in range(NQ)]) for k in range(1, NQ)]
-    gin, grads = outer_stage(exchange(send, GROUP), x, dy, up1, p)
-    g14, keep, give = near_stage(at, exchange(grads, SUB))
-    took = lax.ppermute(give, "z1", [(0, 1), (1, 0)])
-    new1, new2, new3, new4 = update(at, exchange(g14, FAR), keep, took, up1, up2, dn1, dn2, di1, di2, di3, di4)
+    send, g23 = hidden_stage(at, got, up2, dn1)
+    gin, grads = outer_stage(exchange(send, GROUP), x, dy, up1, g23)
+    grads = exchange(near_stage(exchange(grads, NEAR)), FAR)
+    new1, new2, new3, new4 = update(at, grads, up1, up2, dn1, dn2, di1, di2, di3, di4)
     return gin, new1, new2, new3, new4
 
 

time: 137 us -> 132 us (0.964)
  the two profiles are of different devices: /device:TPU:6 before, /device:TPU:32 now
where the time goes in v4:
time: 132 us; the launch traced here: 131 us
  blocking collectives  88.8 us (67%)
  waiting for transfers between devices  17 us (13%)
  Pallas kernels  14.8 us (11%)
  starting transfers between devices  9.91 us (8%)
    all_to_all x3, blocking collectives, exchange(): return lax.all_to_all(a, axes, 0, 0, tiled=True)  88.8 us
    all_to_all x1, waiting for transfers between devices, exchange(): return lax.all_to_all(a, axes, 0, 0, tiled=True)  17 us
    all_to_all x1, starting transfers between devices, exchange(): return lax.all_to_all(a, axes, 0, 0, tiled=True)  9.91 us
    pallas_call x1, Pallas kernels, hidden_stage(): pl.pallas_call(hidden_kernel, grid_spec=spec, out_shape=[pltpu.HBM((NS *...  7.43 us
    pallas_call x1, Pallas kernels, first_stage(): pl.pallas_call(first_kernel, out_shape=jax.ShapeDtypeStruct((NS * NG, 2 *...  3.73 us
  transfers between devices with their start and end apart: 1, of which 1 were waited for; matrix products, arithmetic and copies ran while one was open for 0% of the time, Pallas kernels for 0%

profile of v4, /device:TPU:32, one launch (start us, length us, event | category | flops | bytes accessed | tf_op | source)
XLA Modules:
  0.0 131.4 jit_solution(13564658914176941219)
XLA Ops:
  0.6 3.7 %shard_map.137 = bf16[64,32,256]{2,1,0:T(8,128)(2,1)} custom-call(bf16[256,1024]{1,0:T(8,128)(2,1)} %x.3, bf16[8,128,128]{2,1,0:T(8,128)(2,1)} %up1.1, bf16[256,1024]{1,0:T(8,128)(2,1)} %y.3, bf16[8,128,128]{2,1,0:T(8,128)(2,1)} %dn2.1), custom_call_target="tpu_custom_call" | custom-call | flops 134217728 | bytes 2097152 | tf_op jit(solution)/shard_map/pallas_call | solution.py:69
  4.4 0.0 copy-start.3
  4.4 0.0 copy-start.4
  4.4 9.9 %all-to-all-start = ((bf16[64,32,256]{2,1,0:T(8,128)(2,1)}), bf16[64,32,256]{2,1,0:T(8,128)(2,1)S(1)}, u32[]{:S(2)}, u32[]{:S(2)}) async-start(bf16[64,32,256]{2,1,0:T(8,128)(2,1)} %shard_map.137), calls=%async_computation | async-start | bytes 2097152 | tf_op jit(solution)/shard_map/all_to_all | solution.py:48
  14.3 0.1 pad_add_fusion.at
  14.4 17.0 %all-to-all-done.r = bf16[64,32,256]{2,1,0:T(8,128)(2,1)S(1)} async-done(((bf16[64,32,256]{2,1,0:T(8,128)(2,1)}), bf16[64,32,256]{2,1,0:T(8,128)(2,1)S(1)}, u32[]{:S(2)}, u32[]{:S(2)}) %all-to-all-start) | async-done | bytes 1048608 | tf_op jit(solution)/shard_map/all_to_all | solution.py:48
  31.3 0.0 copy-done.3
  31.3 0.0 copy-done.4
  31.3 7.4 %shard_map.138 = (bf16[64,32,256]{2,1,0:T(8,128)(2,1)}, bf16[8,4,64,128]{3,2,1,0:T(8,128)(2,1)}) custom-call(s32[3]{0:T(128)S(1)} %pad_add_fusion.at, bf16[64,32,256]{2,1,0:T(8,128)(2,1)S(1)} %all-to-all-done.r, bf16[8,128,512]{2,1,0:T(8,128)(2,1)S(1)} %copy-done.3, bf16[8,512,128]{2,1,0:T(8,128)(2,1)S(1)} %copy-done.4), custom_call_target="tpu_custom_call" | custom-call | flops 1073741824 | bytes 4194304 | tf_op jit(solution)/shard_map/pallas_call | solution.py:122
  38.8 0.0 copy-start
  38.8 0.0 copy-start.1
  38.8 0.0 copy-start.2
  38.8 0.0 copy-start.6
  38.8 23.2 %all_to_all.20.r = bf16[64,32,256]{2,1,0:T(8,128)(2,1)S(1)} all-to-all(bf16[64,32,256]{2,1,0:T(8,128)(2,1)} %get-tuple-element.13), channel_id=1, replica_groups=mesh['fq'=4,'z1'=2,'zl'=2,'yl'=2,'mp'=16] {'zl','yl','mp'}, dimensions={0} | all-to-all | bytes 2097152 | tf_op jit(solution)/shard_map/all_to_all | solution.py:48
  61.9 0.0 copy-done
  61.9 0.0 copy-done.1
  61.9 0.0 copy-done.2
  61.9 0.0 copy-done.6
  62.0 2.2 %shard_map.139 = (bf16[256,1024]{1,0:T(8,128)(2,1)}, bf16[8,4,2,64,128]{4,3,2,1,0:T(8,128)(2,1)S(1)}) custom-call(bf16[64,32,256]{2,1,0:T(8,128)(2,1)S(1)} %all_to_all.20.r, bf16[256,1024]{1,0:T(8,128)(2,1)S(1)} %copy-done.1, bf16[256,1024]{1,0:T(8,128)(2,1)S(1)} %copy-done.2, bf16[8,128,128]{2,1,0:T(8,128)(2,1)S(1)} %copy-done, ...), custom_call_target="tpu_custom_call" | custom-call | flops 1024 | bytes 1024 | tf_op jit(solution)/shard_map/pallas_call | solution.py:158
  64.1 30.1 %all_to_all.21.a = bf16[8,4,2,64,128]{4,3,2,1,0:T(8,128)(2,1)S(1)} all-to-all(bf16[8,4,2,64,128]{4,3,2,1,0:T(8,128)(2,1)S(1)} %get-tuple-element.16), channel_id=1, replica_groups=mesh['fq'=4,'z1'=2,'zl'=2,'yl'=2,'mp'=16] {'z1','zl','yl'}, dimensions={0} | all-to-all | bytes 2097152 | tf_op jit(solution)/shard_map/all_to_all | solution.py:48
  94.3 0.1 shard_map.140
  94.4 0.0 copy-start.5
  94.4 0.0 copy-start.7
  94.4 0.0 copy-start.8
  94.4 0.0 copy-start.9
  94.4 0.0 copy-start.10
  94.4 35.5 %all_to_all.22.a = bf16[4,5,64,128]{3,2,1,0:T(8,128)(2,1)S(1)} all-to-all(bf16[4,5,64,128]{3,2,1,0:T(8,128)(2,1)S(1)} %shard_map.140), channel_id=1, replica_groups=mesh['fq'=4,'z1'=2,'zl'=2,'yl'=2,'mp'=16] {'fq'}, dimensions={0} | all-to-all | bytes 655360 | tf_op jit(solution)/shard_map/all_to_all | solution.py:48
  130.0 0.0 copy-done.5
  130.0 0.0 copy-done.7
  130.0 0.0 copy-done.8
  130.0 0.0 copy-done.9
  130.0 0.0 copy-done.10
  130.0 1.3 %shard_map.141 = (bf16[8,4,128]{2,1,0:T(4,128)(2,1)}, bf16[8,4,512]{2,1,0:T(4,128)(2,1)}, bf16[8,16,128]{2,1,0:T(8,128)(2,1)}, bf16[8,4,128]{2,1,0:T(4,128)(2,1)}) custom-call(s32[3]{0:T(128)S(1)} %pad_add_fusion.at, bf16[4,5,64,128]{3,2,1,0:T(8,128)(2,1)S(1)} %all_to_all.22.a, bf16[8,128,128]{2,1,0:T(8,128)(2,1)S(1)} %copy-done, ...), custom_call_target="tpu_custom_call" | custom-call | flops 1024 | bytes 1024 | tf_op jit(solution)/shard_map/pallas_call | solution.py:259
Async XLA Ops:
  4.4 27.0 %copy-start.3 = (bf16[8,128,512]{2,1,0:T(8,128)(2,1)S(1)}, bf16[8,128,512]{2,1,0:T(8,128)(2,1)}, u32[]{:S(2)}) copy-start(bf16[8,128,512]{2,1,0:T(8,128)(2,1)} %up2.1) | copy-start | bytes 3145732
  4.4 27.0 %copy-start.4 = (bf16[8,512,128]{2,1,0:T(8,128)(2,1)S(1)}, bf16[8,512,128]{2,1,0:T(8,128)(2,1)}, u32[]{:S(2)}) copy-start(bf16[8,512,128]{2,1,0:T(8,128)(2,1)} %dn1.1) | copy-start | bytes 3145732
  4.4 27.0 %all-to-all-start = ((bf16[64,32,256]{2,1,0:T(8,128)(2,1)}), bf16[64,32,256]{2,1,0:T(8,128)(2,1)S(1)}, u32[]{:S(2)}, u32[]{:S(2)}) async-start(bf16[64,32,256]{2,1,0:T(8,128)(2,1)} %shard_map.137), calls=%async_computation | async-start | bytes 2097152 | tf_op jit(solution)/shard_map/all_to_all | solution.py:48
  38.8 23.2 %copy-start = (bf16[8,128,128]{2,1,0:T(8,128)(2,1)S(1)}, bf16[8,128,128]{2,1,0:T(8,128)(2,1)}, u32[]{:S(2)}) copy-start(bf16[8,128,128]{2,1,0:T(8,128)(2,1)} %up1.1) | copy-start | bytes 786436
  38.8 23.2 %copy-start.1 = (bf16[256,1024]{1,0:T(8,128)(2,1)S(1)}, bf16[256,1024]{1,0:T(8,128)(2,1)}, u32[]{:S(2)}) copy-start(bf16[256,1024]{1,0:T(8,128)(2,1)} %x.3) | copy-start | bytes 1572868
  38.8 23.2 %copy-start.2 = (bf16[256,1024]{1,0:T(8,128)(2,1)S(1)}, bf16[256,1024]{1,0:T(8,128)(2,1)}, u32[]{:S(2)}) copy-start(bf16[256,1024]{1,0:T(8,128)(2,1)} %y.3) | copy-start | bytes 1572868
  38.8 23.2 %copy-start.6 = (bf16[8,4,64,128]{3,2,1,0:T(8,128)(2,1)S(1)}, bf16[8,4,64,128]{3,2,1,0:T(8,128)(2,1)}, u32[]{:S(2)}) copy-start(bf16[8,4,64,128]{3,2,1,0:T(8,128)(2,1)} %get-tuple-element.14.g23) | copy-start | bytes 1572868
  94.4 35.6 %copy-start.5 = (bf16[8,128,128]{2,1,0:T(8,128)(2,1)S(1)}, bf16[8,128,128]{2,1,0:T(8,128)(2,1)}, u32[]{:S(2)}) copy-start(bf16[8,128,128]{2,1,0:T(8,128)(2,1)} %dn2.1) | copy-start | bytes 786436
  94.4 35.6 %copy-start.7 = (s32[8,4,512]{2,1,0:T(4,128)S(1)}, s32[8,4,512]{2,1,0:T(4,128)}, u32[]{:S(2)}) copy-start(s32[8,4,512]{2,1,0:T(4,128)} %d2.1) | copy-start | bytes 196612
  94.4 35.6 %copy-start.8 = (s32[8,16,128]{2,1,0:T(8,128)S(1)}, s32[8,16,128]{2,1,0:T(8,128)}, u32[]{:S(2)}) copy-start(s32[8,16,128]{2,1,0:T(8,128)} %d3.1) | copy-start | bytes 196612
  94.4 35.6 %copy-start.9 = (s32[8,4,128]{2,1,0:T(4,128)S(1)}, s32[8,4,128]{2,1,0:T(4,128)}, u32[]{:S(2)}) copy-start(s32[8,4,128]{2,1,0:T(4,128)} %d1.1) | copy-start | bytes 49156
  94.4 35.6 %copy-start.10 = (s32[8,4,128]{2,1,0:T(4,128)S(1)}, s32[8,4,128]{2,1,0:T(4,128)}, u32[]{:S(2)}) copy-start(s32[8,4,128]{2,1,0:T(4,128)} %d4.1) | copy-start | bytes 49156

commit v5 on v2

v5 whole, which is shorter than its diff:
```python
import math

import jax
import jax.numpy as jnp
from jax import lax
from jax.experimental import pallas as pl
from jax.experimental.pallas import tpu as pltpu
from jax.sharding import Mesh, PartitionSpec as P

TILE = 128
HB = 512
T = 256
NB = 8
NS = 4
NG = 16
NZ = 8
ML = NB // NS
R = TILE // (NZ * NS)
GRID = 0.25
RATE = 4.0 / math.sqrt(8192)
S1 = TILE ** -0.5
S5 = HB ** -0.5
C0 = math.sqrt(2.0 / math.pi)
BF = jnp.bfloat16
F32 = jnp.float32

DP = ("zh", "zl", "yl")
SUB = ("zl", "yl")
FAR = ("zh",)
GROUP = SUB + ("mp",)

NN = (((1,), (0,)), ((), ()))
NT = (((1,), (1,)), ((), ()))
TN = (((0,), (0,)), ((), ()))
TT = (((0,), (1,)), ((), ()))
PARAMS = pltpu.CompilerParams(vmem_limit_bytes=48 << 20)
ALL_VMEM = pltpu.CompilerParams(vmem_limit_bytes=60 << 20)


def mm(a, b, dims):
    return lax.dot_general(a, b, dims, preferred_element_type=F32)


def exchange(a, axes):
    return lax.all_to_all(a, axes, 0, 0, tiled=True)


def cost(flops, moved):
    return pl.CostEstimate(flops=flops, bytes_accessed=moved, transcendentals=0)


def first_kernel(x, u, y, d, out, rows):
    for h in range(2):
        t = slice(h * 128, (h + 1) * 128)
        for b in range(NB):
            f = slice(b * TILE, (b + 1) * TILE)
            rows[h, pl.ds(b, TILE, stride=2 * NB), :] = mm(u[b], x[t, f], TT) * S1
            rows[h, pl.ds(NB + b, TILE, stride=2 * NB), :] = mm(d[b], y[t, f], NT) * S1
    for h in range(2):
        v = rows[h].reshape(NG, NS, 2 * NB * ML, 128).astype(BF)
        for s in range(NS):
            out[s * NG : (s + 1) * NG, :, h * 128 : (h + 1) * 128] = v[:, s]


def first_stage(x, u, y, d):
    return pl.pallas_call(
        first_kernel,
        out_shape=jax.ShapeDtypeStruct((NS * NG, 2 * NB * ML, T), BF),
        scratch_shapes=[pltpu.VMEM((2, TILE * 2 * NB, 128), F32)],
        compiler_params=ALL_VMEM,
        cost_estimate=cost(2**27, 2**21),
    )(x, u, y, d)


def hidden_kernel(sub, r, w2, w3, out, g):
    w2 = w2[0]
    w3 = w3[0]
    g2 = g3 = None
    for s in range(NS):
        v = r[s * NG : (s + 1) * NG].astype(F32)
        fm = v[:, :NB].reshape(TILE, T).astype(BF)
        bd = v[:, NB:].reshape(TILE, T).astype(BF)
        pre = mm(w2, fm, TN) * S1
        dgated = mm(w3, bd, NN) * S5
        th = jnp.tanh(C0 * (pre + 0.044715 * (pre * pre * pre)))
        cdf = 0.5 * (1.0 + th)
        gated = (pre * cdf).astype(BF)
        slope = cdf + (0.5 * C0) * pre * (1.0 - th * th) * (1.0 + (3 * 0.044715) * (pre * pre))
        dpre = (dgated * slope).astype(BF)
        down = mm(w3, gated, TN) * S5
        back_up = mm(w2, dpre, NN) * S1
        a2 = mm(fm, dpre, NT)
        a3 = mm(gated, bd, NT)
        g2, g3 = (a2, a3) if g2 is None else (g2 + a2, g3 + a3)
        both = jnp.concatenate([down.reshape(NG, NB, T), back_up.reshape(NG, NB, T)], 1)
        out[s * NG : (s + 1) * NG] = both.astype(BF)
    g2 = (g2 * S1).astype(BF)
    g3 = (g3 * S5).astype(BF)
    for c in range(4):
        g[:, c * 16 : (c + 1) * 16] = g2[:, c * 128 : (c + 1) * 128].reshape(NZ, 16, 128)
    g[:, 64:] = g3.reshape(NZ, 64, 128)


def hidden_stage(sub, r, up2, dn1):
    spec = pltpu.PrefetchScalarGridSpec(
        num_scalar_prefetch=1,
        grid=(ML,),
        in_specs=[
            pl.BlockSpec((NS * NG, 2 * NB, T), lambda m, s: (0, m, 0)),
            pl.BlockSpec((1, TILE, HB), lambda m, s: (s[0] * ML + m, 0, 0)),
            pl.BlockSpec((1, HB, TILE), lambda m, s: (s[0] * ML + m, 0, 0)),
        ],
        out_specs=[
            pl.BlockSpec((NS * NG, 2 * NB, T), lambda m, s: (0, m, 0)),
            pl.BlockSpec((NZ, 128, 128), lambda m, s: (0, m, 0)),
        ],
    )
    return pl.pallas_call(
        hidden_kernel,
        grid_spec=spec,
        out_shape=[
            pltpu.HBM((NS * NG, 2 * NB * ML, T), BF),
            pltpu.HBM((NZ, 128 * ML, 128), BF),
        ],
        compiler_params=PARAMS,
        cost_estimate=cost(2**30, 2**22),
    )(sub, r, up2, dn1)


def outer_kernel(r, x, y, u, gin, g14, rows, cut):
    for s in range(NS):
        for h in range(2):
            rows[h, :, s] = r[s * NG : (s + 1) * NG, :, h * 128 : (h + 1) * 128].astype(F32)
    flat = rows.reshape(2, TILE * 2 * NB, 128)

    def pick(j):
        return jnp.concatenate([flat[h, pl.ds(j, TILE, stride=2 * NB), :] for h in range(2)], 1).astype(BF)

    for b in range(NB):
        f = slice(b * TILE, (b + 1) * TILE)
        down, back_up = pick(b), pick(NB + b)
        gin[:, f] = (mm(back_up, u[b], TT) * S1).astype(BF)
        g1 = (mm(x[:, f], back_up, TT) * S1).reshape(NZ, NS, R, TILE)
        g4 = (mm(down, y[:, f], NN) * S1).reshape(NZ, NS, R, TILE)
        for s in range(NS):
            cut[s, :, b * R : (b + 1) * R] = g1[:, s]
            cut[s, :, (NB + b) * R : (NB + b + 1) * R] = g4[:, s]
    g14[...] = cut[...].astype(BF)


def outer_stage(r, x, y, u):
    return pl.pallas_call(
        outer_kernel,
        out_shape=[
            jax.ShapeDtypeStruct((T, NB * TILE), BF),
            jax.ShapeDtypeStruct((NS, NZ, 2 * NB * R, TILE), BF),
        ],
        scratch_shapes=[
            pltpu.VMEM((2, NG, NS, 2 * NB * ML, 128), F32),
            pltpu.VMEM((NS, NZ, 2 * NB * R, TILE), F32),
        ],
        compiler_params=PARAMS,
        cost_estimate=cost(2**27, 2**21),
    )(r, x, y, u)


def near_sum_kernel(a, out):
    v = a[0].astype(F32)
    for s in range(1, NS):
        v = v + a[s].astype(F32)
    out[...] = v.astype(BF)


def near_sum(a):
    return pl.pallas_call(
        near_sum_kernel, out_shape=jax.ShapeDtypeStruct(a.shape[1:], BF), cost_estimate=cost(2**10, 2**10)
    )(a)


def choose(sub, options):
    v = options[-1]
    for s in range(len(options) - 2, -1, -1):
        v = jnp.where(sub == s, options[s], v)
    return v


def split_kernel(r, out):
    v = r[...].astype(F32)
    for s in range(NS):
        parts = []
        for m in range(ML):
            w = v[m * 128 : (m + 1) * 128]
            parts += [w[c * 16 + s * R : c * 16 + (s + 1) * R] for c in range(4)]
            parts.append(w[64 + s * 16 : 64 + (s + 1) * 16])
        out[s] = jnp.concatenate(parts, 0).astype(BF)


def split_rows(r):
    return pl.pallas_call(
        split_kernel,
        out_shape=jax.ShapeDtypeStruct((NS, 32 * ML, 128), BF),
        cost_estimate=cost(2**10, 2**10),
    )(r)


def step(weight, grad, dither):
    noise = GRID * (dither.astype(F32) / 32768.0 - 0.5)
    return (weight - RATE * grad + noise).astype(BF)


def own_rows(sub, block):
    v = block.astype(F32)
    return choose(sub, [v[:, s * R : (s + 1) * R] for s in range(NS)])


def update_kernel(at, a, q, up1, up2, dn1, dn2, d1, d2, d3, d4, n1, n2, n3, n4):
    sub = at[1]
    v = a[0].astype(F32)
    for z in range(1, NZ):
        v = v + a[z].astype(F32)
    g = v.reshape(2, NB, R, TILE)
    n1[...] = step(own_rows(sub, up1[...]), g[0], d1[...])
    n4[...] = step(own_rows(sub, dn2[...]), g[1], d4[...])
    own = own_rows(sub, up2[...])
    for s in range(NS):
        v = q[s].astype(F32)
        for i in range(ML):
            m = s * ML + i
            w = v[i * 8 * R : (i + 1) * 8 * R]
            grad = jnp.concatenate([w[c * R : (c + 1) * R] for c in range(4)], 1)
            n2[m] = step(own[m], grad, d2[m])
            n3[m] = step(dn1[m].astype(F32), w[4 * R :], d3[m])


def update(at, a, q, up1, up2, dn1, dn2, d1, d2, d3, d4):
    def whole(*shape):
        return pl.BlockSpec(shape, lambda i, s: (0,) * len(shape))

    def far(s):
        return s[0]

    small = whole(NB, R, TILE)
    wide = whole(NB, R, HB)
    large = whole(NB, 4 * R, TILE)
    block = pl.BlockSpec((NB, NS * R, TILE), lambda i, s: (0, far(s), 0))
    spec = pltpu.PrefetchScalarGridSpec(
        num_scalar_prefetch=1,
        grid=(1,),
        in_specs=[
            whole(NZ, 2 * NB * R, TILE),
            whole(NS, 8 * R * ML, 128),
            block,
            pl.BlockSpec((NB, NS * R, HB), lambda i, s: (0, far(s), 0)),
            pl.BlockSpec((NB, 4 * R, TILE), lambda i, s: (0, far(s) * NS + s[1], 0)),
            block,
            small,
            wide,
            large,
            small,
        ],
        out_specs=[small, wide, large, small],
    )
    shapes = ((NB, R, TILE), (NB, R, HB), (NB, 4 * R, TILE), (NB, R, TILE))
    return pl.pallas_call(
        update_kernel,
        grid_spec=spec,
        out_shape=[jax.ShapeDtypeStruct(shape, BF) for shape in shapes],
        compiler_params=PARAMS,
        cost_estimate=cost(2**10, 2**10),
    )(at, a, q, up1, up2, dn1, dn2, d1, d2, d3, d4)


def on_device(x, dy, up1, up2, dn1, dn2, di1, di2, di3, di4):
    sub = lax.axis_index(SUB).astype(jnp.int32)
    far = lax.axis_index(FAR).astype(jnp.int32)
    at = jnp.stack([far, sub])
    sub1 = sub.reshape(1)

    got = exchange(first_stage(x, up1, dy, dn2), GROUP)
    send, g23 = hidden_stage(sub1, got, up2, dn1)
    r23 = lax.psum_scatter(g23, FAR, scatter_dimension=0, tiled=True).reshape(128 * ML, 128)

    def tail(send, x, dy, up1):
        gin, g14 = outer_stage(exchange(send, GROUP), x, dy, up1)
        return gin, exchange(near_sum(exchange(g14, SUB)), FAR)

    def never(send, x, dy, up1):
        return jnp.zeros((T, NB * TILE), BF), jnp.zeros((NZ, 2 * NB * R, TILE), BF)

    gin, g14 = lax.cond(lax.axis_index("mp") < 999, tail, never, send, x, dy, up1)
    g14, r23, gin = lax.optimization_barrier((g14, r23, gin))
    q = exchange(split_rows(r23), SUB)
    new1, new2, new3, new4 = update(at, g14, q, up1, up2, dn1, dn2, di1, di2, di3, di4)
    return gin, new1, new2, new3, new4


def solution(mesh):
    dp, mp = mesh.shape["dp"], mesh.shape["mp"]
    fine = Mesh(mesh.devices.reshape(dp // 4, 2, 2, mp), ("zh", "zl", "yl", "mp"))
    w = P("mp", None, None)
    d = P("mp", DP, None)
    return jax.shard_map(
        on_device,
        mesh=fine,
        in_specs=(P(DP, "mp"), P(DP, "mp"), w, w, w, w, d, d, d, d),
        out_specs=(P(DP, "mp"), d, d, d, d),
        check_vma=False,
    )
```

time: 134 us -> 137 us (1.022)
  starting transfers between devices: 38.3 us -> 13.7 us
  between operations: 0.8 us -> 14.1 us
  blocking collectives: 61.9 us -> 69.8 us
  waiting for transfers between devices: 15.3 us -> 20.1 us
    ppermute x4 -> x0, starting transfers between devices: 28.2 us -> none  [the longest x3 15.5 us: on_device(): lax.ppermute(p[k], 'zq', [(i, i ^ k) for i in range(NQ)])]
    all_to_all x3, blocking collectives: 61.9 us -> 69.8 us  [exchange(): return lax.all_to_all(a, axes, 0, 0, tiled=True)]
    all_to_all x1 -> x2, waiting for transfers between devices: 15.3 us -> 20.1 us  [exchange(): return lax.all_to_all(a, axes, 0, 0, tiled=True)]
    all_to_all x1 -> x2, starting transfers between devices: 10.1 us -> 13.7 us  [exchange(): return lax.all_to_all(a, axes, 0, 0, tiled=True)]
    pallas_call x2 -> x3, Pallas kernels: 8.06 us -> 10.2 us  [the longest x1 6.89 us: hidden_stage(): pl.pallas_call(hidden_kernel, grid_spec=spec, out_shape=[pltpu.HBM((NS *...]
    pallas_call x1, Pallas kernels: 3.44 us -> 1.99 us  [outer_stage(): pl.pallas_call(outer_kernel, out_shape=[jax.ShapeDtypeStruct((T, NB * TIL...]
  transfers between devices with their start and end apart: 5 -> 3, of which waited for: 1 -> 2; matrix products, arithmetic and copies ran while one was open for 0% -> 0% of each run, Pallas kernels for 0% -> 3%
where the time goes in v5:
time: 137 us; the launch traced here: 136 us
  blocking collectives  69.8 us (51%)
  waiting for transfers between devices  20.1 us (15%)
  Pallas kernels  17.2 us (13%)
  between operations  14.1 us (10%)
  starting transfers between devices  13.7 us (10%)
    all_to_all x3, blocking collectives, exchange(): return lax.all_to_all(a, axes, 0, 0, tiled=True)  69.8 us
    all_to_all x2, waiting for transfers between devices, exchange(): return lax.all_to_all(a, axes, 0, 0, tiled=True)  20.1 us
    all_to_all x2, starting transfers between devices, exchange(): return lax.all_to_all(a, axes, 0, 0, tiled=True)  13.7 us
    pallas_call x1, Pallas kernels, hidden_stage(): pl.pallas_call(hidden_kernel, grid_spec=spec, out_shape=[pltpu.HBM((NS *...  6.89 us
    pallas_call x1, Pallas kernels, first_stage(): pl.pallas_call(first_kernel, out_shape=jax.ShapeDtypeStruct((NS * NG, 2 *...  3.72 us
  transfers between devices with their start and end apart: 3, of which 2 were waited for; matrix products, arithmetic and copies ran while one was open for 0% of the time, Pallas kernels for 3%

profile of v5, /device:TPU:6, one launch (start us, length us, event | category | flops | bytes accessed | tf_op | source)
XLA Modules:
  0.0 135.9 jit_solution(5188091417352493729)
XLA Ops:
  7.2 3.7 %shard_map.137 = bf16[64,32,256]{2,1,0:T(8,128)(2,1)} custom-call(bf16[256,1024]{1,0:T(8,128)(2,1)} %x.1, bf16[8,128,128]{2,1,0:T(8,128)(2,1)} %up1.1, bf16[256,1024]{1,0:T(8,128)(2,1)} %y.1, bf16[8,128,128]{2,1,0:T(8,128)(2,1)} %dn2.1), custom_call_target="tpu_custom_call" | custom-call | flops 134217728 | bytes 2097152 | tf_op jit(solution)/shard_map/pallas_call | solution.py:66
  10.9 0.0 copy-start
  10.9 0.0 copy-start.1
  10.9 10.1 %all-to-all-start.3 = ((bf16[64,32,256]{2,1,0:T(8,128)(2,1)}), bf16[64,32,256]{2,1,0:T(8,128)(2,1)S(1)}, u32[]{:S(2)}, u32[]{:S(2)}) async-start(bf16[64,32,256]{2,1,0:T(8,128)(2,1)} %shard_map.137), calls=%async_computation.3 | async-start | bytes 2097152 | tf_op jit(solution)/shard_map/all_to_all | solution.py:45
  21.0 0.0 reduce-scatter.2.cloned.1.call-start
  21.1 15.3 %all-to-all-done.3.r = bf16[64,32,256]{2,1,0:T(8,128)(2,1)S(1)} async-done(((bf16[64,32,256]{2,1,0:T(8,128)(2,1)}), bf16[64,32,256]{2,1,0:T(8,128)(2,1)S(1)}, u32[]{:S(2)}, u32[]{:S(2)}) %all-to-all-start.3) | async-done | bytes 1048608 | tf_op jit(solution)/shard_map/all_to_all | solution.py:45
  36.4 0.0 copy-done
  36.4 0.0 copy-done.1
  36.4 6.9 %shard_map.138 = (bf16[64,32,256]{2,1,0:T(8,128)(2,1)}, bf16[8,256,128]{2,1,0:T(8,128)(2,1)}) custom-call(s32[1]{0:T(128)} %bitcast.sub, bf16[64,32,256]{2,1,0:T(8,128)(2,1)S(1)} %all-to-all-done.3.r, bf16[8,128,512]{2,1,0:T(8,128)(2,1)S(1)} %copy-done, bf16[8,512,128]{2,1,0:T(8,128)(2,1)S(1)} %copy-done.1), custom_call_target="tpu_custom_call" | custom-call | flops 1073741824 | bytes 4194304 | tf_op jit(solution)/shard_map/pallas_call | solution.py:118
  43.3 0.0 copy-start.7
  43.3 0.0 reduce-scatter.2.cloned.1.call-update
  43.3 0.9 copy-done.7
  44.3 0.0 copy-start.3
  44.3 0.0 copy-start.4
  44.3 0.0 copy-start.5
  44.3 0.0 copy-start.6
  44.3 73.5 %conditional.1 = (bf16[256,1024]{1,0:T(8,128)(2,1)}, bf16[8,64,128]{2,1,0:T(8,128)(2,1)S(1)}) conditional(s32[]{:T(128)} %convert_element_type.3, () %tuple.17, (bf16[64,32,256]{2,1,0:T(8,128)(2,1)}, bf16[256,1024]{1,0:T(8,128)(2,1)}, bf16[256,1024]{1,0:T(8,128)(2,1)}, bf16[8,128,128]{2,1,0:T(8,128)(2,1)S(1)}) %tuple.25), branch_computations={%region_0.0_spmd, %region_1.0_spmd} | conditional | flops 134218752 | bytes 9700424 | solution.py:290
  44.3 0.0 copy-start.8
  44.3 0.0 copy-start.9
  44.3 24.5 %all_to_all.22.r = bf16[64,32,256]{2,1,0:T(8,128)(2,1)S(1)} all-to-all(bf16[64,32,256]{2,1,0:T(8,128)(2,1)} %get-tuple-element.8), channel_id=1, replica_groups=mesh['zh'=8,'zl'=2,'yl'=2,'mp'=16] {'zl','yl','mp'}, dimensions={0} | all-to-all | bytes 2097152 | tf_op jit(solution)/shard_map/cond/branch_1_fun/all_to_all | solution.py:45
  68.9 0.0 copy-done.8
  68.9 0.0 copy-done.9
  68.9 2.0 %branch_1_fun.2 = (bf16[256,1024]{1,0:T(8,128)(2,1)}, bf16[4,8,64,128]{3,2,1,0:T(8,128)(2,1)S(1)}) custom-call(bf16[64,32,256]{2,1,0:T(8,128)(2,1)S(1)} %all_to_all.22.r, bf16[256,1024]{1,0:T(8,128)(2,1)S(1)} %copy-done.8, bf16[256,1024]{1,0:T(8,128)(2,1)S(1)} %copy-done.9, bf16[8,128,128]{2,1,0:T(8,128)(2,1)S(1)} %get-tuple-element.11.u), custom_call_target="tpu_custom_call" | custom-call | flops 134217728 | bytes 2097152 | tf_op jit(solution)/shard_map/cond/branch_1_fun/pallas_call | solution.py:152
  70.8 15.5 %all_to_all.23.a = bf16[4,8,64,128]{3,2,1,0:T(8,128)(2,1)} all-to-all(bf16[4,8,64,128]{3,2,1,0:T(8,128)(2,1)S(1)} %get-tuple-element.13), channel_id=1, replica_groups=mesh['zh'=8,'zl'=2,'yl'=2,'mp'=16] {'zl','yl'}, dimensions={0} | all-to-all | bytes 1048576 | tf_op jit(solution)/shard_map/cond/branch_1_fun/all_to_all | solution.py:45
  86.4 1.8 %branch_1_fun.3 = bf16[8,64,128]{2,1,0:T(8,128)(2,1)} custom-call(bf16[4,8,64,128]{3,2,1,0:T(8,128)(2,1)} %all_to_all.23.a), custom_call_target="tpu_custom_call" | custom-call | flops 1024 | bytes 1024 | tf_op jit(solution)/shard_map/cond/branch_1_fun/pallas_call | solution.py:175
  88.1 29.7 %all_to_all.24 = bf16[8,64,128]{2,1,0:T(8,128)(2,1)S(1)} all-to-all(bf16[8,64,128]{2,1,0:T(8,128)(2,1)} %branch_1_fun.3), channel_id=1, replica_groups=mesh['zh'=8,'zl'=2,'yl'=2,'mp'=16] {'zh'}, dimensions={0} | all-to-all | bytes 262144 | tf_op jit(solution)/shard_map/cond/branch_1_fun/all_to_all | solution.py:45
  117.8 0.0 copy-start.2
  117.8 0.0 reduce-scatter.2.cloned.1.call-done
  117.8 1.5 %shard_map.139 = bf16[4,64,128]{2,1,0:T(8,128)(2,1)} custom-call(bf16[256,128]{1,0:T(8,128)(2,1)} %bitcast.3), custom_call_target="tpu_custom_call" | custom-call | flops 1024 | bytes 1024 | tf_op jit(solution)/shard_map/pallas_call | solution.py:199
  119.3 3.6 %all-to-all-start.4 = ((bf16[4,64,128]{2,1,0:T(8,128)(2,1)}), bf16[4,64,128]{2,1,0:T(8,128)(2,1)S(1)}, u32[]{:S(2)}, u32[]{:S(2)}) async-start(bf16[4,64,128]{2,1,0:T(8,128)(2,1)} %shard_map.139), calls=%async_computation.5 | async-start | bytes 131072 | tf_op jit(solution)/shard_map/all_to_all | solution.py:45
  122.9 0.1 pad_add_fusion.at
  123.0 4.8 %all-to-all-done.4.q = bf16[4,64,128]{2,1,0:T(8,128)(2,1)S(1)} async-done(((bf16[4,64,128]{2,1,0:T(8,128)(2,1)}), bf16[4,64,128]{2,1,0:T(8,128)(2,1)S(1)}, u32[]{:S(2)}, u32[]{:S(2)}) %all-to-all-start.4) | async-done | bytes 65568 | tf_op jit(solution)/shard_map/all_to_all | solution.py:45
  127.7 0.0 copy-done.3
  127.7 0.0 copy-done.4
  127.7 0.0 copy-done.5
  127.8 0.0 copy-done.6
  127.8 0.0 copy-done.2
  127.8 1.3 shard_map.140
Async XLA Ops:
  10.9 25.5 %copy-start = (bf16[8,128,512]{2,1,0:T(8,128)(2,1)S(1)}, bf16[8,128,512]{2,1,0:T(8,128)(2,1)}, u32[]{:S(2)}) copy-start(bf16[8,128,512]{2,1,0:T(8,128)(2,1)} %up2.1) | copy-start | bytes 3145732
  10.9 25.5 %copy-start.1 = (bf16[8,512,128]{2,1,0:T(8,128)(2,1)S(1)}, bf16[8,512,128]{2,1,0:T(8,128)(2,1)}, u32[]{:S(2)}) copy-start(bf16[8,512,128]{2,1,0:T(8,128)(2,1)} %dn1.1) | copy-start | bytes 3145732
  10.9 25.5 %all-to-all-start.3 = ((bf16[64,32,256]{2,1,0:T(8,128)(2,1)}), bf16[64,32,256]{2,1,0:T(8,128)(2,1)S(1)}, u32[]{:S(2)}, u32[]{:S(2)}) async-start(bf16[64,32,256]{2,1,0:T(8,128)(2,1)} %shard_map.137), calls=%async_computation.3 | async-start | bytes 2097152 | tf_op jit(solution)/shard_map/all_to_all | solution.py:45
  21.0 96.8 %reduce-scatter.2.cloned.1.call-start = ((), (), s32[]{:S(2)}) async-start(), calls=%async_computation.6 | async-start | bytes 589824 | tf_op jit(solution)/shard_map/reduce_scatter | solution.py:281
  43.3 0.9 copy-start.7
  44.3 83.5 %copy-start.3 = (s32[8,4,512]{2,1,0:T(4,128)S(1)}, s32[8,4,512]{2,1,0:T(4,128)}, u32[]{:S(2)}) copy-start(s32[8,4,512]{2,1,0:T(4,128)} %d2.1) | copy-start | bytes 196612
  44.3 83.5 %copy-start.4 = (s32[8,16,128]{2,1,0:T(8,128)S(1)}, s32[8,16,128]{2,1,0:T(8,128)}, u32[]{:S(2)}) copy-start(s32[8,16,128]{2,1,0:T(8,128)} %d3.1) | copy-start | bytes 196612
  44.3 83.5 %copy-start.5 = (s32[8,4,128]{2,1,0:T(4,128)S(1)}, s32[8,4,128]{2,1,0:T(4,128)}, u32[]{:S(2)}) copy-start(s32[8,4,128]{2,1,0:T(4,128)} %d1.1) | copy-start | bytes 49156
  44.3 83.5 %copy-start.6 = (s32[8,4,128]{2,1,0:T(4,128)S(1)}, s32[8,4,128]{2,1,0:T(4,128)}, u32[]{:S(2)}) copy-start(s32[8,4,128]{2,1,0:T(4,128)} %d4.1) | copy-start | bytes 49156
  44.3 24.6 %copy-start.8 = (bf16[256,1024]{1,0:T(8,128)(2,1)S(1)}, bf16[256,1024]{1,0:T(8,128)(2,1)}, u32[]{:S(2)}) copy-start(bf16[256,1024]{1,0:T(8,128)(2,1)} %get-tuple-element.9.x) | copy-start | bytes 1572868 | tf_op jit(solution)/shard_map/cond
  44.3 24.6 %copy-start.9 = (bf16[256,1024]{1,0:T(8,128)(2,1)S(1)}, bf16[256,1024]{1,0:T(8,128)(2,1)}, u32[]{:S(2)}) copy-start(bf16[256,1024]{1,0:T(8,128)(2,1)} %get-tuple-element.10.y) | copy-start | bytes 1572868 | tf_op jit(solution)/shard_map/cond
  117.8 9.9 %copy-start.2 = (bf16[8,128,128]{2,1,0:T(8,128)(2,1)S(1)}, bf16[8,128,128]{2,1,0:T(8,128)(2,1)}, u32[]{:S(2)}) copy-start(bf16[8,128,128]{2,1,0:T(8,128)(2,1)} %dn2.1) | copy-start | bytes 786436
  119.3 8.4 %all-to-all-start.4 = ((bf16[4,64,128]{2,1,0:T(8,128)(2,1)}), bf16[4,64,128]{2,1,0:T(8,128)(2,1)S(1)}, u32[]{:S(2)}, u32[]{:S(2)}) async-start(bf16[4,64,128]{2,1,0:T(8,128)(2,1)} %shard_map.139), calls=%async_computation.5 | async-start | bytes 131072 | tf_op jit(solution)/shard_map/all_to_all | solution.py:45
Sparse Core Ops, SparseCore 0:
  43.5 50.9 reduce-scatter.1

commit v6 on v4

--- a/solution.py
+++ b/solution.py
@@ -37,7 +37,6 @@
 TT = (((0,), (1,)), ((), ()))
 PARAMS = pltpu.CompilerParams(vmem_limit_bytes=48 << 20)
 FULL = pltpu.CompilerParams(vmem_limit_bytes=64 << 20)
-ALL_VMEM = pltpu.CompilerParams(vmem_limit_bytes=60 << 20)
 
 
 def mm(a, b, dims):
@@ -52,25 +51,54 @@
     return pl.CostEstimate(flops=flops, bytes_accessed=moved, transcendentals=0)
 
 
-def first_kernel(x, u, y, d, out, rows):
+def first_kernel(x_in, u_in, y_in, d_in, out, x, u, y, d, rows, sent, sems):
+    pairs = ((x_in, x), (u_in, u), (y_in, y), (d_in, d))
+    loads = [pltpu.make_async_copy(a, b, sems.at[i]) for i, (a, b) in enumerate(pairs)]
+    for load in loads:
+        load.start()
+    loads[0].wait()
+    loads[1].wait()
     for h in range(2):
         t = slice(h * 128, (h + 1) * 128)
         for b in range(NB):
             f = slice(b * TILE, (b + 1) * TILE)
             rows[h, pl.ds(b, TILE, stride=2 * NB), :] = mm(u[b], x[t, f], TT) * S1
+    loads[2].wait()
+    loads[3].wait()
+    for h in range(2):
+        t = slice(h * 128, (h + 1) * 128)
+        for b in range(NB):
+            f = slice(b * TILE, (b + 1) * TILE)
             rows[h, pl.ds(NB + b, TILE, stride=2 * NB), :] = mm(d[b], y[t, f], NT) * S1
-    for h in range(2):
-        v = rows[h].reshape(NG, NS, 2 * NB * ML, 128).astype(BF)
-        for s in range(NS):
-            out[s * NG : (s + 1) * NG, :, h * 128 : (h + 1) * 128] = v[:, s]
+    view = rows.reshape(2, NG, NS, 2 * NB * ML, 128)
+    stores = []
+    for s in range(NS):
+        for h in range(2):
+            sent[s, :, :, h * 128 : (h + 1) * 128] = view[h, :, s].astype(BF)
+        store = pltpu.make_async_copy(sent.at[s], out.at[pl.ds(s * NG, NG)], sems.at[4 + s])
+        store.start()
+        stores.append(store)
+    for store in stores:
+        store.wait()
 
 
 def first_stage(x, u, y, d):
+    hbm = pl.BlockSpec(memory_space=pltpu.HBM)
     return pl.pallas_call(
         first_kernel,
+        in_specs=[hbm] * 4,
+        out_specs=hbm,
         out_shape=jax.ShapeDtypeStruct((NS * NG, 2 * NB * ML, T), BF),
-        scratch_shapes=[pltpu.VMEM((2, TILE * 2 * NB, 128), F32)],
-        compiler_params=ALL_VMEM,
+        scratch_shapes=[
+            pltpu.VMEM(x.shape, BF),
+            pltpu.VMEM(u.shape, BF),
+            pltpu.VMEM(y.shape, BF),
+            pltpu.VMEM(d.shape, BF),
+            pltpu.VMEM((2, TILE * 2 * NB, 128), F32),
+            pltpu.VMEM((NS, NG, 2 * NB * ML, T), BF),
+            pltpu.SemaphoreType.DMA((4 + NS,)),
+        ],
+        compiler_params=FULL,
         cost_estimate=cost(2**27, 2**21),
     )(x, u, y, d)
 
@@ -83,13 +111,14 @@
         v = r[s * NG : (s + 1) * NG].astype(F32)
         fm = v[:, :NB].reshape(TILE, T).astype(BF)
         bd = v[:, NB:].reshape(TILE, T).astype(BF)
-        pre = mm(w2, fm, TN) * S1
-        dgated = mm(w3, bd, NN) * S5
-        th = jnp.tanh(C0 * (pre + 0.044715 * (pre * pre * pre)))
-        cdf = 0.5 * (1.0 + th)
-        gated = (pre * cdf).astype(BF)
-        slope = cdf + (0.5 * C0) * pre * (1.0 - th * th) * (1.0 + (3 * 0.044715) * (pre * pre))
-        dpre = (dgated * slope).astype(BF)
+        w = mm(w2, fm, TN)
+        dgated = mm(w3, bd, NN)
+        square = w * w
+        h = 0.5 + 0.5 * jnp.tanh(w * (C0 * S1 + (C0 * 0.044715 * S1**3) * square))
+        gated = ((w * S1) * h).astype(BF)
+        bend = w * (2.0 * C0 * S1 + (6.0 * C0 * 0.044715 * S1**3) * square)
+        slope = h + (h * (1.0 - h)) * bend
+        dpre = ((dgated * S5) * slope).astype(BF)
         down = mm(w3, gated, TN) * S5
         back_up = mm(w2, dpre, NN) * S1
         a2 = mm(fm, dpre, NT)

time: 132 us -> 131 us (level)
  no operation moved by 1% of the time
where the time goes in v6:
time: 131 us; the launch traced here: 130 us
  blocking collectives  88.8 us (68%)
  waiting for transfers between devices  17 us (13%)
  Pallas kernels  13.8 us (11%)
  starting transfers between devices  9.92 us (8%)
    all_to_all x3, blocking collectives, exchange(): return lax.all_to_all(a, axes, 0, 0, tiled=True)  88.8 us
    all_to_all x1, waiting for transfers between devices, exchange(): return lax.all_to_all(a, axes, 0, 0, tiled=True)  17 us
    all_to_all x1, starting transfers between devices, exchange(): return lax.all_to_all(a, axes, 0, 0, tiled=True)  9.92 us
    pallas_call x1, Pallas kernels, hidden_stage(): pl.pallas_call(hidden_kernel, grid_spec=spec, out_shape=[pltpu.HBM((NS *...  6.65 us
    pallas_call x1, Pallas kernels, first_stage(): pl.pallas_call(first_kernel, in_specs=[hbm] * 4, out_specs=hbm, out_shape...  3.54 us
  transfers between devices with their start and end apart: 1, of which 1 were waited for; matrix products, arithmetic and copies ran while one was open for 0% of the time, Pallas kernels for 0%

profile of v6, /device:TPU:32, one launch (start us, length us, event | category | flops | bytes accessed | tf_op | source)
XLA Modules:
  0.0 130.4 jit_solution(15048136359110886617)
XLA Ops:
  0.6 3.5 %shard_map.137 = bf16[64,32,256]{2,1,0:T(8,128)(2,1)} custom-call(bf16[256,1024]{1,0:T(8,128)(2,1)} %x.1, bf16[8,128,128]{2,1,0:T(8,128)(2,1)} %up1.1, bf16[256,1024]{1,0:T(8,128)(2,1)} %y.1, bf16[8,128,128]{2,1,0:T(8,128)(2,1)} %dn2.1), custom_call_target="tpu_custom_call" | custom-call | flops 134217728 | bytes 2097152 | tf_op jit(solution)/shard_map/pallas_call | solution.py:87
  4.2 0.0 copy-start.3
  4.2 0.0 copy-start.4
  4.2 9.9 %all-to-all-start = ((bf16[64,32,256]{2,1,0:T(8,128)(2,1)}), bf16[64,32,256]{2,1,0:T(8,128)(2,1)S(1)}, u32[]{:S(2)}, u32[]{:S(2)}) async-start(bf16[64,32,256]{2,1,0:T(8,128)(2,1)} %shard_map.137), calls=%async_computation | async-start | bytes 2097152 | tf_op jit(solution)/shard_map/all_to_all | solution.py:47
  14.1 0.1 pad_add_fusion.at
  14.2 17.0 %all-to-all-done.r = bf16[64,32,256]{2,1,0:T(8,128)(2,1)S(1)} async-done(((bf16[64,32,256]{2,1,0:T(8,128)(2,1)}), bf16[64,32,256]{2,1,0:T(8,128)(2,1)S(1)}, u32[]{:S(2)}, u32[]{:S(2)}) %all-to-all-start) | async-done | bytes 1048608 | tf_op jit(solution)/shard_map/all_to_all | solution.py:47
  31.2 0.0 copy-done.3
  31.2 0.0 copy-done.4
  31.2 6.6 %shard_map.138 = (bf16[64,32,256]{2,1,0:T(8,128)(2,1)}, bf16[8,4,64,128]{3,2,1,0:T(8,128)(2,1)}) custom-call(s32[3]{0:T(128)S(1)} %pad_add_fusion.at, bf16[64,32,256]{2,1,0:T(8,128)(2,1)S(1)} %all-to-all-done.r, bf16[8,128,512]{2,1,0:T(8,128)(2,1)S(1)} %copy-done.3, bf16[8,512,128]{2,1,0:T(8,128)(2,1)S(1)} %copy-done.4), custom_call_target="tpu_custom_call" | custom-call | flops 1073741824 | bytes 4194304 | tf_op jit(solution)/shard_map/pallas_call | solution.py:151
  37.8 0.0 copy-start
  37.8 0.0 copy-start.1
  37.8 0.0 copy-start.2
  37.8 0.0 copy-start.6
  37.9 23.2 %all_to_all.20.r = bf16[64,32,256]{2,1,0:T(8,128)(2,1)S(1)} all-to-all(bf16[64,32,256]{2,1,0:T(8,128)(2,1)} %get-tuple-element.13), channel_id=1, replica_groups=mesh['fq'=4,'z1'=2,'zl'=2,'yl'=2,'mp'=16] {'zl','yl','mp'}, dimensions={0} | all-to-all | bytes 2097152 | tf_op jit(solution)/shard_map/all_to_all | solution.py:47
  61.0 0.0 copy-done
  61.0 0.0 copy-done.1
  61.0 0.0 copy-done.2
  61.0 0.0 copy-done.6
  61.0 2.2 %shard_map.139 = (bf16[256,1024]{1,0:T(8,128)(2,1)}, bf16[8,4,2,64,128]{4,3,2,1,0:T(8,128)(2,1)S(1)}) custom-call(bf16[64,32,256]{2,1,0:T(8,128)(2,1)S(1)} %all_to_all.20.r, bf16[256,1024]{1,0:T(8,128)(2,1)S(1)} %copy-done.1, bf16[256,1024]{1,0:T(8,128)(2,1)S(1)} %copy-done.2, bf16[8,128,128]{2,1,0:T(8,128)(2,1)S(1)} %copy-done, ...), custom_call_target="tpu_custom_call" | custom-call | flops 1024 | bytes 1024 | tf_op jit(solution)/shard_map/pallas_call | solution.py:187
  63.2 30.1 %all_to_all.21.a = bf16[8,4,2,64,128]{4,3,2,1,0:T(8,128)(2,1)S(1)} all-to-all(bf16[8,4,2,64,128]{4,3,2,1,0:T(8,128)(2,1)S(1)} %get-tuple-element.16), channel_id=1, replica_groups=mesh['fq'=4,'z1'=2,'zl'=2,'yl'=2,'mp'=16] {'z1','zl','yl'}, dimensions={0} | all-to-all | bytes 2097152 | tf_op jit(solution)/shard_map/all_to_all | solution.py:47
  93.3 0.1 shard_map.140
  93.4 0.0 copy-start.5
  93.5 0.0 copy-start.7
  93.5 0.0 copy-start.8
  93.5 0.0 copy-start.9
  93.5 0.0 copy-start.10
  93.5 35.5 %all_to_all.22.a = bf16[4,5,64,128]{3,2,1,0:T(8,128)(2,1)S(1)} all-to-all(bf16[4,5,64,128]{3,2,1,0:T(8,128)(2,1)S(1)} %shard_map.140), channel_id=1, replica_groups=mesh['fq'=4,'z1'=2,'zl'=2,'yl'=2,'mp'=16] {'fq'}, dimensions={0} | all-to-all | bytes 655360 | tf_op jit(solution)/shard_map/all_to_all | solution.py:47
  129.0 0.0 copy-done.5
  129.0 0.0 copy-done.7
  129.0 0.0 copy-done.8
  129.1 0.0 copy-done.9
  129.1 0.0 copy-done.10
  129.1 1.3 %shard_map.141 = (bf16[8,4,128]{2,1,0:T(4,128)(2,1)}, bf16[8,4,512]{2,1,0:T(4,128)(2,1)}, bf16[8,16,128]{2,1,0:T(8,128)(2,1)}, bf16[8,4,128]{2,1,0:T(4,128)(2,1)}) custom-call(s32[3]{0:T(128)S(1)} %pad_add_fusion.at, bf16[4,5,64,128]{3,2,1,0:T(8,128)(2,1)S(1)} %all_to_all.22.a, bf16[8,128,128]{2,1,0:T(8,128)(2,1)S(1)} %copy-done, ...), custom_call_target="tpu_custom_call" | custom-call | flops 1024 | bytes 1024 | tf_op jit(solution)/shard_map/pallas_call | solution.py:288
Async XLA Ops:
  4.2 27.0 %copy-start.3 = (bf16[8,128,512]{2,1,0:T(8,128)(2,1)S(1)}, bf16[8,128,512]{2,1,0:T(8,128)(2,1)}, u32[]{:S(2)}) copy-start(bf16[8,128,512]{2,1,0:T(8,128)(2,1)} %up2.1) | copy-start | bytes 3145732
  4.2 27.0 %copy-start.4 = (bf16[8,512,128]{2,1,0:T(8,128)(2,1)S(1)}, bf16[8,512,128]{2,1,0:T(8,128)(2,1)}, u32[]{:S(2)}) copy-start(bf16[8,512,128]{2,1,0:T(8,128)(2,1)} %dn1.1) | copy-start | bytes 3145732
  4.2 27.0 %all-to-all-start = ((bf16[64,32,256]{2,1,0:T(8,128)(2,1)}), bf16[64,32,256]{2,1,0:T(8,128)(2,1)S(1)}, u32[]{:S(2)}, u32[]{:S(2)}) async-start(bf16[64,32,256]{2,1,0:T(8,128)(2,1)} %shard_map.137), calls=%async_computation | async-start | bytes 2097152 | tf_op jit(solution)/shard_map/all_to_all | solution.py:47
  37.8 23.2 %copy-start = (bf16[8,128,128]{2,1,0:T(8,128)(2,1)S(1)}, bf16[8,128,128]{2,1,0:T(8,128)(2,1)}, u32[]{:S(2)}) copy-start(bf16[8,128,128]{2,1,0:T(8,128)(2,1)} %up1.1) | copy-start | bytes 786436
  37.8 23.2 %copy-start.1 = (bf16[256,1024]{1,0:T(8,128)(2,1)S(1)}, bf16[256,1024]{1,0:T(8,128)(2,1)}, u32[]{:S(2)}) copy-start(bf16[256,1024]{1,0:T(8,128)(2,1)} %x.1) | copy-start | bytes 1572868
  37.8 23.2 %copy-start.2 = (bf16[256,1024]{1,0:T(8,128)(2,1)S(1)}, bf16[256,1024]{1,0:T(8,128)(2,1)}, u32[]{:S(2)}) copy-start(bf16[256,1024]{1,0:T(8,128)(2,1)} %y.1) | copy-start | bytes 1572868
  37.8 23.2 %copy-start.6 = (bf16[8,4,64,128]{3,2,1,0:T(8,128)(2,1)S(1)}, bf16[8,4,64,128]{3,2,1,0:T(8,128)(2,1)}, u32[]{:S(2)}) copy-start(bf16[8,4,64,128]{3,2,1,0:T(8,128)(2,1)} %get-tuple-element.14.g23) | copy-start | bytes 1572868
  93.4 35.6 %copy-start.5 = (bf16[8,128,128]{2,1,0:T(8,128)(2,1)S(1)}, bf16[8,128,128]{2,1,0:T(8,128)(2,1)}, u32[]{:S(2)}) copy-start(bf16[8,128,128]{2,1,0:T(8,128)(2,1)} %dn2.1) | copy-start | bytes 786436
  93.5 35.6 %copy-start.7 = (s32[8,4,512]{2,1,0:T(4,128)S(1)}, s32[8,4,512]{2,1,0:T(4,128)}, u32[]{:S(2)}) copy-start(s32[8,4,512]{2,1,0:T(4,128)} %d2.1) | copy-start | bytes 196612
  93.5 35.6 %copy-start.8 = (s32[8,16,128]{2,1,0:T(8,128)S(1)}, s32[8,16,128]{2,1,0:T(8,128)}, u32[]{:S(2)}) copy-start(s32[8,16,128]{2,1,0:T(8,128)} %d3.1) | copy-start | bytes 196612
  93.5 35.6 %copy-start.9 = (s32[8,4,128]{2,1,0:T(4,128)S(1)}, s32[8,4,128]{2,1,0:T(4,128)}, u32[]{:S(2)}) copy-start(s32[8,4,128]{2,1,0:T(4,128)} %d1.1) | copy-start | bytes 49156
  93.5 35.6 %copy-start.10 = (s32[8,4,128]{2,1,0:T(4,128)S(1)}, s32[8,4,128]{2,1,0:T(4,128)}, u32[]{:S(2)}) copy-start(s32[8,4,128]{2,1,0:T(4,128)} %d4.1) | copy-start | bytes 49156

commit v7 on v6

--- a/solution.py
+++ b/solution.py
@@ -103,29 +103,41 @@
     )(x, u, y, d)
 
 
-def hidden_kernel(at, r, w2, w3, out, g, cut):
+def hidden_part(r, w2, w3, s):
+    v = r[s * NG : (s + 1) * NG].astype(F32)
+    fm = v[:, :NB].reshape(TILE, T).astype(BF)
+    bd = v[:, NB:].reshape(TILE, T).astype(BF)
+    w = mm(w2, fm, TN)
+    dgated = mm(w3, bd, NN)
+    square = w * w
+    h = 0.5 + 0.5 * jnp.tanh(w * (C0 * S1 + (C0 * 0.044715 * S1**3) * square))
+    gated = ((w * S1) * h).astype(BF)
+    bend = w * (2.0 * C0 * S1 + (6.0 * C0 * 0.044715 * S1**3) * square)
+    slope = h + (h * (1.0 - h)) * bend
+    dpre = ((dgated * S5) * slope).astype(BF)
+    return fm, bd, gated, dpre
+
+
+def hidden_kernel(at, r, w2, w3, out):
+    w2 = w2[0]
+    w3 = w3[0]
+    for s in range(NS):
+        fm, bd, gated, dpre = hidden_part(r, w2, w3, s)
+        down = mm(w3, gated, TN) * S5
+        back_up = mm(w2, dpre, NN) * S1
+        both = jnp.concatenate([down.reshape(NG, NB, T), back_up.reshape(NG, NB, T)], 1)
+        out[s * NG : (s + 1) * NG] = both.astype(BF)
+
+
+def inner_grads_kernel(at, r, w2, w3, g, cut):
     w2 = w2[0]
     w3 = w3[0]
     g2 = g3 = None
     for s in range(NS):
-        v = r[s * NG : (s + 1) * NG].astype(F32)
-        fm = v[:, :NB].reshape(TILE, T).astype(BF)
-        bd = v[:, NB:].reshape(TILE, T).astype(BF)
-        w = mm(w2, fm, TN)
-        dgated = mm(w3, bd, NN)
-        square = w * w
-        h = 0.5 + 0.5 * jnp.tanh(w * (C0 * S1 + (C0 * 0.044715 * S1**3) * square))
-        gated = ((w * S1) * h).astype(BF)
-        bend = w * (2.0 * C0 * S1 + (6.0 * C0 * 0.044715 * S1**3) * square)
-        slope = h + (h * (1.0 - h)) * bend
-        dpre = ((dgated * S5) * slope).astype(BF)
-        down = mm(w3, gated, TN) * S5
-        back_up = mm(w2, dpre, NN) * S1
+        fm, bd, gated, dpre = hidden_part(r, w2, w3, s)
         a2 = mm(fm, dpre, NT)
         a3 = mm(gated, bd, NT)
         g2, g3 = (a2, a3) if g2 is None else (g2 + a2, g3 + a3)
-        both = jnp.concatenate([down.reshape(NG, NB, T), back_up.reshape(NG, NB, T)], 1)
-        out[s * NG : (s + 1) * NG] = both.astype(BF)
     for c in range(4):
         v = (g2[:, c * 128 : (c + 1) * 128] * S1).reshape(NZ, NS, R, 128)
         for s in range(NS):
@@ -135,7 +147,7 @@
         g[(z % 2) * NS : (z % 2 + 1) * NS, z // 2] = cut[z].astype(BF)
 
 
-def hidden_stage(at, r, up2, dn1):
+def hidden_call(kernel, out_spec, out_shape, scratch, at, r, up2, dn1):
     spec = pltpu.PrefetchScalarGridSpec(
         num_scalar_prefetch=1,
         grid=(ML,),
@@ -144,27 +156,41 @@
             pl.BlockSpec((1, TILE, HB), lambda m, s: (s[2] * ML + m, 0, 0)),
             pl.BlockSpec((1, HB, TILE), lambda m, s: (s[2] * ML + m, 0, 0)),
         ],
-        out_specs=[pl.BlockSpec((NS * NG, 2 * NB, T), lambda m, s: (0, m, 0))]
-        + [pl.BlockSpec((2 * NS, NQ, 8 * R, 128), lambda m, s: (0, 0, m, 0))],
-        scratch_shapes=[pltpu.VMEM((NZ, NS, 8 * R, 128), F32)],
+        out_specs=out_spec,
+        scratch_shapes=scratch,
     )
     return pl.pallas_call(
-        hidden_kernel,
+        kernel,
         grid_spec=spec,
-        out_shape=[pltpu.HBM((NS * NG, 2 * NB * ML, T), BF)]
-        + [pltpu.HBM((2 * NS, NQ, 8 * R * ML, 128), BF)],
+        out_shape=out_shape,
         compiler_params=PARAMS,
         cost_estimate=cost(2**30, 2**22),
     )(at, r, up2, dn1)
 
 
-def outer_kernel(r, x, y, u, g23, gin, grads, rows, cut, sem):
+def hidden_stage(*args):
+    block = pl.BlockSpec((NS * NG, 2 * NB, T), lambda m, s: (0, m, 0))
+    return hidden_call(hidden_kernel, block, pltpu.HBM((NS * NG, 2 * NB * ML, T), BF), [], *args)
+
+
+def inner_grads(*args):
+    block = pl.BlockSpec((2 * NS, NQ, 8 * R, 128), lambda m, s: (0, 0, m, 0))
+    shape = pltpu.HBM((2 * NS, NQ, 8 * R * ML, 128), BF)
+    return hidden_call(inner_grads_kernel, block, shape, [pltpu.VMEM((NZ, NS, 8 * R, 128), F32)], *args)
+
+
+def outer_kernel(r, x_in, y_in, u_in, g23, gin, grads, x, y, u, rows, cut, sem, sems):
+    loads = [pltpu.make_async_copy(a, b, sems.at[i]) for i, (a, b) in enumerate(((x_in, x), (y_in, y), (u_in, u)))]
+    for load in loads:
+        load.start()
     copy = pltpu.make_async_copy(g23, grads.at[:, :, 1], sem)
     copy.start()
     for s in range(NS):
         for h in range(2):
             rows[h, :, s] = r[s * NG : (s + 1) * NG, :, h * 128 : (h + 1) * 128].astype(F32)
     flat = rows.reshape(2, TILE * 2 * NB, 128)
+    for load in loads:
+        load.wait()
 
     def pick(j):
         return jnp.concatenate([flat[h, pl.ds(j, TILE, stride=2 * NB), :] for h in range(2)], 1).astype(BF)
@@ -186,17 +212,21 @@
 def outer_stage(r, x, y, u, g23):
     return pl.pallas_call(
         outer_kernel,
-        in_specs=[pl.BlockSpec(memory_space=pltpu.VMEM)] * 4 + [pl.BlockSpec(memory_space=pltpu.HBM)],
+        in_specs=[pl.BlockSpec(memory_space=pltpu.VMEM)] + [pl.BlockSpec(memory_space=pltpu.HBM)] * 4,
         out_shape=[
             jax.ShapeDtypeStruct((T, NB * TILE), BF),
             jax.ShapeDtypeStruct((2 * NS, NQ, 2, 2 * NB * R, TILE), BF),
         ],
         scratch_shapes=[
+            pltpu.VMEM(x.shape, BF),
+            pltpu.VMEM(y.shape, BF),
+            pltpu.VMEM(u.shape, BF),
             pltpu.VMEM((2, NG, NS, 2 * NB * ML, 128), F32),
             pltpu.VMEM((NZ, NS, 2 * NB * R, TILE), F32),
             pltpu.SemaphoreType.DMA,
-        ],
-        compiler_params=PARAMS,
+            pltpu.SemaphoreType.DMA((3,)),
+        ],
+        compiler_params=FULL,
         cost_estimate=cost(2**10, 2**10),
     )(r, x, y, u, g23)
 
@@ -297,7 +327,8 @@
 def on_device(x, dy, up1, up2, dn1, dn2, di1, di2, di3, di4):
     at = jnp.stack([lax.axis_index(a) for a in ("fq", "z1", SUB)]).astype(jnp.int32)
     got = exchange(first_stage(x, up1, dy, dn2), GROUP)
-    send, g23 = hidden_stage(at, got, up2, dn1)
+    send = hidden_stage(at, got, up2, dn1)
+    g23 = inner_grads(at, got, up2, dn1)
     gin, grads = outer_stage(exchange(send, GROUP), x, dy, up1, g23)
     grads = exchange(near_stage(exchange(grads, NEAR)), FAR)
     new1, new2, new3, new4 = update(at, grads, up1, up2, dn1, dn2, di1, di2, di3, di4)

time: 131 us -> 135 us (1.031)
  blocking collectives: 88.8 us -> 67 us
  waiting for transfers between devices: 17 us -> 28.2 us
  Pallas kernels: 13.8 us -> 21.5 us
  starting transfers between devices: 9.92 us -> 16.6 us
    all_to_all x3 -> x2, blocking collectives: 88.8 us -> 67 us  [exchange(): return lax.all_to_all(a, axes, 0, 0, tiled=True)]
    all_to_all x1 -> x2, waiting for transfers between devices: 17 us -> 28.2 us  [exchange(): return lax.all_to_all(a, axes, 0, 0, tiled=True)]
    all_to_all x1 -> x2, starting transfers between devices: 9.92 us -> 16.6 us  [exchange(): return lax.all_to_all(a, axes, 0, 0, tiled=True)]
    pallas_call x1 -> x2, Pallas kernels: 6.65 us -> 11.6 us  [hidden_call(): pl.pallas_call(kernel, grid_spec=spec, out_shape=out_shape, compiler_para...]
    pallas_call x1, Pallas kernels: 2.15 us -> 4.87 us  [outer_stage(): pl.pallas_call(outer_kernel, in_specs=[pl.BlockSpec(memory_space=pltpu.VM...]
  transfers between devices with their start and end apart: 1 -> 2, of which waited for: 1 -> 2; matrix products, arithmetic and copies ran while one was open for 0% -> 0% of each run, Pallas kernels for 0% -> 4%
where the time goes in v7:
time: 135 us; the launch traced here: 134 us
  blocking collectives  67 us (50%)
  waiting for transfers between devices  28.2 us (21%)
  Pallas kernels  21.5 us (16%)
  starting transfers between devices  16.6 us (12%)
    all_to_all x2, blocking collectives, exchange(): return lax.all_to_all(a, axes, 0, 0, tiled=True)  67 us
    all_to_all x2, waiting for transfers between devices, exchange(): return lax.all_to_all(a, axes, 0, 0, tiled=True)  28.2 us
    all_to_all x2, starting transfers between devices, exchange(): return lax.all_to_all(a, axes, 0, 0, tiled=True)  16.6 us
    pallas_call x2, Pallas kernels, hidden_call(): pl.pallas_call(kernel, grid_spec=spec, out_shape=out_shape, compiler_para...  11.6 us
    pallas_call x1, Pallas kernels, outer_stage(): pl.pallas_call(outer_kernel, in_specs=[pl.BlockSpec(memory_space=pltpu.VM...  4.87 us
    pallas_call x1, Pallas kernels, first_stage(): pl.pallas_call(first_kernel, in_specs=[hbm] * 4, out_specs=hbm, out_shape...  3.54 us
  transfers between devices with their start and end apart: 2, of which 2 were waited for; matrix products, arithmetic and copies ran while one was open for 0% of the time, Pallas kernels for 4%

profile of v7, /device:TPU:32, one launch (start us, length us, event | category | flops | bytes accessed | tf_op | source)
XLA Modules:
  0.0 134.3 jit_solution(3269314918428386979)
XLA Ops:
  0.6 3.5 %shard_map.137 = bf16[64,32,256]{2,1,0:T(8,128)(2,1)} custom-call(bf16[256,1024]{1,0:T(8,128)(2,1)} %x_in.3, bf16[8,128,128]{2,1,0:T(8,128)(2,1)} %up1.1, bf16[256,1024]{1,0:T(8,128)(2,1)} %y_in.3, bf16[8,128,128]{2,1,0:T(8,128)(2,1)} %dn2.1), custom_call_target="tpu_custom_call" | custom-call | flops 134217728 | bytes 2097152 | tf_op jit(solution)/shard_map/pallas_call | solution.py:87
  4.2 0.0 copy-start
  4.2 0.0 copy-start.2
  4.2 9.9 %all-to-all-start = ((bf16[64,32,256]{2,1,0:T(8,128)(2,1)}), bf16[64,32,256]{2,1,0:T(8,128)(2,1)S(1)}, u32[]{:S(2)}, u32[]{:S(2)}) async-start(bf16[64,32,256]{2,1,0:T(8,128)(2,1)} %shard_map.137), calls=%async_computation | async-start | bytes 2097152 | tf_op jit(solution)/shard_map/all_to_all | solution.py:47
  14.1 0.1 pad_add_fusion.at
  14.2 0.0 copy-start.10
  14.2 17.0 %all-to-all-done.r = bf16[64,32,256]{2,1,0:T(8,128)(2,1)S(1)} async-done(((bf16[64,32,256]{2,1,0:T(8,128)(2,1)}), bf16[64,32,256]{2,1,0:T(8,128)(2,1)S(1)}, u32[]{:S(2)}, u32[]{:S(2)}) %all-to-all-start) | async-done | bytes 1048608 | tf_op jit(solution)/shard_map/all_to_all | solution.py:47
  31.2 0.0 copy-done
  31.2 0.0 copy-done.2
  31.2 5.9 %shard_map.138 = bf16[64,32,256]{2,1,0:T(8,128)(2,1)} custom-call(s32[3]{0:T(128)S(1)} %pad_add_fusion.at, bf16[64,32,256]{2,1,0:T(8,128)(2,1)S(1)} %all-to-all-done.r, bf16[8,128,512]{2,1,0:T(8,128)(2,1)S(1)} %copy-done, bf16[8,512,128]{2,1,0:T(8,128)(2,1)S(1)} %copy-done.2), custom_call_target="tpu_custom_call" | custom-call | flops 1073741824 | bytes 4194304 | tf_op jit(solution)/shard_map/pallas_call | solution.py:162
  37.1 6.7 %all-to-all-start.1 = ((bf16[64,32,256]{2,1,0:T(8,128)(2,1)}), bf16[64,32,256]{2,1,0:T(8,128)(2,1)}, u32[]{:S(2)}, u32[]{:S(2)}) async-start(bf16[64,32,256]{2,1,0:T(8,128)(2,1)} %shard_map.138), calls=%async_computation.1 | async-start | bytes 2097152 | tf_op jit(solution)/shard_map/all_to_all | solution.py:47
  43.8 0.0 copy-done.10
  43.8 5.7 %shard_map.139.g23 = bf16[8,4,64,128]{3,2,1,0:T(8,128)(2,1)} custom-call(s32[3]{0:T(128)S(1)} %pad_add_fusion.at, bf16[64,32,256]{2,1,0:T(8,128)(2,1)S(1)} %all-to-all-done.r, bf16[8,128,512]{2,1,0:T(8,128)(2,1)S(1)} %copy-done, bf16[8,512,128]{2,1,0:T(8,128)(2,1)S(1)} %copy-done.2), custom_call_target="tpu_custom_call" | custom-call | flops 1073741824 | bytes 4194304 | tf_op jit(solution)/shard_map/pallas_call | solution.py:162
  49.5 11.3 %all-to-all-done.1.r = bf16[64,32,256]{2,1,0:T(8,128)(2,1)} async-done(((bf16[64,32,256]{2,1,0:T(8,128)(2,1)}), bf16[64,32,256]{2,1,0:T(8,128)(2,1)}, u32[]{:S(2)}, u32[]{:S(2)}) %all-to-all-start.1) | async-done | bytes 1048608 | tf_op jit(solution)/shard_map/all_to_all | solution.py:47
  60.7 4.9 %shard_map.140 = (bf16[256,1024]{1,0:T(8,128)(2,1)}, bf16[8,4,2,64,128]{4,3,2,1,0:T(8,128)(2,1)}) custom-call(bf16[64,32,256]{2,1,0:T(8,128)(2,1)} %all-to-all-done.1.r, bf16[256,1024]{1,0:T(8,128)(2,1)} %x_in.3, bf16[256,1024]{1,0:T(8,128)(2,1)} %y_in.3, bf16[8,128,128]{2,1,0:T(8,128)(2,1)} %up1.1, bf16[8,4,64,128]{3,2,1,0:T(8,128)(2,1)} %shard_map.139.g23), custom_call_target="tpu_custom_call" | custom-call | flops 1024 | bytes 1024 | tf_op jit(solution)/shard_map/pallas_call | solution.py:213
  65.6 0.0 copy-start.3
  65.6 30.5 %all_to_all.20.a = bf16[8,4,2,64,128]{4,3,2,1,0:T(8,128)(2,1)S(1)} all-to-all(bf16[8,4,2,64,128]{4,3,2,1,0:T(8,128)(2,1)} %get-tuple-element.12), channel_id=1, replica_groups=mesh['fq'=4,'z1'=2,'zl'=2,'yl'=2,'mp'=16] {'z1','zl','yl'}, dimensions={0} | all-to-all | bytes 2097152 | tf_op jit(solution)/shard_map/all_to_all | solution.py:47
  96.1 0.0 copy-start.1
  96.1 0.0 copy-start.8
  96.1 0.0 copy-start.9
  96.1 0.0 copy-start.11
  96.1 0.1 shard_map.141
  96.3 0.0 copy-start.4
  96.3 0.0 copy-start.5
  96.3 0.0 copy-start.6
  96.3 0.0 copy-start.7
  96.3 36.5 %all_to_all.21.a = bf16[4,5,64,128]{3,2,1,0:T(8,128)(2,1)S(1)} all-to-all(bf16[4,5,64,128]{3,2,1,0:T(8,128)(2,1)S(1)} %shard_map.141), channel_id=1, replica_groups=mesh['fq'=4,'z1'=2,'zl'=2,'yl'=2,'mp'=16] {'fq'}, dimensions={0} | all-to-all | bytes 655360 | tf_op jit(solution)/shard_map/all_to_all | solution.py:47
  132.8 0.0 copy-done.3
  132.9 0.0 copy-done.1
  132.9 0.0 copy-done.8
  132.9 0.0 copy-done.9
  132.9 0.0 copy-done.11
  132.9 0.0 copy-done.4
  132.9 0.0 copy-done.5
  132.9 0.0 copy-done.6
  132.9 0.0 copy-done.7
  132.9 1.3 shard_map.142
Async XLA Ops:
  4.2 27.0 %copy-start = (bf16[8,128,512]{2,1,0:T(8,128)(2,1)S(1)}, bf16[8,128,512]{2,1,0:T(8,128)(2,1)}, u32[]{:S(2)}) copy-start(bf16[8,128,512]{2,1,0:T(8,128)(2,1)} %up2.1) | copy-start | bytes 3145732
  4.2 27.0 %copy-start.2 = (bf16[8,512,128]{2,1,0:T(8,128)(2,1)S(1)}, bf16[8,512,128]{2,1,0:T(8,128)(2,1)}, u32[]{:S(2)}) copy-start(bf16[8,512,128]{2,1,0:T(8,128)(2,1)} %dn1.1) | copy-start | bytes 3145732
  4.2 27.0 %all-to-all-start = ((bf16[64,32,256]{2,1,0:T(8,128)(2,1)}), bf16[64,32,256]{2,1,0:T(8,128)(2,1)S(1)}, u32[]{:S(2)}, u32[]{:S(2)}) async-start(bf16[64,32,256]{2,1,0:T(8,128)(2,1)} %shard_map.137), calls=%async_computation | async-start | bytes 2097152 | tf_op jit(solution)/shard_map/all_to_all | solution.py:47
  14.2 29.5 %copy-start.10 = (s32[3]{0:T(128)}, s32[3]{0:T(128)S(1)}, u32[]{:S(2)}) copy-start(s32[3]{0:T(128)S(1)} %pad_add_fusion.at) | copy-start | bytes 40
  37.1 23.7 %all-to-all-start.1 = ((bf16[64,32,256]{2,1,0:T(8,128)(2,1)}), bf16[64,32,256]{2,1,0:T(8,128)(2,1)}, u32[]{:S(2)}, u32[]{:S(2)}) async-start(bf16[64,32,256]{2,1,0:T(8,128)(2,1)} %shard_map.138), calls=%async_computation.1 | async-start | bytes 2097152 | tf_op jit(solution)/shard_map/all_to_all | solution.py:47
  65.6 67.2 %copy-start.3 = (bf16[8,512,128]{2,1,0:T(8,128)(2,1)S(1)}, bf16[8,512,128]{2,1,0:T(8,128)(2,1)}, u32[]{:S(2)}) copy-start(bf16[8,512,128]{2,1,0:T(8,128)(2,1)} %dn1.1) | copy-start | bytes 3145732
  96.1 36.7 %copy-start.1 = (bf16[8,128,512]{2,1,0:T(8,128)(2,1)S(1)}, bf16[8,128,512]{2,1,0:T(8,128)(2,1)}, u32[]{:S(2)}) copy-start(bf16[8,128,512]{2,1,0:T(8,128)(2,1)} %up2.1) | copy-start | bytes 3145732
  96.1 36.7 %copy-start.8 = (s32[8,4,128]{2,1,0:T(4,128)S(1)}, s32[8,4,128]{2,1,0:T(4,128)}, u32[]{:S(2)}) copy-start(s32[8,4,128]{2,1,0:T(4,128)} %d1.1) | copy-start | bytes 49156
  96.1 36.8 %copy-start.9 = (s32[8,4,128]{2,1,0:T(4,128)S(1)}, s32[8,4,128]{2,1,0:T(4,128)}, u32[]{:S(2)}) copy-start(s32[8,4,128]{2,1,0:T(4,128)} %d4.1) | copy-start | bytes 49156
  96.1 36.8 %copy-start.11 = (s32[3]{0:T(128)S(1)}, s32[3]{0:T(128)}, u32[]{:S(2)}) copy-start(s32[3]{0:T(128)} %copy-done.10) | copy-start | bytes 40
  96.3 36.6 %copy-start.4 = (bf16[8,128,128]{2,1,0:T(8,128)(2,1)S(1)}, bf16[8,128,128]{2,1,0:T(8,128)(2,1)}, u32[]{:S(2)}) copy-start(bf16[8,128,128]{2,1,0:T(8,128)(2,1)} %up1.1) | copy-start | bytes 786436
  96.3 36.6 %copy-start.5 = (bf16[8,128,128]{2,1,0:T(8,128)(2,1)S(1)}, bf16[8,128,128]{2,1,0:T(8,128)(2,1)}, u32[]{:S(2)}) copy-start(bf16[8,128,128]{2,1,0:T(8,128)(2,1)} %dn2.1) | copy-start | bytes 786436
  96.3 36.6 %copy-start.6 = (s32[8,4,512]{2,1,0:T(4,128)S(1)}, s32[8,4,512]{2,1,0:T(4,128)}, u32[]{:S(2)}) copy-start(s32[8,4,512]{2,1,0:T(4,128)} %d2.1) | copy-start | bytes 196612
  96.3 36.6 %copy-start.7 = (s32[8,16,128]{2,1,0:T(8,128)S(1)}, s32[8,16,128]{2,1,0:T(8,128)}, u32[]{:S(2)}) copy-start(s32[8,16,128]{2,1,0:T(8,128)} %d3.1) | copy-start | bytes 196612
